TPU v7x, 32 devices: a whole 2x2x4 slice. The times are simulated.
32 devices in a mesh: groups: 2 (over y), gx: 4 (over z), gy: 4 (over x, core).
Axes of the slice: x: 2, y: 2, z: 4, core: 2. Of those that a mesh axis runs over, the one named last changes fastest.
Arguments:
- velocity0: float32 [6, 8, 4, 2048], P(None, ('groups', 'gx'), 'gy'), parts along dimension 1, may hold values from -6 to 6
- inv_mass: float32 [6, 8, 4, 2048], P(None, ('groups', 'gx'), 'gy'), parts along dimension 1, may hold values from 0.2 to 1
- jac_a: float32 [18, 8, 4, 32, 128], P(None, ('groups', 'gx'), 'gy'), parts along dimension 1, may hold values from -3 to 3
- jac_b: float32 [18, 8, 4, 32, 128], P(None, ('groups', 'gx'), 'gy'), parts along dimension 1, may hold values from -3 to 3
- precond: float32 [9, 8, 4, 32, 128], P(None, ('groups', 'gx'), 'gy'), parts along dimension 1, as said below
- bias: float32 [3, 8, 4, 32, 128], P(None, ('groups', 'gx'), 'gy'), parts along dimension 1, may hold values from -4 to 4
- friction: float32 [8, 4, 32, 128], P(('groups', 'gx'), 'gy'), parts along dimension 0, may hold values from 0.2 to 0.9
- impulse0: float32 [3, 8, 4, 32, 128], P(None, ('groups', 'gx'), 'gy'), parts along dimension 1, may hold values from -4 to 4
- body_a: int32 [8, 4, 32, 128], P(('groups', 'gx'), 'gy'), parts along dimension 0, may hold values from 0 to 2047
- body_b: int32 [8, 4, 32, 128], P(('groups', 'gx'), 'gy'), parts along dimension 0, may hold values from 0 to 3871, as said below
- active: int32 [8, 4, 32, 128], P(('groups', 'gx'), 'gy'), parts along dimension 0, may hold values 0 or 1
- sticking: int32 [8, 4, 32, 128], P(('groups', 'gx'), 'gy'), parts along dimension 0, may hold values 0 or 1
Outputs:
- impulses: float32 [3, 8, 4, 32, 128], P(None, ('groups', 'gx'), 'gy'), parts along dimension 1
- velocity: float32 [6, 8, 4, 2048], P(None, ('groups', 'gx'), 'gy'), parts along dimension 1
There are 2 independent parts, one for each index of `groups`. A program takes and returns all parts, laid end to end along the dimension named above; each array names one. Nothing has to cross between parts.
Inputs may be any that keep to these rules, and one draw needn't show every extreme that they name: `body_b`: values under 2048 name a body of the contact's own device; a value 2048 + s * 256 + i names the body i of the neighbouring device in slot s's set facing back, with i under 256 // 8 for the corner slots 0, 2, 5, 7 and under 256 for the others; such a device always exists in the grid. `precond`: diagonal entries lie between 0.3 and 0.6, off-diagonal ones between -0.12 and 0.12.
All inputs are finite; a program needn't handle non-finite values. No bound on the sum of `active` or of `sticking` on one device may be relied on, other than what follows from the above.
Results may differ from a plain program's by a relative error of at most 0.0001.
Values sent between devices are 32-bit elements; how exact they have to be, the bound alone decides.
No kernel may reach another device: no remote copies, remote signals or barrier semaphores. Data moves between devices by JAX's collectives and lax.ppermute only.
A program may use at most 64 MiB of HBM per device.

v0:
```python
import jax
import jax.numpy as jnp
from jax import lax
from jax.sharding import PartitionSpec as P

ROWS = 3
DOF = 6
NBND = 256
ITERS = 3


directions = ((-1, -1), (-1, 0), (-1, 1), (0, -1), (0, 1), (1, -1), (1, 0), (1, 1))


def passed_along(value, axis, steps):
    count = lax.axis_size(axis)
    initial, last = (max(0, -steps), min(count, count - steps))
    return lax.ppermute(value, axis, [(source, source + steps) for source in range(initial, last)])


def with_halo(cells, sides, width):
    for axis, dim in sides:
        count = lax.axis_size(axis)
        ends = count - 1
        head = lax.slice_in_dim(cells, 0, width, axis=dim)
        tail = lax.slice_in_dim(cells, cells.shape[dim] - width, cells.shape[dim], axis=dim)
        cells = jnp.concatenate(
            [
                lax.ppermute(tail, axis, [(i, (i + 1) % count) for i in range(ends)]),
                cells,
                lax.ppermute(head, axis, [((i + 1) % count, i) for i in range(ends)]),
            ],
            axis=dim,
        )
    return cells


def project(raw, mu, stick, act):
    normal = jnp.maximum(raw[0], 0.0)
    bound = mu * (1.0 + 0.5 * stick) * normal + 0.1
    square = raw[1] * raw[1] + raw[2] * raw[2]
    scale = bound / jnp.sqrt(jnp.maximum(square, bound * bound))
    return act[None] * jnp.stack([normal, raw[1] * scale, raw[2] * scale])


def set_layout(nborder):
    corner = nborder // 8
    lengths = [corner, nborder, corner, nborder, nborder, corner, nborder, corner]
    starts = [0]
    for length in lengths[:-1]:
        starts.append(starts[-1] + length)
    return (lengths, starts)


def pass_x(upward, downward):
    from_low = passed_along(upward, "gx", 1)
    from_high = passed_along(downward, "gx", -1)
    return (from_low, from_high)


def pass_y(upward, downward):
    from_low = passed_along(upward, "gy", 1)
    from_high = passed_along(downward, "gy", -1)
    return (from_low, from_high)


def gather_bounds(border, lengths, starts):

    def facing(array, slot):
        return array[:, starts[slot] : starts[slot] + lengths[slot]]

    beside_all = with_halo(border[:, None, None, :], (("gx", 1), ("gy", 2)), 1)
    return [
        facing(beside_all[:, 1 + step_x, 1 + step_y], 7 - slot)
        for slot, (step_x, step_y) in enumerate(directions)
    ]


def on_device(
    velocity0,
    inv_mass,
    jac_a,
    jac_b,
    precond,
    bias,
    friction,
    impulse0,
    body_a,
    body_b,
    active,
    sticking,
):
    nbodies = velocity0.shape[3]
    nborder = NBND
    lengths, starts = set_layout(nborder)
    region = starts[7] + lengths[7]
    corner = lengths[0]
    middle = corner + lengths[1]
    start = velocity0[:, 0, 0]
    minv = inv_mass[:, 0, 0]
    j_a = jac_a.reshape(ROWS, DOF, -1)
    j_b = jac_b.reshape(ROWS, DOF, -1)
    w_mat = precond.reshape(ROWS, ROWS, -1)
    bias_flat = bias.reshape(ROWS, -1)
    mu = friction.reshape(-1)
    stick = sticking.reshape(-1).astype(jnp.float32)
    act = active.reshape(-1).astype(jnp.float32)
    first = body_a.reshape(-1)
    second = body_b.reshape(-1)
    width = nbodies + 8 * nborder

    def velocities(lam):
        force_a = jnp.sum(j_a * lam[:, None], axis=0)
        force_b = jnp.sum(j_b * lam[:, None], axis=0)
        buffer = (
            jnp.zeros((DOF, width), jnp.float32)
            .at[:, first]
            .add(force_a)
            .at[:, second]
            .add(force_b)
        )
        own = buffer[:, :nbodies]
        others = buffer[:, nbodies:].reshape(DOF, 8, nborder)
        parts = [others[:, slot, : lengths[slot]] for slot in range(8)]
        from_low, from_high = pass_x(
            jnp.concatenate([parts[5], parts[6], parts[7]], axis=1),
            jnp.concatenate([parts[0], parts[1], parts[2]], axis=1),
        )
        from_ylow, from_yhigh = pass_y(
            jnp.concatenate([from_low[:, middle:], parts[4], from_high[:, middle:]], axis=1),
            jnp.concatenate([from_low[:, :corner], parts[3], from_high[:, :corner]], axis=1),
        )
        received = [
            from_ylow[:, :corner],
            from_low[:, corner:middle],
            from_yhigh[:, :corner],
            from_ylow[:, corner:middle],
            from_yhigh[:, corner:middle],
            from_ylow[:, middle:],
            from_high[:, corner:middle],
            from_yhigh[:, middle:],
        ]
        incoming = jnp.concatenate(received, axis=1)
        total = own.at[:, :region].add(incoming)
        return start + minv * total

    lam = act[None] * impulse0.reshape(ROWS, -1)
    for step in range(ITERS):
        vel = velocities(lam)
        pieces = gather_bounds(vel[:, :region], lengths, starts)
        padded = [jnp.pad(piece, ((0, 0), (0, nborder - piece.shape[1]))) for piece in pieces]
        table = jnp.concatenate([vel] + padded, axis=1)
        rel_vel = jnp.sum(j_a * vel[:, first][None], axis=1) + jnp.sum(
            j_b * table[:, second][None], axis=1
        )
        target = rel_vel + bias_flat
        change = jnp.sum(w_mat * target[None], axis=1)
        lam = project(lam - change, mu, stick, act)
    vel = velocities(lam)
    return (lam.reshape(impulse0.shape), vel.reshape(velocity0.shape))


def solution(mesh):
    placed = (
        P(None, ("groups", "gx"), "gy", None),
        P(None, ("groups", "gx"), "gy", None),
        P(None, ("groups", "gx"), "gy", None, None),
        P(None, ("groups", "gx"), "gy", None, None),
        P(None, ("groups", "gx"), "gy", None, None),
        P(None, ("groups", "gx"), "gy", None, None),
        P(("groups", "gx"), "gy", None, None),
        P(None, ("groups", "gx"), "gy", None, None),
        P(("groups", "gx"), "gy", None, None),
        P(("groups", "gx"), "gy", None, None),
        P(("groups", "gx"), "gy", None, None),
        P(("groups", "gx"), "gy", None, None),
    )
    return jax.shard_map(
        on_device,
        mesh=mesh,
        in_specs=placed,
        out_specs=(
            P(None, ("groups", "gx"), "gy", None, None),
            P(None, ("groups", "gx"), "gy", None),
        ),
        check_vma=False,
    )
```

profile of v0, /device:TPU:1, one launch (start us, length us, event | category | flops | bytes accessed | tf_op | source)
XLA Modules:
  0.0 555.3 jit_solution(11367613826507653664)
XLA Ops:
  9.0 23.2 %scatter_custom_fusion = f32[6,4096]{0,1:T(8,128)S(1)} fusion(s32[4096]{0:T(1024)S(1)} %bitcast.219, f32[4096,6]{1,0:T(8,128)} %copy.95, f32[]{:T(128)} %constant.101.clone.1), kind=kCustom, calls=%fused_computation.29 | custom fusion | flops 24576 | bytes 98816 | tf_op jit(solution)/shard_map/scatter-add | solution.py:118
  32.2 23.4 %scatter_fusion = f32[6,4096]{0,1:T(8,128)S(1)} fusion(f32[6,4096]{0,1:T(8,128)S(1)} %scatter_custom_fusion, s32[4096]{0:T(1024)S(1)} %bitcast.177, f32[4096,6]{1,0:T(8,128)} %copy.96), kind=kCustom, calls=%fused_computation.7 | custom fusion | flops 24576 | bytes 311296 | tf_op jit(solution)/shard_map/scatter-add | solution.py:120
  57.6 4.0 collective-permute-start
  67.3 3.3 collective-permute-start.3
  70.7 3.0 collective-permute-start.2
  76.4 2.5 fusion.13
  78.9 2.4 constant_dynamic-update-slice_fusion
  82.6 3.8 collective-permute-start.4
  89.4 15.4 %gather_fusion = f32[4096,6]{1,0:T(8,128)} fusion(f32[6,2048]{0,1:T(8,128)} %copy-done.1, s32[4096]{0:T(1024)S(1)} %get-tuple-element.177), kind=kCustom, calls=%fused_computation | custom fusion | bytes 212992 | tf_op jit(solution)/shard_map/gather | solution.py:153
  104.8 2.2 copy.106
  107.2 4.5 collective-permute-start.6
  136.3 15.8 %gather_fusion.1 = f32[4096,6]{1,0:T(8,128)} fusion(f32[6,4096]{0,1:T(8,128)} %fusion.19, s32[4096]{0:T(1024)S(1)} %copy-done.5), kind=kCustom, calls=%fused_computation.1 | custom fusion | bytes 212992 | tf_op jit(solution)/shard_map/gather | solution.py:154
  152.0 2.2 copy.118
  157.0 24.1 %scatter_custom_fusion.2 = f32[6,4096]{0,1:T(8,128)} fusion(s32[4096]{0:T(1024)} %bitcast.220, f32[4096,6]{1,0:T(8,128)} %copy.119, f32[]{:T(128)} %constant.101.clone.1), kind=kCustom, calls=%fused_computation.27 | custom fusion | flops 24576 | bytes 98816 | tf_op jit(solution)/shard_map/scatter-add | solution.py:118
  183.0 23.3 %scatter_fusion.1 = f32[6,4096]{0,1:T(8,128)} fusion(f32[6,4096]{0,1:T(8,128)} %scatter_custom_fusion.2, s32[4096]{0:T(1024)S(1)} %bitcast.179, f32[4096,6]{1,0:T(8,128)} %copy.120), kind=kCustom, calls=%fused_computation.9 | custom fusion | flops 24576 | bytes 311296 | tf_op jit(solution)/shard_map/scatter-add | solution.py:120
  206.4 2.7 fusion.28
  216.1 4.9 collective-permute-start.8
  226.2 2.2 collective-permute-done.9
  230.5 5.1 collective-permute-start.10
  237.9 2.7 fusion.14
  240.6 2.4 constant_dynamic-update-slice_fusion.1
  246.2 2.6 collective-permute-start.12
  250.2 15.4 %gather_fusion.2 = f32[4096,6]{1,0:T(8,128)} fusion(f32[6,2048]{0,1:T(8,128)} %copy-done.3, s32[4096]{0:T(1024)S(1)} %copy-done.9), kind=kCustom, calls=%fused_computation.2 | custom fusion | bytes 212992 | tf_op jit(solution)/shard_map/gather | solution.py:153
  265.6 2.2 copy.130
  267.9 4.3 collective-permute-start.14
  296.8 15.8 %gather_fusion.3 = f32[4096,6]{1,0:T(8,128)} fusion(f32[6,4096]{0,1:T(8,128)} %fusion.18, s32[4096]{0:T(1024)S(1)} %copy-done.6), kind=kCustom, calls=%fused_computation.3 | custom fusion | bytes 212992 | tf_op jit(solution)/shard_map/gather | solution.py:154
  312.7 2.2 copy.142
  317.6 24.1 %scatter_custom_fusion.4 = f32[6,4096]{0,1:T(8,128)} fusion(s32[4096]{0:T(1024)} %bitcast.221, f32[4096,6]{1,0:T(8,128)} %copy.143, f32[]{:T(128)} %constant.101.clone.1), kind=kCustom, calls=%fused_computation.25 | custom fusion | flops 24576 | bytes 98816 | tf_op jit(solution)/shard_map/scatter-add | solution.py:118
  343.7 23.3 %scatter_fusion.2 = f32[6,4096]{0,1:T(8,128)} fusion(f32[6,4096]{0,1:T(8,128)} %scatter_custom_fusion.4, s32[4096]{0:T(1024)S(1)} %bitcast.180, f32[4096,6]{1,0:T(8,128)} %copy.144), kind=kCustom, calls=%fused_computation.11 | custom fusion | flops 24576 | bytes 311296 | tf_op jit(solution)/shard_map/scatter-add | solution.py:120
  367.0 2.7 fusion.27
  376.7 4.9 collective-permute-start.16
  386.8 2.2 collective-permute-done.17
  391.2 5.1 collective-permute-start.18
  398.6 2.7 fusion.15
  401.3 2.4 constant_dynamic-update-slice_fusion.2
  406.9 2.6 collective-permute-start.20
  410.8 15.4 %gather_fusion.4 = f32[4096,6]{1,0:T(8,128)} fusion(f32[6,2048]{0,1:T(8,128)} %copy-done.2, s32[4096]{0:T(1024)S(1)} %copy-done.10), kind=kCustom, calls=%fused_computation.4 | custom fusion | bytes 212992 | tf_op jit(solution)/shard_map/gather | solution.py:153
  428.5 4.3 collective-permute-start.22
  457.5 15.8 %gather_fusion.5 = f32[4096,6]{1,0:T(8,128)} fusion(f32[6,4096]{0,1:T(8,128)} %fusion.17, s32[4096]{0:T(1024)S(1)} %copy-done.7), kind=kCustom, calls=%fused_computation.5 | custom fusion | bytes 212992 | tf_op jit(solution)/shard_map/gather | solution.py:154
  473.3 2.2 copy.166
  478.3 24.1 %scatter_custom_fusion.6 = f32[6,4096]{0,1:T(8,128)} fusion(s32[4096]{0:T(1024)} %bitcast.222, f32[4096,6]{1,0:T(8,128)} %copy.167, f32[]{:T(128)} %constant.101.clone.1), kind=kCustom, calls=%fused_computation.23 | custom fusion | flops 24576 | bytes 98816 | tf_op jit(solution)/shard_map/scatter-add | solution.py:118
  504.3 23.3 %scatter_fusion.3 = f32[6,4096]{0,1:T(8,128)} fusion(f32[6,4096]{0,1:T(8,128)} %scatter_custom_fusion.6, s32[4096]{0:T(1024)S(1)} %bitcast.181, f32[4096,6]{1,0:T(8,128)} %copy.168), kind=kCustom, calls=%fused_computation.13 | custom fusion | flops 24576 | bytes 311296 | tf_op jit(solution)/shard_map/scatter-add | solution.py:120
  527.7 2.7 fusion.26
  530.7 4.3 collective-permute-start.24
  537.5 2.3 collective-permute-done.25
  541.9 5.1 collective-permute-start.26
  548.3 2.5 fusion.16
  550.8 2.4 fusion.4
  (326 shorter events, 163.8 us)
Async XLA Ops:
  7.0 25.2 %copy-start.29 = (s32[4096,1]{0,1:T(1,128)}, s32[4096,1]{0,1:T(1,128)S(1)}, u32[]{:S(2)}) copy-start(s32[4096,1]{0,1:T(1,128)S(1)} %get-tuple-element.143) | copy-start | bytes 49156
  57.6 9.4 %collective-permute-start = (f32[6,320]{1,0:T(8,128)S(1)}, f32[6,320]{1,0:T(8,128)S(1)}, u32[]{:S(2)}, u32[]{:S(2)}) collective-permute-start(f32[6,320]{1,0:T(8,128)S(1)} %pad_maximum_fusion.3), channel_id=1, source_target_pairs={{0,4},{4,8},{8,12},{1,5},{5,9},{9,13},{2,6},{6,10},{10,14},{3,7},{... | collective-permute-start | bytes 23048 | tf_op jit(solution)/shard_map/ppermute | solution.py:18
  62.0 5.1 collective-permute-start.1
  63.9 25.5 %copy-start.8 = (s32[4096]{0:T(1024)}, s32[4096]{0:T(1024)S(1)}, u32[]{:S(2)}) copy-start(s32[4096]{0:T(1024)S(1)} %get-tuple-element.177) | copy-start | bytes 49156
  67.3 6.6 %collective-permute-start.3 = (f32[6,320]{1,0:T(8,128)S(1)}, f32[6,320]{1,0:T(8,128)S(1)}, u32[]{:S(2)}, u32[]{:S(2)}) collective-permute-start(f32[6,320]{1,0:T(8,128)S(1)} %pad_maximum_fusion.6), channel_id=1, source_target_pairs={{1,0},{2,1},{3,2},{5,4},{6,5},{7,6},{9,8},{10,9},{11,10},{13,12},{... | collective-permute-start | bytes 23048 | tf_op jit(solution)/shard_map/ppermute | solution.py:18
  70.7 3.8 collective-permute-start.2
  82.6 24.5 %collective-permute-start.4 = (f32[6,1,1,1152]{3,2,1,0:T(1,128)S(1)}, f32[6,1,1,1152]{3,2,1,0:T(1,128)S(1)}, u32[]{:S(2)}, u32[]{:S(2)}) collective-permute-start(f32[6,1,1,1152]{3,2,1,0:T(1,128)S(1)} %copy.107), channel_id=1, source_target_pairs={{0,4},{4,8},{8,12},{1,5},{5,9},{9,13},{2,6},{6,10},{10,14},{3,7},{... | collective-permute-start | bytes 82952 | tf_op jit(solution)/shard_map/ppermute | solution.py:29
  86.4 20.7 %collective-permute-start.5 = (f32[6,1,1,1152]{3,2,1,0:T(1,128)S(1)}, f32[6,1,1,1152]{3,2,1,0:T(1,128)S(1)}, u32[]{:S(2)}, u32[]{:S(2)}) collective-permute-start(f32[6,1,1,1152]{3,2,1,0:T(1,128)S(1)} %copy.107), channel_id=1, source_target_pairs={{4,0},{8,4},{12,8},{5,1},{9,5},{13,9},{6,2},{10,6},{14,10},{7,3},{... | collective-permute-start | bytes 82952 | tf_op jit(solution)/shard_map/ppermute | solution.py:31
  88.4 66.2 %copy-start.11 = (f32[1,1,32,128]{3,2,1,0:T(8,128)}, f32[1,1,32,128]{3,2,1,0:T(8,128)S(1)}, u32[]{:S(2)}) copy-start(f32[1,1,32,128]{3,2,1,0:T(8,128)S(1)} %add_multiply_fusion) | copy-start | bytes 49156
  107.2 8.9 %collective-permute-start.6 = (f32[6,3,1,1152]{3,2,1,0:T(1,128)S(1)}, f32[6,3,1,1152]{3,2,1,0:T(1,128)}, u32[]{:S(2)}, u32[]{:S(2)}) collective-permute-start(f32[6,3,1,1152]{3,2,1,0:T(1,128)S(1)} %pad_maximum_fusion), channel_id=1, source_target_pairs={{0,1},{1,2},{2,3},{4,5},{5,6},{6,7},{8,9},{9,10},{10,11},{12,13},{... | collective-permute-start | bytes 248840 | tf_op jit(solution)/shard_map/ppermute | solution.py:29
  111.8 6.9 %collective-permute-start.7 = (f32[6,3,1,1152]{3,2,1,0:T(1,128)S(1)}, f32[6,3,1,1152]{3,2,1,0:T(1,128)}, u32[]{:S(2)}, u32[]{:S(2)}) collective-permute-start(f32[6,3,1,1152]{3,2,1,0:T(1,128)S(1)} %pad_maximum_fusion), channel_id=1, source_target_pairs={{1,0},{2,1},{3,2},{5,4},{6,5},{7,6},{9,8},{10,9},{11,10},{13,12},{... | collective-permute-start | bytes 248840 | tf_op jit(solution)/shard_map/ppermute | solution.py:31
  121.3 15.0 %copy-start.5 = (s32[4096]{0:T(1024)S(1)}, s32[4096]{0:T(1024)}, u32[]{:S(2)}) copy-start(s32[4096]{0:T(1024)} %get-tuple-element.176) | copy-start | bytes 49156
  134.6 19.8 %copy-start.4 = (f32[3,1,1,32,128]{4,3,2,1,0:T(8,128)S(1)}, f32[3,1,1,32,128]{4,3,2,1,0:T(8,128)}, u32[]{:S(2)}) copy-start(f32[3,1,1,32,128]{4,3,2,1,0:T(8,128)} %param.25) | copy-start | bytes 147460
  136.3 18.4 %copy-start.14 = (f32[3,1,1,32,128]{4,3,2,1,0:T(8,128)S(1)}, f32[3,1,1,32,128]{4,3,2,1,0:T(8,128)}, u32[]{:S(2)}) copy-start(f32[3,1,1,32,128]{4,3,2,1,0:T(8,128)} %param.27) | copy-start | bytes 147460
  154.8 26.3 %copy-start.25 = (f32[1,4096]{1,0:T(1,128)}, f32[1,4096]{1,0:T(1,128)S(1)}, u32[]{:S(2)}) copy-start(f32[1,4096]{1,0:T(1,128)S(1)} %get-tuple-element.72) | copy-start | bytes 49156
  154.8 26.2 %copy-start.19 = (f32[1,4096]{1,0:T(1,128)}, f32[1,4096]{1,0:T(1,128)S(1)}, u32[]{:S(2)}) copy-start(f32[1,4096]{1,0:T(1,128)S(1)} %get-tuple-element.138) | copy-start | bytes 49156
  154.8 26.2 %copy-start.21 = (f32[1,4096]{1,0:T(1,128)}, f32[1,4096]{1,0:T(1,128)S(1)}, u32[]{:S(2)}) copy-start(f32[1,4096]{1,0:T(1,128)S(1)} %get-tuple-element.139) | copy-start | bytes 49156
  216.1 9.4 %collective-permute-start.8 = (f32[6,320]{1,0:T(8,128)}, f32[6,320]{1,0:T(8,128)}, u32[]{:S(2)}, u32[]{:S(2)}) collective-permute-start(f32[6,320]{1,0:T(8,128)} %pad_maximum_fusion.7), channel_id=1, source_target_pairs={{0,4},{4,8},{8,12},{1,5},{5,9},{9,13},{2,6},{6,10},{10,14},{3,7},{... | collective-permute-start | bytes 23048 | tf_op jit(solution)/shard_map/ppermute | solution.py:18
  224.0 4.4 collective-permute-start.9
  228.6 7.9 %collective-permute-start.11 = (f32[6,320]{1,0:T(8,128)S(1)}, f32[6,320]{1,0:T(8,128)S(1)}, u32[]{:S(2)}, u32[]{:S(2)}) collective-permute-start(f32[6,320]{1,0:T(8,128)S(1)} %pad_maximum_fusion.10), channel_id=1, source_target_pairs={{1,0},{2,1},{3,2},{5,4},{6,5},{7,6},{9,8},{10,9},{11,10},{13,12},{... | collective-permute-start | bytes 23048 | tf_op jit(solution)/shard_map/ppermute | solution.py:18
  230.5 6.1 %collective-permute-start.10 = (f32[6,320]{1,0:T(8,128)S(1)}, f32[6,320]{1,0:T(8,128)S(1)}, u32[]{:S(2)}, u32[]{:S(2)}) collective-permute-start(f32[6,320]{1,0:T(8,128)S(1)} %pad_maximum_fusion.9), channel_id=1, source_target_pairs={{0,1},{1,2},{2,3},{4,5},{5,6},{6,7},{8,9},{9,10},{10,11},{12,13},{... | collective-permute-start | bytes 23048 | tf_op jit(solution)/shard_map/ppermute | solution.py:18
  246.2 21.6 %collective-permute-start.12 = (f32[6,1,1,1152]{3,2,1,0:T(1,128)S(1)}, f32[6,1,1,1152]{3,2,1,0:T(1,128)S(1)}, u32[]{:S(2)}, u32[]{:S(2)}) collective-permute-start(f32[6,1,1,1152]{3,2,1,0:T(1,128)S(1)} %copy.131), channel_id=1, source_target_pairs={{0,4},{4,8},{8,12},{1,5},{5,9},{9,13},{2,6},{6,10},{10,14},{3,7},{... | collective-permute-start | bytes 82952 | tf_op jit(solution)/shard_map/ppermute | solution.py:29
  248.9 18.9 %collective-permute-start.13 = (f32[6,1,1,1152]{3,2,1,0:T(1,128)S(1)}, f32[6,1,1,1152]{3,2,1,0:T(1,128)S(1)}, u32[]{:S(2)}, u32[]{:S(2)}) collective-permute-start(f32[6,1,1,1152]{3,2,1,0:T(1,128)S(1)} %copy.131), channel_id=1, source_target_pairs={{4,0},{8,4},{12,8},{5,1},{9,5},{13,9},{6,2},{10,6},{14,10},{7,3},{... | collective-permute-start | bytes 82952 | tf_op jit(solution)/shard_map/ppermute | solution.py:31
  267.9 8.8 %collective-permute-start.14 = (f32[6,3,1,1152]{3,2,1,0:T(1,128)S(1)}, f32[6,3,1,1152]{3,2,1,0:T(1,128)}, u32[]{:S(2)}, u32[]{:S(2)}) collective-permute-start(f32[6,3,1,1152]{3,2,1,0:T(1,128)S(1)} %pad_maximum_fusion.1), channel_id=1, source_target_pairs={{0,1},{1,2},{2,3},{4,5},{5,6},{6,7},{8,9},{9,10},{10,11},{12,13},{... | collective-permute-start | bytes 248840 | tf_op jit(solution)/shard_map/ppermute | solution.py:29
  272.3 6.9 %collective-permute-start.15 = (f32[6,3,1,1152]{3,2,1,0:T(1,128)S(1)}, f32[6,3,1,1152]{3,2,1,0:T(1,128)}, u32[]{:S(2)}, u32[]{:S(2)}) collective-permute-start(f32[6,3,1,1152]{3,2,1,0:T(1,128)S(1)} %pad_maximum_fusion.1), channel_id=1, source_target_pairs={{1,0},{2,1},{3,2},{5,4},{6,5},{7,6},{9,8},{10,9},{11,10},{13,12},{... | collective-permute-start | bytes 248840 | tf_op jit(solution)/shard_map/ppermute | solution.py:31
  296.8 18.4 %copy-start.20 = (f32[1,4096]{1,0:T(1,128)S(1)}, f32[1,4096]{1,0:T(1,128)}, u32[]{:S(2)}) copy-start(f32[1,4096]{1,0:T(1,128)} %copy-done.19) | copy-start | bytes 49156
  296.8 18.4 %copy-start.22 = (f32[1,4096]{1,0:T(1,128)S(1)}, f32[1,4096]{1,0:T(1,128)}, u32[]{:S(2)}) copy-start(f32[1,4096]{1,0:T(1,128)} %copy-done.21) | copy-start | bytes 49156
  296.8 18.4 %copy-start.26 = (f32[1,4096]{1,0:T(1,128)S(1)}, f32[1,4096]{1,0:T(1,128)}, u32[]{:S(2)}) copy-start(f32[1,4096]{1,0:T(1,128)} %copy-done.25) | copy-start | bytes 49156
  296.8 18.5 %copy-start.12 = (f32[1,1,32,128]{3,2,1,0:T(8,128)S(1)}, f32[1,1,32,128]{3,2,1,0:T(8,128)}, u32[]{:S(2)}) copy-start(f32[1,1,32,128]{3,2,1,0:T(8,128)} %copy-done.11) | copy-start | bytes 49156
  315.4 26.3 %copy-start.23 = (f32[1,4096]{1,0:T(1,128)}, f32[1,4096]{1,0:T(1,128)S(1)}, u32[]{:S(2)}) copy-start(f32[1,4096]{1,0:T(1,128)S(1)} %get-tuple-element.68) | copy-start | bytes 49156
  315.5 26.2 %copy-start.15 = (f32[1,4096]{1,0:T(1,128)}, f32[1,4096]{1,0:T(1,128)S(1)}, u32[]{:S(2)}) copy-start(f32[1,4096]{1,0:T(1,128)S(1)} %get-tuple-element.136) | copy-start | bytes 49156
  315.5 26.2 %copy-start.17 = (f32[1,4096]{1,0:T(1,128)}, f32[1,4096]{1,0:T(1,128)S(1)}, u32[]{:S(2)}) copy-start(f32[1,4096]{1,0:T(1,128)S(1)} %get-tuple-element.137) | copy-start | bytes 49156
  376.7 9.4 %collective-permute-start.16 = (f32[6,320]{1,0:T(8,128)}, f32[6,320]{1,0:T(8,128)}, u32[]{:S(2)}, u32[]{:S(2)}) collective-permute-start(f32[6,320]{1,0:T(8,128)} %pad_maximum_fusion.11), channel_id=1, source_target_pairs={{0,4},{4,8},{8,12},{1,5},{5,9},{9,13},{2,6},{6,10},{10,14},{3,7},{... | collective-permute-start | bytes 23048 | tf_op jit(solution)/shard_map/ppermute | solution.py:18
  384.6 4.4 collective-permute-start.17
  389.2 7.9 %collective-permute-start.19 = (f32[6,320]{1,0:T(8,128)S(1)}, f32[6,320]{1,0:T(8,128)S(1)}, u32[]{:S(2)}, u32[]{:S(2)}) collective-permute-start(f32[6,320]{1,0:T(8,128)S(1)} %pad_maximum_fusion.14), channel_id=1, source_target_pairs={{1,0},{2,1},{3,2},{5,4},{6,5},{7,6},{9,8},{10,9},{11,10},{13,12},{... | collective-permute-start | bytes 23048 | tf_op jit(solution)/shard_map/ppermute | solution.py:18
  391.2 6.1 %collective-permute-start.18 = (f32[6,320]{1,0:T(8,128)S(1)}, f32[6,320]{1,0:T(8,128)S(1)}, u32[]{:S(2)}, u32[]{:S(2)}) collective-permute-start(f32[6,320]{1,0:T(8,128)S(1)} %pad_maximum_fusion.13), channel_id=1, source_target_pairs={{0,1},{1,2},{2,3},{4,5},{5,6},{6,7},{8,9},{9,10},{10,11},{12,13},{... | collective-permute-start | bytes 23048 | tf_op jit(solution)/shard_map/ppermute | solution.py:18
  406.9 21.6 %collective-permute-start.20 = (f32[6,1,1,1152]{3,2,1,0:T(1,128)S(1)}, f32[6,1,1,1152]{3,2,1,0:T(1,128)S(1)}, u32[]{:S(2)}, u32[]{:S(2)}) collective-permute-start(f32[6,1,1,1152]{3,2,1,0:T(1,128)S(1)} %copy.155), channel_id=1, source_target_pairs={{0,4},{4,8},{8,12},{1,5},{5,9},{9,13},{2,6},{6,10},{10,14},{3,7},{... | collective-permute-start | bytes 82952 | tf_op jit(solution)/shard_map/ppermute | solution.py:29
  409.5 18.9 %collective-permute-start.21 = (f32[6,1,1,1152]{3,2,1,0:T(1,128)S(1)}, f32[6,1,1,1152]{3,2,1,0:T(1,128)S(1)}, u32[]{:S(2)}, u32[]{:S(2)}) collective-permute-start(f32[6,1,1,1152]{3,2,1,0:T(1,128)S(1)} %copy.155), channel_id=1, source_target_pairs={{4,0},{8,4},{12,8},{5,1},{9,5},{13,9},{6,2},{10,6},{14,10},{7,3},{... | collective-permute-start | bytes 82952 | tf_op jit(solution)/shard_map/ppermute | solution.py:31
  428.5 8.8 %collective-permute-start.22 = (f32[6,3,1,1152]{3,2,1,0:T(1,128)S(1)}, f32[6,3,1,1152]{3,2,1,0:T(1,128)}, u32[]{:S(2)}, u32[]{:S(2)}) collective-permute-start(f32[6,3,1,1152]{3,2,1,0:T(1,128)S(1)} %pad_maximum_fusion.2), channel_id=1, source_target_pairs={{0,1},{1,2},{2,3},{4,5},{5,6},{6,7},{8,9},{9,10},{10,11},{12,13},{... | collective-permute-start | bytes 248840 | tf_op jit(solution)/shard_map/ppermute | solution.py:29
  433.0 7.0 %collective-permute-start.23 = (f32[6,3,1,1152]{3,2,1,0:T(1,128)S(1)}, f32[6,3,1,1152]{3,2,1,0:T(1,128)}, u32[]{:S(2)}, u32[]{:S(2)}) collective-permute-start(f32[6,3,1,1152]{3,2,1,0:T(1,128)S(1)} %pad_maximum_fusion.2), channel_id=1, source_target_pairs={{1,0},{2,1},{3,2},{5,4},{6,5},{7,6},{9,8},{10,9},{11,10},{13,12},{... | collective-permute-start | bytes 248840 | tf_op jit(solution)/shard_map/ppermute | solution.py:31
  457.5 18.4 %copy-start.16 = (f32[1,4096]{1,0:T(1,128)S(1)}, f32[1,4096]{1,0:T(1,128)}, u32[]{:S(2)}) copy-start(f32[1,4096]{1,0:T(1,128)} %copy-done.15) | copy-start | bytes 49156
  457.5 18.4 %copy-start.18 = (f32[1,4096]{1,0:T(1,128)S(1)}, f32[1,4096]{1,0:T(1,128)}, u32[]{:S(2)}) copy-start(f32[1,4096]{1,0:T(1,128)} %copy-done.17) | copy-start | bytes 49156
  457.5 18.4 %copy-start.24 = (f32[1,4096]{1,0:T(1,128)S(1)}, f32[1,4096]{1,0:T(1,128)}, u32[]{:S(2)}) copy-start(f32[1,4096]{1,0:T(1,128)} %copy-done.23) | copy-start | bytes 49156
  457.5 18.5 %copy-start.13 = (f32[1,1,32,128]{3,2,1,0:T(8,128)S(1)}, f32[1,1,32,128]{3,2,1,0:T(8,128)}, u32[]{:S(2)}) copy-start(f32[1,1,32,128]{3,2,1,0:T(8,128)} %copy-done.11) | copy-start | bytes 49156
  530.7 6.7 %collective-permute-start.24 = (f32[6,320]{1,0:T(8,128)S(1)}, f32[6,320]{1,0:T(8,128)S(1)}, u32[]{:S(2)}, u32[]{:S(2)}) collective-permute-start(f32[6,320]{1,0:T(8,128)S(1)} %pad_maximum_fusion.15), channel_id=1, source_target_pairs={{0,4},{4,8},{8,12},{1,5},{5,9},{9,13},{2,6},{6,10},{10,14},{3,7},{... | collective-permute-start | bytes 23048 | tf_op jit(solution)/shard_map/ppermute | solution.py:18
  535.3 4.4 collective-permute-start.25
  539.9 7.2 %collective-permute-start.27 = (f32[6,320]{1,0:T(8,128)S(1)}, f32[6,320]{1,0:T(8,128)S(1)}, u32[]{:S(2)}, u32[]{:S(2)}) collective-permute-start(f32[6,320]{1,0:T(8,128)S(1)} %pad_maximum_fusion.18), channel_id=1, source_target_pairs={{1,0},{2,1},{3,2},{5,4},{6,5},{7,6},{9,8},{10,9},{11,10},{13,12},{... | collective-permute-start | bytes 23048 | tf_op jit(solution)/shard_map/ppermute | solution.py:18
  541.9 5.9 %collective-permute-start.26 = (f32[6,320]{1,0:T(8,128)S(1)}, f32[6,320]{1,0:T(8,128)S(1)}, u32[]{:S(2)}, u32[]{:S(2)}) collective-permute-start(f32[6,320]{1,0:T(8,128)S(1)} %pad_maximum_fusion.17), channel_id=1, source_target_pairs={{0,1},{1,2},{2,3},{4,5},{5,6},{6,7},{8,9},{9,10},{10,11},{12,13},{... | collective-permute-start | bytes 23048 | tf_op jit(solution)/shard_map/ppermute | solution.py:18
  (14 other events, 112.8 us)
where the time goes:
time: 560 us; the launch traced here: 555 us
  local copies, waits for them, and re-layouts  237 us (42%)
  other arithmetic  227 us (41%)
  starting transfers between devices  82.8 us (15%)
  waiting for transfers between devices  7.77 us (1%)
    scatter-add x8, other arithmetic, velocities(): buffer = jnp.zeros((DOF, width), jnp.float32).at[:, first].add(force_a).a...  189 us
    unnamed x142, local copies, waits for them, and re-layouts  67.1 us
    gather x6, local copies, waits for them, and re-layouts, on_device(): table[:, second][None]  54 us
    gather x6, local copies, waits for them, and re-layouts, on_device(): vel[:, first][None]  52.9 us
    ppermute x16, starting transfers between devices, passed_along(): lax.ppermute(value, axis, [(source, source + steps) for source in range(i...  50.4 us
    ppermute x6, starting transfers between devices, with_halo(): lax.ppermute(tail, axis, [(i, (i + 1) % count) for i in range(ends)])  22.1 us
  transfers between devices with their start and end apart: 28, of which 5 were waited for; matrix products, arithmetic and copies ran while one was open for 15% of the time, Pallas kernels for 0%

commit v1 on v0

v1 whole, which is shorter than its diff:
```python
import jax
import jax.numpy as jnp
import numpy as np
from jax import lax
from jax.experimental import pallas as pl
from jax.experimental.pallas import tpu as pltpu
from jax.sharding import PartitionSpec as P

ROWS = 3
DOF = 6
ITERS = 3
LANES = 128
NB = 2048
NBND = 256
CORNER = NBND // 8
OWN_TILES = NB // LANES
EDGE_TILES = 2
HALO_TILES = 9
CORNER_TILE = OWN_TILES - 1
HALO_CORNER = HALO_TILES - 1
SET_START = (0, 32, 288, 320, 576, 832, 864, 1120)
TABLE_START = (1920, 0, 1952, 256, 512, 1984, 768, 2016)
INTERIOR_START = 1152
INTERIOR_TABLE = 1024
EDGE_SLOTS = (1, 3, 4, 6)
CORNER_SLOTS = (0, 2, 5, 7)


def table_index(body):
    steps = []
    for slot in range(8):
        steps.append((SET_START[slot], TABLE_START[slot] - SET_START[slot]))
    steps.append((INTERIOR_START, INTERIOR_TABLE - INTERIOR_START))
    for slot in range(8):
        steps.append((NB + slot * NBND, TABLE_START[slot] - slot * NBND))
    shift = jnp.full(body.shape, steps[0][1], jnp.int32)
    for start, delta in steps[1:]:
        shift = jnp.where(body >= start, delta, shift)
    return body + shift


def lane_iota():
    return lax.broadcasted_iota(jnp.int32, (8, LANES), 1)


def to_tables(ref):
    zero = jnp.zeros((2, LANES), jnp.float32)
    blocks = [
        jnp.concatenate([ref[pl.ds(k, DOF, stride=OWN_TILES), :], zero], axis=0)
        for k in range(OWN_TILES)
    ]
    lane = lane_iota()
    tiles = []
    for slot in EDGE_SLOTS:
        first, off = divmod(SET_START[slot], LANES)
        rolled = [pltpu.roll(blocks[first + j], LANES - off, 1) for j in range(3)]
        for j in range(2):
            tiles.append(jnp.where(lane < LANES - off, rolled[j], rolled[j + 1]))
    tiles += blocks[INTERIOR_START // LANES :]
    corner = jnp.zeros((8, LANES), jnp.float32)
    for place, slot in enumerate(CORNER_SLOTS):
        block = blocks[SET_START[slot] // LANES]
        corner = jnp.where(lane // CORNER == place, block, corner)
    tiles.append(corner)
    return tiles


def from_tables(tiles, out_ref):
    lane = lane_iota()
    blocks = [jnp.zeros((8, LANES), jnp.float32) for _ in range(INTERIOR_START // LANES)]
    for e, slot in enumerate(EDGE_SLOTS):
        first, off = divmod(SET_START[slot], LANES)
        rolled = [pltpu.roll(tiles[2 * e + j], off, 1) for j in range(2)]
        blocks[first] = jnp.where(lane >= off, rolled[0], blocks[first])
        blocks[first + 1] = jnp.where(lane >= off, rolled[1], rolled[0])
        blocks[first + 2] = jnp.where(lane < off, rolled[1], blocks[first + 2])
    for place, slot in enumerate(CORNER_SLOTS):
        k = SET_START[slot] // LANES
        blocks[k] = jnp.where(lane // CORNER == place, tiles[CORNER_TILE], blocks[k])
    blocks += tiles[8:CORNER_TILE]
    for k in range(OWN_TILES):
        out_ref[pl.ds(k, DOF, stride=OWN_TILES), :] = blocks[k][:DOF]


def row_of(ref, r):
    return ref[pl.ds(r, 1), :]


def build_onehot(index_ref, onehot_ref):
    rows = index_ref.shape[0]
    base = lax.broadcasted_iota(jnp.int32, (NBND, LANES), 0)
    for r in range(rows):
        q = row_of(index_ref, r) & (NBND - 1)
        hit = (base == q).astype(jnp.float32).astype(jnp.bfloat16)
        onehot_ref[:, r * LANES : (r + 1) * LANES] = hit


def forces(lam, jac_ref, force_ref):
    rows = lam[0].shape[0]
    for d in range(DOF):
        f = jac_ref[d] * lam[0]
        f = f + jac_ref[DOF + d] * lam[1]
        f = f + jac_ref[2 * DOF + d] * lam[2]
        force_ref[d * rows : (d + 1) * rows, :] = f
    for d in range(DOF, 8):
        force_ref[d * rows : (d + 1) * rows, :] = jnp.zeros_like(f)


def spread(force_ref, index_ref, left_ref, heads):
    rows = index_ref.shape[0]
    for r in range(rows):
        f = force_ref[pl.ds(r, 8, stride=rows), :]
        hi = f.astype(jnp.bfloat16).astype(jnp.float32)
        lo = f - hi
        both = jnp.concatenate([hi, lo], axis=0)
        head = jnp.broadcast_to(row_of(index_ref, r) >> 8, (16, LANES))
        for k, h in enumerate(heads):
            left_ref[16 * k : 16 * (k + 1), r * LANES : (r + 1) * LANES] = jnp.where(
                head == h, both, 0.0
            ).astype(jnp.bfloat16)


OWN_HEADS = tuple(range(8))
ALL_HEADS = OWN_HEADS + (8, 9, 10, 11, 15)


def scatter(lam, jac_a, jac_b, id_a, id_b, hot_a, hot_b, force, left_a, left_b):
    contract = (((1,), (1,)), ((), ()))
    forces(lam, jac_a, force)
    spread(force, id_a, left_a, OWN_HEADS)
    sum_a = lax.dot_general(left_a[...], hot_a[...], contract, preferred_element_type=jnp.float32)
    forces(lam, jac_b, force)
    spread(force, id_b, left_b, ALL_HEADS)
    sum_b = lax.dot_general(left_b[...], hot_b[...], contract, preferred_element_type=jnp.float32)

    def tile(s, k, j):
        lanes = slice(j * LANES, (j + 1) * LANES)
        return s[16 * k : 16 * k + 8, lanes] + s[16 * k + 8 : 16 * k + 16, lanes]

    own = [tile(sum_a, t // 2, t % 2) + tile(sum_b, t // 2, t % 2) for t in range(OWN_TILES)]
    halo = [tile(sum_b, 8 + t // 2, t % 2) for t in range(8)] + [tile(sum_b, 12, 1)]
    return own, halo


def put_x(even, planes, a_ref, b_ref):
    high = lane_iota() >= 2 * CORNER
    for p, tiles in enumerate(planes):
        up = (tiles[6], tiles[7], jnp.where(high, tiles[-1], 0.0))
        down = (tiles[0], tiles[1], jnp.where(high, 0.0, tiles[-1]))
        for k in range(3):
            a_ref[p, k] = jnp.where(even, up[k], down[k])
            b_ref[p, k] = jnp.where(even, down[k], up[k])


def is_even():
    return lax.rem(lax.axis_index("gy"), 2) == 0


def corners_in(y_low, y_high, p):
    lane = lane_iota()
    odd = (lane & CORNER) != 0
    return jnp.where(odd, pltpu.roll(y_high(p, 2), 96, 1), pltpu.roll(y_low(p, 2), 32, 1))


class Received:
    def __init__(self, even, a_ref, b_ref, e_ref, o_ref):
        def pick(first, second):
            return lambda p, k: jnp.where(even, first[p, k], second[p, k])

        self.x_low, self.x_high = pick(a_ref, b_ref), pick(b_ref, a_ref)
        if e_ref is not None:
            self.y_high, self.y_low = pick(e_ref, o_ref), pick(o_ref, e_ref)

    def plane(self, p):
        tiles = []
        for side in (self.x_low, self.y_low, self.y_high, self.x_high):
            tiles += [side(p, 0), side(p, 1)]
        return tiles + [corners_in(self.y_low, self.y_high, p)]


def add_own(own, came):
    out = [own[t] + came[t] for t in range(8)]
    out += [own[t] for t in range(8, CORNER_TILE)]
    return out + [own[CORNER_TILE] + came[HALO_CORNER]]


def first_kernel(*refs):
    sources, kept, outs = refs[:12], refs[12:20], refs[20:30]
    body_a, body_b, start, minv, force, left_a, left_b, sems = refs[30:]
    id_a, id_b, hot_a, hot_b, own, halo, v_own, m_own, xa, xb = outs
    jac_a, jac_b, precond, bias, mu, stick, act, lam0 = kept
    goals = (body_a, body_b, act, lam0, jac_a, jac_b, start, minv, precond, bias, mu, stick)
    copies = [pltpu.make_async_copy(s, g, sems.at[k]) for k, (s, g) in enumerate(zip(sources, goals))]
    for copy in copies:
        copy.start()
    even = is_even()
    copies[0].wait()
    id_a[...] = table_index(body_a[...])
    build_onehot(id_a, hot_a)
    copies[1].wait()
    id_b[...] = table_index(body_b[...])
    build_onehot(id_b, hot_b)
    for copy in copies[2:6]:
        copy.wait()
    active = act[...].astype(jnp.float32)
    lam = [active * lam0[k] for k in range(ROWS)]
    sums, sums_halo = scatter(lam, jac_a, jac_b, id_a, id_b, hot_a, hot_b, force, left_a, left_b)
    for copy in copies[6:8]:
        copy.wait()
    v, m = to_tables(start), to_tables(minv)
    for t in range(OWN_TILES):
        own[t], v_own[t], m_own[t] = sums[t], v[t], m[t]
    for t in range(HALO_TILES):
        halo[t] = sums_halo[t]
    put_x(even, [sums, sums_halo, v, m], xa, xb)
    for copy in copies[8:]:
        copy.wait()


def turn_kernel(planes, ra, rb, *refs):
    sources, (e_ref, o_ref) = refs[:-2], refs[-2:]
    even = is_even()
    came = Received(even, ra, rb, None, None)
    lane = lane_iota()
    for p in range(planes):
        corner = jnp.where(lane < 2 * CORNER, came.x_high(p, 2), came.x_low(p, 2))
        for k in range(2):
            minus, plus = sources[p][2 + k], sources[p][4 + k]
            e_ref[p, k] = jnp.where(even, plus, minus)
            o_ref[p, k] = jnp.where(even, minus, plus)
        e_ref[p, 2] = corner
        o_ref[p, 2] = corner


TILE_CODES = tuple((t, t) for t in range(24)) + ((31, 24),)


def gather(table, index, codes):
    lane = index & (LANES - 1)
    code = index >> 7
    values = [jnp.zeros(index.shape, jnp.float32) for _ in range(DOF)]
    for c, t in codes:
        mask = code == c
        for d in range(DOF):
            row = jnp.broadcast_to(table[t, d : d + 1, :], index.shape)
            got = jnp.take_along_axis(row, lane, axis=1, mode="promise_in_bounds")
            values[d] = jnp.where(mask, got, values[d])
    return values


def relative(jac, values):
    out = []
    for k in range(ROWS):
        u = jac[k * DOF] * values[0]
        for d in range(1, DOF):
            u = u + jac[k * DOF + d] * values[d]
        out.append(u)
    return out


def middle_kernel(
    first, jac_a, jac_b, precond, bias, mu, stick, act, lam_in,
    id_a, id_b, hot_a, hot_b, own, halo, v_own, m_own, *refs,
):
    if first:
        ra, rb, qe, qo, lam_out, own_out, halo_out, xa, xb, v_halo, m_halo = refs[:11]
    else:
        v_halo, m_halo, ra, rb, qe, qo, lam_out, own_out, halo_out, xa, xb = refs[:11]
    table, force, left_a, left_b = refs[11:]
    even = is_even()
    came = Received(even, ra, rb, qe, qo)
    if first:
        for ref, p in ((v_halo, 2), (m_halo, 3)):
            for t, value in enumerate(came.plane(p)):
                ref[t] = value
    total = add_own(own, came.plane(1))
    total_halo = [a + b for a, b in zip([halo[t] for t in range(HALO_TILES)], came.plane(0))]
    for t in range(OWN_TILES):
        table[t] = v_own[t] + m_own[t] * total[t]
    for t in range(HALO_TILES):
        table[OWN_TILES + t] = v_halo[t] + m_halo[t] * total_halo[t]
    u_a = relative(jac_a, gather(table, id_a[...], TILE_CODES[:OWN_TILES]))
    u_b = relative(jac_b, gather(table, id_b[...], TILE_CODES))
    target = [u_a[k] + u_b[k] + bias[k] for k in range(ROWS)]
    active = act[...].astype(jnp.float32)
    if first:
        lam = [active * lam_in[k] for k in range(ROWS)]
    else:
        lam = [lam_in[k] for k in range(ROWS)]
    raw = []
    for k in range(ROWS):
        w = precond[k * ROWS] * target[0]
        for j in range(1, ROWS):
            w = w + precond[k * ROWS + j] * target[j]
        raw.append(lam[k] - w)
    normal = jnp.maximum(raw[0], 0.0)
    bound = mu[...] * (1.0 + 0.5 * stick[...].astype(jnp.float32)) * normal + 0.1
    square = raw[1] * raw[1] + raw[2] * raw[2]
    scale = bound / jnp.sqrt(jnp.maximum(square, bound * bound))
    lam = [active * normal, active * (raw[1] * scale), active * (raw[2] * scale)]
    for k in range(ROWS):
        lam_out[k] = lam[k]
    sums, sums_halo = scatter(lam, jac_a, jac_b, id_a, id_b, hot_a, hot_b, force, left_a, left_b)
    for t in range(OWN_TILES):
        own_out[t] = sums[t]
    for t in range(HALO_TILES):
        halo_out[t] = sums_halo[t]
    put_x(even, [sums, sums_halo], xa, xb)


def last_kernel(own, v_own, m_own, ra, rb, qe, qo, out):
    came = Received(is_even(), ra, rb, qe, qo)
    total = add_own(own, came.plane(1))
    from_tables([v_own[t] + m_own[t] * total[t] for t in range(OWN_TILES)], out)


def exchange_pairs(nx, ny):
    up = []
    for x in range(nx):
        for y in range(ny):
            to = x + 1 if y % 2 == 0 else x - 1
            goal = (to, y) if 0 <= to < nx else (x, y ^ 1)
            up.append((x * ny + y, goal[0] * ny + goal[1]))
    down = [(b, a) for a, b in up]
    near = [(y, y ^ 1) for y in range(ny)]
    far = [(y, (((y + 1) ^ 1) - 1) % ny) for y in range(ny)]
    return up, down, near, far


def on_device(
    velocity0, inv_mass, jac_a, jac_b, precond, bias, friction, impulse0, body_a, body_b, active, sticking
):
    nx, ny = lax.axis_size("gx"), lax.axis_size("gy")
    up, down, near, far = exchange_pairs(nx, ny)
    rows, lanes = body_a.shape[-2:]
    flat = lambda a: a.reshape(-1, rows, lanes)
    plain = lambda a: a.reshape(rows, lanes)
    jac_a, jac_b, precond, bias, impulse0 = map(flat, (jac_a, jac_b, precond, bias, impulse0))
    friction, body_a, body_b, active, sticking = map(plain, (friction, body_a, body_b, active, sticking))
    start, minv = (a.reshape(-1, lanes) for a in (velocity0, inv_mass))
    contacts = rows * lanes
    f32, i32, bf16 = jnp.float32, jnp.int32, jnp.bfloat16
    arr = jax.ShapeDtypeStruct
    vmem = pl.BlockSpec(memory_space=pltpu.VMEM)
    own_t, halo_t = arr((OWN_TILES, 8, lanes), f32), arr((HALO_TILES, 8, lanes), f32)
    lam_t = arr((ROWS, rows, lanes), f32)
    ids_t, hot_t = arr((rows, lanes), i32), arr((NBND, contacts), bf16)
    message = lambda p: arr((p, 3, 8, lanes), f32)
    work = [
        pltpu.VMEM((8 * rows, lanes), f32),
        pltpu.VMEM((16 * len(OWN_HEADS), contacts), bf16),
        pltpu.VMEM((16 * len(ALL_HEADS), contacts), bf16),
    ]
    table = [pltpu.VMEM((OWN_TILES + HALO_TILES, 8, lanes), f32)]

    def call(kernel, outs, scratch, name, *operands, space=pltpu.VMEM):
        return pl.pallas_call(
            kernel,
            out_shape=outs,
            in_specs=[pl.BlockSpec(memory_space=space)] * len(operands),
            out_specs=jax.tree.map(lambda _: vmem, outs),
            scratch_shapes=scratch,
            compiler_params=pltpu.CompilerParams(vmem_limit_bytes=32 * 1024 * 1024),
            name=name,
        )(*operands)

    def exchange(xa, xb, sources):
        planes = xa.shape[0]
        ra = lax.ppermute(xa, ("gx", "gy"), up)
        rb = lax.ppermute(xb, ("gx", "gy"), down)
        ye, yo = call(
            lambda *refs: turn_kernel(planes, *refs), (message(planes), message(planes)), [], "turn", ra, rb, *sources
        )
        return ra, rb, lax.ppermute(ye, "gy", near), lax.ppermute(yo, "gy", far)

    sources = (body_a, body_b, active, impulse0, jac_a, jac_b, start, minv, precond, bias, friction, sticking)
    like = lambda a: arr(a.shape, a.dtype)
    kept = (jac_a, jac_b, precond, bias, friction, sticking, active, impulse0)
    made = call(
        first_kernel,
        (*map(like, kept), ids_t, ids_t, hot_t, hot_t, own_t, halo_t, own_t, own_t, message(4), message(4)),
        [pltpu.VMEM(a.shape, a.dtype) for a in (body_a, body_b, start, minv)]
        + work
        + [pltpu.SemaphoreType.DMA((len(sources),))],
        "first",
        *sources,
        space=pltpu.HBM,
    )
    fixed, lam = made[:7], made[7]
    id_a, id_b, hot_a, hot_b, own, halo, v_own, m_own, xa, xb = made[8:]
    for step in range(ITERS):
        first = step == 0
        sources = (own, halo, v_own, m_own) if first else (own, halo)
        received = exchange(xa, xb, sources)
        ins = (*fixed, lam, id_a, id_b, hot_a, hot_b, own, halo, v_own, m_own)
        outs = (lam_t, own_t, halo_t, message(2), message(2))
        kernel = lambda *refs, first=first: middle_kernel(first, *refs)
        if first:
            lam, own, halo, xa, xb, v_halo, m_halo = call(
                kernel, outs + (halo_t, halo_t), table + work, "middle0", *ins, *received
            )
        else:
            lam, own, halo, xa, xb = call(
                kernel, outs, table + work, "middle", *ins, v_halo, m_halo, *received
            )
    received = exchange(xa, xb, (own, halo))
    out = call(last_kernel, arr(start.shape, f32), [], "last", own, v_own, m_own, *received)
    return lam.reshape(ROWS, 1, 1, rows, lanes), out.reshape(velocity0.shape)


def solution(mesh):
    whole = ("groups", "gx")
    body = P(None, whole, "gy", None)
    many = P(None, whole, "gy", None, None)
    one = P(whole, "gy", None, None)
    return jax.shard_map(
        on_device,
        mesh=mesh,
        in_specs=(body, body, many, many, many, many, one, many, one, one, one, one),
        out_specs=(many, body),
        check_vma=False,
    )
```

time: 560 us -> 61.3 us (0.11)
  local copies, waits for them, and re-layouts: 237 us -> 9.6 us
  other arithmetic: 227 us -> 0 us
  starting transfers between devices: 82.8 us -> 21.7 us
  Pallas kernels: 0 us -> 14.6 us
  waiting for transfers between devices: 7.77 us -> 13.9 us
    scatter-add x12 -> x0, other arithmetic: 199 us -> none  [the longest x8 189 us: velocities(): buffer = jnp.zeros((DOF, width), jnp.float32).at[:, first].add(force_a).a...]
    gather x12 -> x0, local copies, waits for them, and re-layouts: 107 us -> none  [the longest x6 54 us: on_device(): table[:, second][None]]
    ppermute x28 -> x16, starting transfers between devices: 82.8 us -> 21.7 us  [the longest x8 15.1 us: exchange(): return (ra, rb, lax.ppermute(ye, 'gy', near), lax.ppermute(yo, 'gy', far))]
    unnamed x142 -> x24, local copies, waits for them, and re-layouts: 67.1 us -> 9.6 us
    slice x59 -> x0, local copies, waits for them, and re-layouts: 28.4 us -> none  [the longest x4 9.32 us: velocities(): others = buffer[:, nbodies:].reshape(DOF, 8, nborder)]
    reduce_sum x8 -> x0, local copies, waits for them, and re-layouts: 15.8 us -> none  [the longest x4 7.91 us: velocities(): force_a = jnp.sum(j_a * lam[:, None], axis=0)]
    pallas_call x0 -> x9, Pallas kernels: none -> 14.6 us  [call(): pl.pallas_call(kernel, out_shape=outs, in_specs=[pl.BlockSpec(memory_spac...]
    concatenate x22 -> x0, other arithmetic: 10.5 us -> none  [the longest x3 4.98 us: on_device(): table = jnp.concatenate([vel] + padded, axis=1)]
  transfers between devices with their start and end apart: 28 -> 16, of which waited for: 5 -> 9; matrix products, arithmetic and copies ran while one was open for 15% -> 0% of each run, Pallas kernels for 0% -> 0%
where the time goes in v1:
time: 61.3 us; the launch traced here: 60.6 us
  starting transfers between devices  21.7 us (35%)
  Pallas kernels  14.6 us (24%)
  waiting for transfers between devices  13.9 us (23%)
  local copies, waits for them, and re-layouts  9.6 us (16%)
  between operations  0.71 us (1%)
    ppermute x8, starting transfers between devices, exchange(): return (ra, rb, lax.ppermute(ye, 'gy', near), lax.ppermute(yo, 'gy', far))  15.1 us
    pallas_call x9, Pallas kernels, call(): pl.pallas_call(kernel, out_shape=outs, in_specs=[pl.BlockSpec(memory_spac...  14.6 us
    unnamed x24, local copies, waits for them, and re-layouts  9.6 us
    ppermute x8, waiting for transfers between devices, exchange(): return (ra, rb, lax.ppermute(ye, 'gy', near), lax.ppermute(yo, 'gy', far))  8.64 us
    ppermute x4, starting transfers between devices, exchange(): rb = lax.ppermute(xb, ('gx', 'gy'), down)  6.32 us
    ppermute x4, waiting for transfers between devices, exchange(): ra = lax.ppermute(xa, ('gx', 'gy'), up)  5.08 us
  transfers between devices with their start and end apart: 16, of which 9 were waited for; matrix products, arithmetic and copies ran while one was open for 0% of the time, Pallas kernels for 0%

profile of v1, /device:TPU:1, one launch (start us, length us, event | category | flops | bytes accessed | tf_op | source)
XLA Modules:
  0.0 60.6 jit_solution(6177456040337377342)
XLA Ops:
  0.6 1.0 %copy-done = f32[18,1,1,32,128]{4,3,2,1,0:T(8,128)S(1)} copy-done((f32[18,1,1,32,128]{4,3,2,1,0:T(8,128)S(1)}, f32[18,1,1,32,128]{4,3,2,1,0:T(8,128)}, u32[]{:S(2)}) %copy-start) | copy-done | bytes 294936
  1.6 1.0 %copy-done.1 = f32[18,1,1,32,128]{4,3,2,1,0:T(8,128)S(1)} copy-done((f32[18,1,1,32,128]{4,3,2,1,0:T(8,128)S(1)}, f32[18,1,1,32,128]{4,3,2,1,0:T(8,128)}, u32[]{:S(2)}) %copy-start.1) | copy-done | bytes 294936
  2.6 0.9 %copy-done.2 = f32[9,1,1,32,128]{4,3,2,1,0:T(8,128)S(1)} copy-done((f32[9,1,1,32,128]{4,3,2,1,0:T(8,128)S(1)}, f32[9,1,1,32,128]{4,3,2,1,0:T(8,128)}, u32[]{:S(2)}) %copy-start.2) | copy-done | bytes 147480
  3.5 0.8 %copy-done.3 = f32[3,1,1,32,128]{4,3,2,1,0:T(8,128)S(1)} copy-done((f32[3,1,1,32,128]{4,3,2,1,0:T(8,128)S(1)}, f32[3,1,1,32,128]{4,3,2,1,0:T(8,128)}, u32[]{:S(2)}) %copy-start.3) | copy-done | bytes 49176
  4.3 0.8 %copy-done.4 = f32[6,1,1,2048]{3,2,1,0:T(1,128)S(1)} copy-done((f32[6,1,1,2048]{3,2,1,0:T(1,128)S(1)}, f32[6,1,1,2048]{3,2,1,0:T(1,128)}, u32[]{:S(2)}) %copy-start.4) | copy-done | bytes 49176
  5.1 0.8 %copy-done.5 = f32[6,1,1,2048]{3,2,1,0:T(1,128)S(1)} copy-done((f32[6,1,1,2048]{3,2,1,0:T(1,128)S(1)}, f32[6,1,1,2048]{3,2,1,0:T(1,128)}, u32[]{:S(2)}) %copy-start.5) | copy-done | bytes 49176
  5.9 0.8 %copy-done.6 = f32[3,1,1,32,128]{4,3,2,1,0:T(8,128)S(1)} copy-done((f32[3,1,1,32,128]{4,3,2,1,0:T(8,128)S(1)}, f32[3,1,1,32,128]{4,3,2,1,0:T(8,128)}, u32[]{:S(2)}) %copy-start.6) | copy-done | bytes 49176
  6.7 0.7 %copy-done.7 = s32[1,1,32,128]{3,2,1,0:T(8,128)S(1)} copy-done((s32[1,1,32,128]{3,2,1,0:T(8,128)S(1)}, s32[1,1,32,128]{3,2,1,0:T(8,128)}, u32[]{:S(2)}) %copy-start.7) | copy-done | bytes 16408
  7.4 0.7 %copy-done.8 = s32[1,1,32,128]{3,2,1,0:T(8,128)S(1)} copy-done((s32[1,1,32,128]{3,2,1,0:T(8,128)S(1)}, s32[1,1,32,128]{3,2,1,0:T(8,128)}, u32[]{:S(2)}) %copy-start.8) | copy-done | bytes 16408
  8.1 0.7 %copy-done.9 = s32[1,1,32,128]{3,2,1,0:T(8,128)S(1)} copy-done((s32[1,1,32,128]{3,2,1,0:T(8,128)S(1)}, s32[1,1,32,128]{3,2,1,0:T(8,128)}, u32[]{:S(2)}) %copy-start.9) | copy-done | bytes 16408
  8.8 0.7 %copy-done.10 = f32[1,1,32,128]{3,2,1,0:T(8,128)S(1)} copy-done((f32[1,1,32,128]{3,2,1,0:T(8,128)S(1)}, f32[1,1,32,128]{3,2,1,0:T(8,128)}, u32[]{:S(2)}) %copy-start.10) | copy-done | bytes 16408
  9.5 0.7 %copy-done.11 = s32[1,1,32,128]{3,2,1,0:T(8,128)S(1)} copy-done((s32[1,1,32,128]{3,2,1,0:T(8,128)S(1)}, s32[1,1,32,128]{3,2,1,0:T(8,128)}, u32[]{:S(2)}) %copy-start.11) | copy-done | bytes 16408
  10.3 4.5 %first.1 = (f32[18,32,128]{2,1,0:T(8,128)S(1)}, f32[18,32,128]{2,1,0:T(8,128)S(1)}, f32[9,32,128]{2,1,0:T(8,128)S(1)}, f32[3,32,128]{2,1,0:T(8,128)S(1)}, f32[32...) custom-call(s32[32,128]{1,0:T(8,128)S(1)} %bitcast.23, ...), custom_call_target="tpu_custom_call" | custom-call | tf_op jit(solution)/shard_map/first/pallas_call | solution.py:357
  14.7 0.1 collective-permute-start
  14.8 2.1 %collective-permute-start.1 = (f32[4,3,8,128]{3,2,1,0:T(8,128)S(1)}, f32[4,3,8,128]{3,2,1,0:T(8,128)S(1)}, u32[]{:S(2)}, u32[]{:S(2)}) collective-permute-start(f32[4,3,8,128]{3,2,1,0:T(8,128)S(1)} %get-tuple-element.62), channel_id=1, source_target_pairs={{4,0},{0,1},{6,2},{2,3},{8,4},{1,5},{10,6},{3,7},{12,8},{5,9},{14,... | collective-permute-start | bytes 147464 | tf_op jit(solution)/shard_map/ppermute | solution.py:370
  16.9 1.4 %collective-permute-done.refs_0_.refs_16_ = f32[4,3,8,128]{3,2,1,0:T(8,128)S(1)} collective-permute-done((f32[4,3,8,128]{3,2,1,0:T(8,128)S(1)}, f32[4,3,8,128]{3,2,1,0:T(8,128)S(1)}, u32[]{:S(2)}, u32[]{:S(2)}) %collective-permute-start) | collective-permute-done | bytes 49184 | tf_op jit(solution)/shard_map/ppermute | solution.py:369
  18.4 0.2 collective-permute-done.1.refs_1_.refs_17_
  18.6 3.4 %collective-permute-start.2 = (f32[4,3,8,128]{3,2,1,0:T(8,128)S(1)}, f32[4,3,8,128]{3,2,1,0:T(8,128)S(1)}, u32[]{:S(2)}, u32[]{:S(2)}) collective-permute-start(f32[4,3,8,128]{3,2,1,0:T(8,128)S(1)} %get-tuple-element.63), channel_id=1, source_target_pairs={{0,1},{1,0},{2,3},{3,2},{4,5},{5,4},{6,7},{7,6},{8,9},{9,8},{10,11... | collective-permute-start | bytes 147464 | tf_op jit(solution)/shard_map/ppermute | solution.py:374
  22.0 1.2 %collective-permute-start.3 = (f32[4,3,8,128]{3,2,1,0:T(8,128)S(1)}, f32[4,3,8,128]{3,2,1,0:T(8,128)S(1)}, u32[]{:S(2)}, u32[]{:S(2)}) collective-permute-start(f32[4,3,8,128]{3,2,1,0:T(8,128)S(1)} %get-tuple-element.64), channel_id=1, source_target_pairs={{0,3},{1,2},{2,1},{3,0},{4,7},{5,6},{6,5},{7,4},{8,11},{9,10},{10,... | collective-permute-start | bytes 147464 | tf_op jit(solution)/shard_map/ppermute | solution.py:374
  23.2 0.0 collective-permute-done.2.refs_18_
  23.2 2.4 %collective-permute-done.3.refs_19_ = f32[4,3,8,128]{3,2,1,0:T(8,128)S(1)} collective-permute-done((f32[4,3,8,128]{3,2,1,0:T(8,128)S(1)}, f32[4,3,8,128]{3,2,1,0:T(8,128)S(1)}, u32[]{:S(2)}, u32[]{:S(2)}) %collective-permute-start.3) | collective-permute-done | bytes 49184 | tf_op jit(solution)/shard_map/ppermute | solution.py:374
  25.6 3.0 %middle0.1 = (f32[3,32,128]{2,1,0:T(8,128)S(1)}, f32[16,8,128]{2,1,0:T(8,128)S(1)}, f32[9,8,128]{2,1,0:T(8,128)S(1)}, f32[2,3,8,128]{3,2,1,0:T(8,128)S(1)}, f32[...) custom-call(f32[18,32,128]{2,1,0:T(8,128)S(1)} %get-tuple-element.45.refs_0_, ...), custom_call_target="tpu_custom_call" | custom-call | tf_op jit(solution)/shard_map/middle0/pallas_call | solution.py:357
  28.5 0.1 collective-permute-start.4
  28.6 1.4 %collective-permute-start.5 = (f32[2,3,8,128]{3,2,1,0:T(8,128)S(1)}, f32[2,3,8,128]{3,2,1,0:T(8,128)S(1)}, u32[]{:S(2)}, u32[]{:S(2)}) collective-permute-start(f32[2,3,8,128]{3,2,1,0:T(8,128)S(1)} %get-tuple-element.71), channel_id=1, source_target_pairs={{4,0},{0,1},{6,2},{2,3},{8,4},{1,5},{10,6},{3,7},{12,8},{5,9},{14,... | collective-permute-start | bytes 73736 | tf_op jit(solution)/shard_map/ppermute | solution.py:370
  30.0 1.2 %collective-permute-done.4.refs_0_.refs_18_ = f32[2,3,8,128]{3,2,1,0:T(8,128)S(1)} collective-permute-done((f32[2,3,8,128]{3,2,1,0:T(8,128)S(1)}, f32[2,3,8,128]{3,2,1,0:T(8,128)S(1)}, u32[]{:S(2)}, u32[]{:S(2)}) %collective-permute-start.4) | collective-permute-done | bytes 24608 | tf_op jit(solution)/shard_map/ppermute | solution.py:369
  31.2 0.0 collective-permute-done.5.refs_1_.refs_19_
  31.2 2.9 %collective-permute-start.6 = (f32[2,3,8,128]{3,2,1,0:T(8,128)S(1)}, f32[2,3,8,128]{3,2,1,0:T(8,128)S(1)}, u32[]{:S(2)}, u32[]{:S(2)}) collective-permute-start(f32[2,3,8,128]{3,2,1,0:T(8,128)S(1)} %get-tuple-element.72), channel_id=1, source_target_pairs={{0,1},{1,0},{2,3},{3,2},{4,5},{5,4},{6,7},{7,6},{8,9},{9,8},{10,11... | collective-permute-start | bytes 73736 | tf_op jit(solution)/shard_map/ppermute | solution.py:374
  34.1 1.2 %collective-permute-start.7 = (f32[2,3,8,128]{3,2,1,0:T(8,128)S(1)}, f32[2,3,8,128]{3,2,1,0:T(8,128)S(1)}, u32[]{:S(2)}, u32[]{:S(2)}) collective-permute-start(f32[2,3,8,128]{3,2,1,0:T(8,128)S(1)} %get-tuple-element.73), channel_id=1, source_target_pairs={{0,3},{1,2},{2,1},{3,0},{4,7},{5,6},{6,5},{7,4},{8,11},{9,10},{10,... | collective-permute-start | bytes 73736 | tf_op jit(solution)/shard_map/ppermute | solution.py:374
  35.3 0.0 collective-permute-done.6.refs_20_
  35.3 2.1 %collective-permute-done.7.refs_21_ = f32[2,3,8,128]{3,2,1,0:T(8,128)S(1)} collective-permute-done((f32[2,3,8,128]{3,2,1,0:T(8,128)S(1)}, f32[2,3,8,128]{3,2,1,0:T(8,128)S(1)}, u32[]{:S(2)}, u32[]{:S(2)}) %collective-permute-start.7) | collective-permute-done | bytes 24608 | tf_op jit(solution)/shard_map/ppermute | solution.py:374
  37.4 3.0 %middle.2 = (f32[3,32,128]{2,1,0:T(8,128)S(1)}, f32[16,8,128]{2,1,0:T(8,128)S(1)}, f32[9,8,128]{2,1,0:T(8,128)S(1)}, f32[2,3,8,128]{3,2,1,0:T(8,128)S(1)}, f32[2,3,8,128]{3,2,1,0:T(8,128)S(1)}) custom-call(f32[18,32,128]{2,1,0:T(8,128)S(1)} %get-tuple-element.45.refs_0_, f32[18,32,128]{2,1,0:T(8,128)S(1)} %get-tuple-element.46.refs_1_, ...), custom_call_target="tpu_custom_call" | custom-call | tf_op jit(solution)/shard_map/middle/pallas_call | solution.py:357
  40.4 0.1 collective-permute-start.8
  40.4 1.4 %collective-permute-start.9 = (f32[2,3,8,128]{3,2,1,0:T(8,128)S(1)}, f32[2,3,8,128]{3,2,1,0:T(8,128)S(1)}, u32[]{:S(2)}, u32[]{:S(2)}) collective-permute-start(f32[2,3,8,128]{3,2,1,0:T(8,128)S(1)} %get-tuple-element.78), channel_id=1, source_target_pairs={{4,0},{0,1},{6,2},{2,3},{8,4},{1,5},{10,6},{3,7},{12,8},{5,9},{14,... | collective-permute-start | bytes 73736 | tf_op jit(solution)/shard_map/ppermute | solution.py:370
  41.8 1.2 %collective-permute-done.8.refs_0_.refs_18_ = f32[2,3,8,128]{3,2,1,0:T(8,128)S(1)} collective-permute-done((f32[2,3,8,128]{3,2,1,0:T(8,128)S(1)}, f32[2,3,8,128]{3,2,1,0:T(8,128)S(1)}, u32[]{:S(2)}, u32[]{:S(2)}) %collective-permute-start.8) | collective-permute-done | bytes 24608 | tf_op jit(solution)/shard_map/ppermute | solution.py:369
  43.1 0.0 collective-permute-done.9.refs_1_.refs_19_
  43.1 2.9 %collective-permute-start.10 = (f32[2,3,8,128]{3,2,1,0:T(8,128)S(1)}, f32[2,3,8,128]{3,2,1,0:T(8,128)S(1)}, u32[]{:S(2)}, u32[]{:S(2)}) collective-permute-start(f32[2,3,8,128]{3,2,1,0:T(8,128)S(1)} %get-tuple-element.79), channel_id=1, source_target_pairs={{0,1},{1,0},{2,3},{3,2},{4,5},{5,4},{6,7},{7,6},{8,9},{9,8},{10,11... | collective-permute-start | bytes 73736 | tf_op jit(solution)/shard_map/ppermute | solution.py:374
  45.9 1.2 %collective-permute-start.11 = (f32[2,3,8,128]{3,2,1,0:T(8,128)S(1)}, f32[2,3,8,128]{3,2,1,0:T(8,128)S(1)}, u32[]{:S(2)}, u32[]{:S(2)}) collective-permute-start(f32[2,3,8,128]{3,2,1,0:T(8,128)S(1)} %get-tuple-element.80), channel_id=1, source_target_pairs={{0,3},{1,2},{2,1},{3,0},{4,7},{5,6},{6,5},{7,4},{8,11},{9,10},{10,... | collective-permute-start | bytes 73736 | tf_op jit(solution)/shard_map/ppermute | solution.py:374
  47.1 0.0 collective-permute-done.10.refs_20_
  47.1 2.1 %collective-permute-done.11.refs_21_ = f32[2,3,8,128]{3,2,1,0:T(8,128)S(1)} collective-permute-done((f32[2,3,8,128]{3,2,1,0:T(8,128)S(1)}, f32[2,3,8,128]{3,2,1,0:T(8,128)S(1)}, u32[]{:S(2)}, u32[]{:S(2)}) %collective-permute-start.11) | collective-permute-done | bytes 24608 | tf_op jit(solution)/shard_map/ppermute | solution.py:374
  49.2 3.4 %middle.3 = (f32[3,32,128]{2,1,0:T(8,128)}, f32[16,8,128]{2,1,0:T(8,128)S(1)}, f32[9,8,128]{2,1,0:T(8,128)S(1)}, f32[2,3,8,128]{3,2,1,0:T(8,128)S(1)}, f32[2,3,8,128]{3,2,1,0:T(8,128)S(1)}) custom-call(f32[18,32,128]{2,1,0:T(8,128)S(1)} %get-tuple-element.45.refs_0_, f32[18,32,128]{2,1,0:T(8,128)S(1)} %get-tuple-element.46.refs_1_, ...), custom_call_target="tpu_custom_call" | custom-call | tf_op jit(solution)/shard_map/middle/pallas_call | solution.py:357
  52.6 0.1 collective-permute-start.12
  52.7 1.4 %collective-permute-start.13 = (f32[2,3,8,128]{3,2,1,0:T(8,128)S(1)}, f32[2,3,8,128]{3,2,1,0:T(8,128)S(1)}, u32[]{:S(2)}, u32[]{:S(2)}) collective-permute-start(f32[2,3,8,128]{3,2,1,0:T(8,128)S(1)} %get-tuple-element.84), channel_id=1, source_target_pairs={{4,0},{0,1},{6,2},{2,3},{8,4},{1,5},{10,6},{3,7},{12,8},{5,9},{14,... | collective-permute-start | bytes 73736 | tf_op jit(solution)/shard_map/ppermute | solution.py:370
  54.1 1.2 %collective-permute-done.12.refs_0_.ra = f32[2,3,8,128]{3,2,1,0:T(8,128)S(1)} collective-permute-done((f32[2,3,8,128]{3,2,1,0:T(8,128)S(1)}, f32[2,3,8,128]{3,2,1,0:T(8,128)S(1)}, u32[]{:S(2)}, u32[]{:S(2)}) %collective-permute-start.12) | collective-permute-done | bytes 24608 | tf_op jit(solution)/shard_map/ppermute | solution.py:369
  55.3 1.3 %collective-permute-start.14 = (f32[2,3,8,128]{3,2,1,0:T(8,128)S(1)}, f32[2,3,8,128]{3,2,1,0:T(8,128)S(1)}, u32[]{:S(2)}, u32[]{:S(2)}) collective-permute-start(f32[2,3,8,128]{3,2,1,0:T(8,128)S(1)} %get-tuple-element.86), channel_id=1, source_target_pairs={{0,1},{1,0},{2,3},{3,2},{4,5},{5,4},{6,7},{7,6},{8,9},{9,8},{10,11... | collective-permute-start | bytes 73736 | tf_op jit(solution)/shard_map/ppermute | solution.py:374
  56.6 1.2 %collective-permute-start.15 = (f32[2,3,8,128]{3,2,1,0:T(8,128)S(1)}, f32[2,3,8,128]{3,2,1,0:T(8,128)S(1)}, u32[]{:S(2)}, u32[]{:S(2)}) collective-permute-start(f32[2,3,8,128]{3,2,1,0:T(8,128)S(1)} %get-tuple-element.87), channel_id=1, source_target_pairs={{0,3},{1,2},{2,1},{3,0},{4,7},{5,6},{6,5},{7,4},{8,11},{9,10},{10,... | collective-permute-start | bytes 73736 | tf_op jit(solution)/shard_map/ppermute | solution.py:374
  57.8 0.0 collective-permute-done.14.qe
  57.8 2.1 %collective-permute-done.15.qo = f32[2,3,8,128]{3,2,1,0:T(8,128)S(1)} collective-permute-done((f32[2,3,8,128]{3,2,1,0:T(8,128)S(1)}, f32[2,3,8,128]{3,2,1,0:T(8,128)S(1)}, u32[]{:S(2)}, u32[]{:S(2)}) %collective-permute-start.15) | collective-permute-done | bytes 24608 | tf_op jit(solution)/shard_map/ppermute | solution.py:374
  59.9 0.7 %last.1 = f32[96,128]{1,0:T(8,128)} custom-call(f32[16,8,128]{2,1,0:T(8,128)S(1)} %get-tuple-element.82.refs_2_.own, f32[16,8,128]{2,1,0:T(8,128)S(1)} %get-tuple-element.59.refs_4_.refs_14_.v_own, f32[16,8,128]{2,1,0:T(8,128)S(1)} %get-tuple-element.60.refs_5_.refs_15_.m_own, f32[2,3,8,128]{3,2,1,0:T(8,128)S(1)} %collective-permute-done.12.refs_0_.ra, ...), custom_call_target="tpu_custom_call" | custom-call | tf_op jit(solution)/shard_map/last/pallas_call | solution.py:357
  (17 shorter events, 0.1 us)
Async XLA Ops:
  0.6 1.0 %copy-start = (f32[18,1,1,32,128]{4,3,2,1,0:T(8,128)S(1)}, f32[18,1,1,32,128]{4,3,2,1,0:T(8,128)}, u32[]{:S(2)}) copy-start(f32[18,1,1,32,128]{4,3,2,1,0:T(8,128)} %param.14) | copy-start | bytes 884740
  1.6 1.0 %copy-start.1 = (f32[18,1,1,32,128]{4,3,2,1,0:T(8,128)S(1)}, f32[18,1,1,32,128]{4,3,2,1,0:T(8,128)}, u32[]{:S(2)}) copy-start(f32[18,1,1,32,128]{4,3,2,1,0:T(8,128)} %param.15) | copy-start | bytes 884740
  2.6 0.9 %copy-start.2 = (f32[9,1,1,32,128]{4,3,2,1,0:T(8,128)S(1)}, f32[9,1,1,32,128]{4,3,2,1,0:T(8,128)}, u32[]{:S(2)}) copy-start(f32[9,1,1,32,128]{4,3,2,1,0:T(8,128)} %param.16) | copy-start | bytes 442372
  3.5 0.8 %copy-start.3 = (f32[3,1,1,32,128]{4,3,2,1,0:T(8,128)S(1)}, f32[3,1,1,32,128]{4,3,2,1,0:T(8,128)}, u32[]{:S(2)}) copy-start(f32[3,1,1,32,128]{4,3,2,1,0:T(8,128)} %param.19) | copy-start | bytes 147460
  4.3 0.8 %copy-start.4 = (f32[6,1,1,2048]{3,2,1,0:T(1,128)S(1)}, f32[6,1,1,2048]{3,2,1,0:T(1,128)}, u32[]{:S(2)}) copy-start(f32[6,1,1,2048]{3,2,1,0:T(1,128)} %param.12) | copy-start | bytes 147460
  5.1 0.8 %copy-start.5 = (f32[6,1,1,2048]{3,2,1,0:T(1,128)S(1)}, f32[6,1,1,2048]{3,2,1,0:T(1,128)}, u32[]{:S(2)}) copy-start(f32[6,1,1,2048]{3,2,1,0:T(1,128)} %param.13) | copy-start | bytes 147460
  5.9 0.8 %copy-start.6 = (f32[3,1,1,32,128]{4,3,2,1,0:T(8,128)S(1)}, f32[3,1,1,32,128]{4,3,2,1,0:T(8,128)}, u32[]{:S(2)}) copy-start(f32[3,1,1,32,128]{4,3,2,1,0:T(8,128)} %param.17) | copy-start | bytes 147460
  6.7 0.7 %copy-start.7 = (s32[1,1,32,128]{3,2,1,0:T(8,128)S(1)}, s32[1,1,32,128]{3,2,1,0:T(8,128)}, u32[]{:S(2)}) copy-start(s32[1,1,32,128]{3,2,1,0:T(8,128)} %param.20) | copy-start | bytes 49156
  7.4 0.7 %copy-start.8 = (s32[1,1,32,128]{3,2,1,0:T(8,128)S(1)}, s32[1,1,32,128]{3,2,1,0:T(8,128)}, u32[]{:S(2)}) copy-start(s32[1,1,32,128]{3,2,1,0:T(8,128)} %param.21) | copy-start | bytes 49156
  8.1 0.7 %copy-start.9 = (s32[1,1,32,128]{3,2,1,0:T(8,128)S(1)}, s32[1,1,32,128]{3,2,1,0:T(8,128)}, u32[]{:S(2)}) copy-start(s32[1,1,32,128]{3,2,1,0:T(8,128)} %param.22) | copy-start | bytes 49156
  8.8 0.7 %copy-start.10 = (f32[1,1,32,128]{3,2,1,0:T(8,128)S(1)}, f32[1,1,32,128]{3,2,1,0:T(8,128)}, u32[]{:S(2)}) copy-start(f32[1,1,32,128]{3,2,1,0:T(8,128)} %param.18) | copy-start | bytes 49156
  9.5 0.7 %copy-start.11 = (s32[1,1,32,128]{3,2,1,0:T(8,128)S(1)}, s32[1,1,32,128]{3,2,1,0:T(8,128)}, u32[]{:S(2)}) copy-start(s32[1,1,32,128]{3,2,1,0:T(8,128)} %param.23) | copy-start | bytes 49156
  14.7 3.6 %collective-permute-start = (f32[4,3,8,128]{3,2,1,0:T(8,128)S(1)}, f32[4,3,8,128]{3,2,1,0:T(8,128)S(1)}, u32[]{:S(2)}, u32[]{:S(2)}) collective-permute-start(f32[4,3,8,128]{3,2,1,0:T(8,128)S(1)} %get-tuple-element.61), channel_id=1, source_target_pairs={{0,4},{1,0},{2,6},{3,2},{4,8},{5,1},{6,10},{7,3},{8,12},{9,5},{10,... | collective-permute-start | bytes 147464 | tf_op jit(solution)/shard_map/ppermute | solution.py:369
  14.8 3.7 %collective-permute-start.1 = (f32[4,3,8,128]{3,2,1,0:T(8,128)S(1)}, f32[4,3,8,128]{3,2,1,0:T(8,128)S(1)}, u32[]{:S(2)}, u32[]{:S(2)}) collective-permute-start(f32[4,3,8,128]{3,2,1,0:T(8,128)S(1)} %get-tuple-element.62), channel_id=1, source_target_pairs={{4,0},{0,1},{6,2},{2,3},{8,4},{1,5},{10,6},{3,7},{12,8},{5,9},{14,... | collective-permute-start | bytes 147464 | tf_op jit(solution)/shard_map/ppermute | solution.py:370
  18.6 4.6 %collective-permute-start.2 = (f32[4,3,8,128]{3,2,1,0:T(8,128)S(1)}, f32[4,3,8,128]{3,2,1,0:T(8,128)S(1)}, u32[]{:S(2)}, u32[]{:S(2)}) collective-permute-start(f32[4,3,8,128]{3,2,1,0:T(8,128)S(1)} %get-tuple-element.63), channel_id=1, source_target_pairs={{0,1},{1,0},{2,3},{3,2},{4,5},{5,4},{6,7},{7,6},{8,9},{9,8},{10,11... | collective-permute-start | bytes 147464 | tf_op jit(solution)/shard_map/ppermute | solution.py:374
  22.0 3.5 %collective-permute-start.3 = (f32[4,3,8,128]{3,2,1,0:T(8,128)S(1)}, f32[4,3,8,128]{3,2,1,0:T(8,128)S(1)}, u32[]{:S(2)}, u32[]{:S(2)}) collective-permute-start(f32[4,3,8,128]{3,2,1,0:T(8,128)S(1)} %get-tuple-element.64), channel_id=1, source_target_pairs={{0,3},{1,2},{2,1},{3,0},{4,7},{5,6},{6,5},{7,4},{8,11},{9,10},{10,... | collective-permute-start | bytes 147464 | tf_op jit(solution)/shard_map/ppermute | solution.py:374
  28.5 2.7 %collective-permute-start.4 = (f32[2,3,8,128]{3,2,1,0:T(8,128)S(1)}, f32[2,3,8,128]{3,2,1,0:T(8,128)S(1)}, u32[]{:S(2)}, u32[]{:S(2)}) collective-permute-start(f32[2,3,8,128]{3,2,1,0:T(8,128)S(1)} %get-tuple-element.70), channel_id=1, source_target_pairs={{0,4},{1,0},{2,6},{3,2},{4,8},{5,1},{6,10},{7,3},{8,12},{9,5},{10,... | collective-permute-start | bytes 73736 | tf_op jit(solution)/shard_map/ppermute | solution.py:369
  28.6 2.6 %collective-permute-start.5 = (f32[2,3,8,128]{3,2,1,0:T(8,128)S(1)}, f32[2,3,8,128]{3,2,1,0:T(8,128)S(1)}, u32[]{:S(2)}, u32[]{:S(2)}) collective-permute-start(f32[2,3,8,128]{3,2,1,0:T(8,128)S(1)} %get-tuple-element.71), channel_id=1, source_target_pairs={{4,0},{0,1},{6,2},{2,3},{8,4},{1,5},{10,6},{3,7},{12,8},{5,9},{14,... | collective-permute-start | bytes 73736 | tf_op jit(solution)/shard_map/ppermute | solution.py:370
  31.2 4.0 %collective-permute-start.6 = (f32[2,3,8,128]{3,2,1,0:T(8,128)S(1)}, f32[2,3,8,128]{3,2,1,0:T(8,128)S(1)}, u32[]{:S(2)}, u32[]{:S(2)}) collective-permute-start(f32[2,3,8,128]{3,2,1,0:T(8,128)S(1)} %get-tuple-element.72), channel_id=1, source_target_pairs={{0,1},{1,0},{2,3},{3,2},{4,5},{5,4},{6,7},{7,6},{8,9},{9,8},{10,11... | collective-permute-start | bytes 73736 | tf_op jit(solution)/shard_map/ppermute | solution.py:374
  34.1 3.3 %collective-permute-start.7 = (f32[2,3,8,128]{3,2,1,0:T(8,128)S(1)}, f32[2,3,8,128]{3,2,1,0:T(8,128)S(1)}, u32[]{:S(2)}, u32[]{:S(2)}) collective-permute-start(f32[2,3,8,128]{3,2,1,0:T(8,128)S(1)} %get-tuple-element.73), channel_id=1, source_target_pairs={{0,3},{1,2},{2,1},{3,0},{4,7},{5,6},{6,5},{7,4},{8,11},{9,10},{10,... | collective-permute-start | bytes 73736 | tf_op jit(solution)/shard_map/ppermute | solution.py:374
  40.4 2.7 %collective-permute-start.8 = (f32[2,3,8,128]{3,2,1,0:T(8,128)S(1)}, f32[2,3,8,128]{3,2,1,0:T(8,128)S(1)}, u32[]{:S(2)}, u32[]{:S(2)}) collective-permute-start(f32[2,3,8,128]{3,2,1,0:T(8,128)S(1)} %get-tuple-element.77), channel_id=1, source_target_pairs={{0,4},{1,0},{2,6},{3,2},{4,8},{5,1},{6,10},{7,3},{8,12},{9,5},{10,... | collective-permute-start | bytes 73736 | tf_op jit(solution)/shard_map/ppermute | solution.py:369
  40.4 2.6 %collective-permute-start.9 = (f32[2,3,8,128]{3,2,1,0:T(8,128)S(1)}, f32[2,3,8,128]{3,2,1,0:T(8,128)S(1)}, u32[]{:S(2)}, u32[]{:S(2)}) collective-permute-start(f32[2,3,8,128]{3,2,1,0:T(8,128)S(1)} %get-tuple-element.78), channel_id=1, source_target_pairs={{4,0},{0,1},{6,2},{2,3},{8,4},{1,5},{10,6},{3,7},{12,8},{5,9},{14,... | collective-permute-start | bytes 73736 | tf_op jit(solution)/shard_map/ppermute | solution.py:370
  43.1 4.0 %collective-permute-start.10 = (f32[2,3,8,128]{3,2,1,0:T(8,128)S(1)}, f32[2,3,8,128]{3,2,1,0:T(8,128)S(1)}, u32[]{:S(2)}, u32[]{:S(2)}) collective-permute-start(f32[2,3,8,128]{3,2,1,0:T(8,128)S(1)} %get-tuple-element.79), channel_id=1, source_target_pairs={{0,1},{1,0},{2,3},{3,2},{4,5},{5,4},{6,7},{7,6},{8,9},{9,8},{10,11... | collective-permute-start | bytes 73736 | tf_op jit(solution)/shard_map/ppermute | solution.py:374
  45.9 3.3 %collective-permute-start.11 = (f32[2,3,8,128]{3,2,1,0:T(8,128)S(1)}, f32[2,3,8,128]{3,2,1,0:T(8,128)S(1)}, u32[]{:S(2)}, u32[]{:S(2)}) collective-permute-start(f32[2,3,8,128]{3,2,1,0:T(8,128)S(1)} %get-tuple-element.80), channel_id=1, source_target_pairs={{0,3},{1,2},{2,1},{3,0},{4,7},{5,6},{6,5},{7,4},{8,11},{9,10},{10,... | collective-permute-start | bytes 73736 | tf_op jit(solution)/shard_map/ppermute | solution.py:374
  52.6 2.7 %collective-permute-start.12 = (f32[2,3,8,128]{3,2,1,0:T(8,128)S(1)}, f32[2,3,8,128]{3,2,1,0:T(8,128)S(1)}, u32[]{:S(2)}, u32[]{:S(2)}) collective-permute-start(f32[2,3,8,128]{3,2,1,0:T(8,128)S(1)} %get-tuple-element.83), channel_id=1, source_target_pairs={{0,4},{1,0},{2,6},{3,2},{4,8},{5,1},{6,10},{7,3},{8,12},{9,5},{10,... | collective-permute-start | bytes 73736 | tf_op jit(solution)/shard_map/ppermute | solution.py:369
  52.7 2.6 %collective-permute-start.13 = (f32[2,3,8,128]{3,2,1,0:T(8,128)S(1)}, f32[2,3,8,128]{3,2,1,0:T(8,128)S(1)}, u32[]{:S(2)}, u32[]{:S(2)}) collective-permute-start(f32[2,3,8,128]{3,2,1,0:T(8,128)S(1)} %get-tuple-element.84), channel_id=1, source_target_pairs={{4,0},{0,1},{6,2},{2,3},{8,4},{1,5},{10,6},{3,7},{12,8},{5,9},{14,... | collective-permute-start | bytes 73736 | tf_op jit(solution)/shard_map/ppermute | solution.py:370
  55.3 2.5 %collective-permute-start.14 = (f32[2,3,8,128]{3,2,1,0:T(8,128)S(1)}, f32[2,3,8,128]{3,2,1,0:T(8,128)S(1)}, u32[]{:S(2)}, u32[]{:S(2)}) collective-permute-start(f32[2,3,8,128]{3,2,1,0:T(8,128)S(1)} %get-tuple-element.86), channel_id=1, source_target_pairs={{0,1},{1,0},{2,3},{3,2},{4,5},{5,4},{6,7},{7,6},{8,9},{9,8},{10,11... | collective-permute-start | bytes 73736 | tf_op jit(solution)/shard_map/ppermute | solution.py:374
  56.6 3.3 %collective-permute-start.15 = (f32[2,3,8,128]{3,2,1,0:T(8,128)S(1)}, f32[2,3,8,128]{3,2,1,0:T(8,128)S(1)}, u32[]{:S(2)}, u32[]{:S(2)}) collective-permute-start(f32[2,3,8,128]{3,2,1,0:T(8,128)S(1)} %get-tuple-element.87), channel_id=1, source_target_pairs={{0,3},{1,2},{2,1},{3,0},{4,7},{5,6},{6,5},{7,4},{8,11},{9,10},{10,... | collective-permute-start | bytes 73736 | tf_op jit(solution)/shard_map/ppermute | solution.py:374

commit v2 on v1

--- a/solution.py
+++ b/solution.py
@@ -376,6 +376,7 @@
     sources = (body_a, body_b, active, impulse0, jac_a, jac_b, start, minv, precond, bias, friction, sticking)
     like = lambda a: arr(a.shape, a.dtype)
     kept = (jac_a, jac_b, precond, bias, friction, sticking, active, impulse0)
+    sources = [pltpu.with_memory_space_constraint(a, pltpu.HBM) for a in sources]
     made = call(
         first_kernel,
         (*map(like, kept), ids_t, ids_t, hot_t, hot_t, own_t, halo_t, own_t, own_t, message(4), message(4)),

time: 61.3 us -> 50.9 us (0.83)
  local copies, waits for them, and re-layouts: 9.6 us -> 0 us
    unnamed x24 -> x0, local copies, waits for them, and re-layouts: 9.6 us -> none
where the time goes in v2:
time: 50.9 us; the launch traced here: 50.7 us
  starting transfers between devices  21.7 us (43%)
  Pallas kernels  14.3 us (28%)
  waiting for transfers between devices  13.9 us (27%)
  between operations  0.69 us (1%)
    ppermute x8, starting transfers between devices, exchange(): return (ra, rb, lax.ppermute(ye, 'gy', near), lax.ppermute(yo, 'gy', far))  15.1 us
    pallas_call x9, Pallas kernels, call(): pl.pallas_call(kernel, out_shape=outs, in_specs=[pl.BlockSpec(memory_spac...  14.3 us
    ppermute x8, waiting for transfers between devices, exchange(): return (ra, rb, lax.ppermute(ye, 'gy', near), lax.ppermute(yo, 'gy', far))  8.63 us
    ppermute x4, starting transfers between devices, exchange(): rb = lax.ppermute(xb, ('gx', 'gy'), down)  6.32 us
    ppermute x4, waiting for transfers between devices, exchange(): ra = lax.ppermute(xa, ('gx', 'gy'), up)  5.08 us
  transfers between devices with their start and end apart: 16, of which 9 were waited for; matrix products, arithmetic and copies ran while one was open for 0% of the time, Pallas kernels for 0%

profile of v2, /device:TPU:1, one launch (start us, length us, event | category | flops | bytes accessed | tf_op | source)
XLA Modules:
  0.0 50.7 jit_solution(16282440722031811629)
XLA Ops:
  0.6 4.5 %first.1 = (f32[18,32,128]{2,1,0:T(8,128)S(1)}, f32[18,32,128]{2,1,0:T(8,128)S(1)}, f32[9,32,128]{2,1,0:T(8,128)S(1)}, f32[3,32,128]{2,1,0:T(8,128)S(1)}, f32[32...) custom-call(s32[32,128]{1,0:T(8,128)} %bitcast.24, ...), custom_call_target="tpu_custom_call" | custom-call | tf_op jit(solution)/shard_map/first/pallas_call | solution.py:357
  5.2 0.1 collective-permute-start
  5.3 2.1 %collective-permute-start.1 = (f32[4,3,8,128]{3,2,1,0:T(8,128)S(1)}, f32[4,3,8,128]{3,2,1,0:T(8,128)S(1)}, u32[]{:S(2)}, u32[]{:S(2)}) collective-permute-start(f32[4,3,8,128]{3,2,1,0:T(8,128)S(1)} %get-tuple-element.62), channel_id=1, source_target_pairs={{4,0},{0,1},{6,2},{2,3},{8,4},{1,5},{10,6},{3,7},{12,8},{5,9},{14,... | collective-permute-start | bytes 147464 | tf_op jit(solution)/shard_map/ppermute | solution.py:370
  7.4 1.4 %collective-permute-done.refs_0_.refs_16_ = f32[4,3,8,128]{3,2,1,0:T(8,128)S(1)} collective-permute-done((f32[4,3,8,128]{3,2,1,0:T(8,128)S(1)}, f32[4,3,8,128]{3,2,1,0:T(8,128)S(1)}, u32[]{:S(2)}, u32[]{:S(2)}) %collective-permute-start) | collective-permute-done | bytes 49184 | tf_op jit(solution)/shard_map/ppermute | solution.py:369
  8.8 0.2 collective-permute-done.1.refs_1_.refs_17_
  9.0 3.4 %collective-permute-start.2 = (f32[4,3,8,128]{3,2,1,0:T(8,128)S(1)}, f32[4,3,8,128]{3,2,1,0:T(8,128)S(1)}, u32[]{:S(2)}, u32[]{:S(2)}) collective-permute-start(f32[4,3,8,128]{3,2,1,0:T(8,128)S(1)} %get-tuple-element.63), channel_id=1, source_target_pairs={{0,1},{1,0},{2,3},{3,2},{4,5},{5,4},{6,7},{7,6},{8,9},{9,8},{10,11... | collective-permute-start | bytes 147464 | tf_op jit(solution)/shard_map/ppermute | solution.py:374
  12.5 1.2 %collective-permute-start.3 = (f32[4,3,8,128]{3,2,1,0:T(8,128)S(1)}, f32[4,3,8,128]{3,2,1,0:T(8,128)S(1)}, u32[]{:S(2)}, u32[]{:S(2)}) collective-permute-start(f32[4,3,8,128]{3,2,1,0:T(8,128)S(1)} %get-tuple-element.64), channel_id=1, source_target_pairs={{0,3},{1,2},{2,1},{3,0},{4,7},{5,6},{6,5},{7,4},{8,11},{9,10},{10,... | collective-permute-start | bytes 147464 | tf_op jit(solution)/shard_map/ppermute | solution.py:374
  13.6 0.0 collective-permute-done.2.refs_18_
  13.6 2.4 %collective-permute-done.3.refs_19_ = f32[4,3,8,128]{3,2,1,0:T(8,128)S(1)} collective-permute-done((f32[4,3,8,128]{3,2,1,0:T(8,128)S(1)}, f32[4,3,8,128]{3,2,1,0:T(8,128)S(1)}, u32[]{:S(2)}, u32[]{:S(2)}) %collective-permute-start.3) | collective-permute-done | bytes 49184 | tf_op jit(solution)/shard_map/ppermute | solution.py:374
  16.0 2.9 %middle0.1 = (f32[3,32,128]{2,1,0:T(8,128)S(1)}, f32[16,8,128]{2,1,0:T(8,128)S(1)}, f32[9,8,128]{2,1,0:T(8,128)S(1)}, f32[2,3,8,128]{3,2,1,0:T(8,128)S(1)}, f32[...) custom-call(f32[18,32,128]{2,1,0:T(8,128)S(1)} %get-tuple-element.45.refs_0_, ...), custom_call_target="tpu_custom_call" | custom-call | tf_op jit(solution)/shard_map/middle0/pallas_call | solution.py:357
  18.8 0.1 collective-permute-start.4
  18.9 1.4 %collective-permute-start.5 = (f32[2,3,8,128]{3,2,1,0:T(8,128)S(1)}, f32[2,3,8,128]{3,2,1,0:T(8,128)S(1)}, u32[]{:S(2)}, u32[]{:S(2)}) collective-permute-start(f32[2,3,8,128]{3,2,1,0:T(8,128)S(1)} %get-tuple-element.71), channel_id=1, source_target_pairs={{4,0},{0,1},{6,2},{2,3},{8,4},{1,5},{10,6},{3,7},{12,8},{5,9},{14,... | collective-permute-start | bytes 73736 | tf_op jit(solution)/shard_map/ppermute | solution.py:370
  20.3 1.2 %collective-permute-done.4.refs_0_.refs_18_ = f32[2,3,8,128]{3,2,1,0:T(8,128)S(1)} collective-permute-done((f32[2,3,8,128]{3,2,1,0:T(8,128)S(1)}, f32[2,3,8,128]{3,2,1,0:T(8,128)S(1)}, u32[]{:S(2)}, u32[]{:S(2)}) %collective-permute-start.4) | collective-permute-done | bytes 24608 | tf_op jit(solution)/shard_map/ppermute | solution.py:369
  21.5 0.0 collective-permute-done.5.refs_1_.refs_19_
  21.6 2.9 %collective-permute-start.6 = (f32[2,3,8,128]{3,2,1,0:T(8,128)S(1)}, f32[2,3,8,128]{3,2,1,0:T(8,128)S(1)}, u32[]{:S(2)}, u32[]{:S(2)}) collective-permute-start(f32[2,3,8,128]{3,2,1,0:T(8,128)S(1)} %get-tuple-element.72), channel_id=1, source_target_pairs={{0,1},{1,0},{2,3},{3,2},{4,5},{5,4},{6,7},{7,6},{8,9},{9,8},{10,11... | collective-permute-start | bytes 73736 | tf_op jit(solution)/shard_map/ppermute | solution.py:374
  24.4 1.2 %collective-permute-start.7 = (f32[2,3,8,128]{3,2,1,0:T(8,128)S(1)}, f32[2,3,8,128]{3,2,1,0:T(8,128)S(1)}, u32[]{:S(2)}, u32[]{:S(2)}) collective-permute-start(f32[2,3,8,128]{3,2,1,0:T(8,128)S(1)} %get-tuple-element.73), channel_id=1, source_target_pairs={{0,3},{1,2},{2,1},{3,0},{4,7},{5,6},{6,5},{7,4},{8,11},{9,10},{10,... | collective-permute-start | bytes 73736 | tf_op jit(solution)/shard_map/ppermute | solution.py:374
  25.6 0.0 collective-permute-done.6.refs_20_
  25.6 2.1 %collective-permute-done.7.refs_21_ = f32[2,3,8,128]{3,2,1,0:T(8,128)S(1)} collective-permute-done((f32[2,3,8,128]{3,2,1,0:T(8,128)S(1)}, f32[2,3,8,128]{3,2,1,0:T(8,128)S(1)}, u32[]{:S(2)}, u32[]{:S(2)}) %collective-permute-start.7) | collective-permute-done | bytes 24608 | tf_op jit(solution)/shard_map/ppermute | solution.py:374
  27.7 2.9 %middle.2 = (f32[3,32,128]{2,1,0:T(8,128)S(1)}, f32[16,8,128]{2,1,0:T(8,128)S(1)}, f32[9,8,128]{2,1,0:T(8,128)S(1)}, f32[2,3,8,128]{3,2,1,0:T(8,128)S(1)}, f32[2,3,8,128]{3,2,1,0:T(8,128)S(1)}) custom-call(f32[18,32,128]{2,1,0:T(8,128)S(1)} %get-tuple-element.45.refs_0_, f32[18,32,128]{2,1,0:T(8,128)S(1)} %get-tuple-element.46.refs_1_, ...), custom_call_target="tpu_custom_call" | custom-call | tf_op jit(solution)/shard_map/middle/pallas_call | solution.py:357
  30.6 0.1 collective-permute-start.8
  30.6 1.4 %collective-permute-start.9 = (f32[2,3,8,128]{3,2,1,0:T(8,128)S(1)}, f32[2,3,8,128]{3,2,1,0:T(8,128)S(1)}, u32[]{:S(2)}, u32[]{:S(2)}) collective-permute-start(f32[2,3,8,128]{3,2,1,0:T(8,128)S(1)} %get-tuple-element.78), channel_id=1, source_target_pairs={{4,0},{0,1},{6,2},{2,3},{8,4},{1,5},{10,6},{3,7},{12,8},{5,9},{14,... | collective-permute-start | bytes 73736 | tf_op jit(solution)/shard_map/ppermute | solution.py:370
  32.0 1.2 %collective-permute-done.8.refs_0_.refs_18_ = f32[2,3,8,128]{3,2,1,0:T(8,128)S(1)} collective-permute-done((f32[2,3,8,128]{3,2,1,0:T(8,128)S(1)}, f32[2,3,8,128]{3,2,1,0:T(8,128)S(1)}, u32[]{:S(2)}, u32[]{:S(2)}) %collective-permute-start.8) | collective-permute-done | bytes 24608 | tf_op jit(solution)/shard_map/ppermute | solution.py:369
  33.3 0.0 collective-permute-done.9.refs_1_.refs_19_
  33.3 2.9 %collective-permute-start.10 = (f32[2,3,8,128]{3,2,1,0:T(8,128)S(1)}, f32[2,3,8,128]{3,2,1,0:T(8,128)S(1)}, u32[]{:S(2)}, u32[]{:S(2)}) collective-permute-start(f32[2,3,8,128]{3,2,1,0:T(8,128)S(1)} %get-tuple-element.79), channel_id=1, source_target_pairs={{0,1},{1,0},{2,3},{3,2},{4,5},{5,4},{6,7},{7,6},{8,9},{9,8},{10,11... | collective-permute-start | bytes 73736 | tf_op jit(solution)/shard_map/ppermute | solution.py:374
  36.1 1.2 %collective-permute-start.11 = (f32[2,3,8,128]{3,2,1,0:T(8,128)S(1)}, f32[2,3,8,128]{3,2,1,0:T(8,128)S(1)}, u32[]{:S(2)}, u32[]{:S(2)}) collective-permute-start(f32[2,3,8,128]{3,2,1,0:T(8,128)S(1)} %get-tuple-element.80), channel_id=1, source_target_pairs={{0,3},{1,2},{2,1},{3,0},{4,7},{5,6},{6,5},{7,4},{8,11},{9,10},{10,... | collective-permute-start | bytes 73736 | tf_op jit(solution)/shard_map/ppermute | solution.py:374
  37.3 0.0 collective-permute-done.10.refs_20_
  37.3 2.1 %collective-permute-done.11.refs_21_ = f32[2,3,8,128]{3,2,1,0:T(8,128)S(1)} collective-permute-done((f32[2,3,8,128]{3,2,1,0:T(8,128)S(1)}, f32[2,3,8,128]{3,2,1,0:T(8,128)S(1)}, u32[]{:S(2)}, u32[]{:S(2)}) %collective-permute-start.11) | collective-permute-done | bytes 24608 | tf_op jit(solution)/shard_map/ppermute | solution.py:374
  39.4 3.3 %middle.3 = (f32[3,32,128]{2,1,0:T(8,128)}, f32[16,8,128]{2,1,0:T(8,128)S(1)}, f32[9,8,128]{2,1,0:T(8,128)S(1)}, f32[2,3,8,128]{3,2,1,0:T(8,128)S(1)}, f32[2,3,8,128]{3,2,1,0:T(8,128)S(1)}) custom-call(f32[18,32,128]{2,1,0:T(8,128)S(1)} %get-tuple-element.45.refs_0_, f32[18,32,128]{2,1,0:T(8,128)S(1)} %get-tuple-element.46.refs_1_, ...), custom_call_target="tpu_custom_call" | custom-call | tf_op jit(solution)/shard_map/middle/pallas_call | solution.py:357
  42.7 0.1 collective-permute-start.12
  42.8 1.4 %collective-permute-start.13 = (f32[2,3,8,128]{3,2,1,0:T(8,128)S(1)}, f32[2,3,8,128]{3,2,1,0:T(8,128)S(1)}, u32[]{:S(2)}, u32[]{:S(2)}) collective-permute-start(f32[2,3,8,128]{3,2,1,0:T(8,128)S(1)} %get-tuple-element.84), channel_id=1, source_target_pairs={{4,0},{0,1},{6,2},{2,3},{8,4},{1,5},{10,6},{3,7},{12,8},{5,9},{14,... | collective-permute-start | bytes 73736 | tf_op jit(solution)/shard_map/ppermute | solution.py:370
  44.2 1.2 %collective-permute-done.12.refs_0_.ra = f32[2,3,8,128]{3,2,1,0:T(8,128)S(1)} collective-permute-done((f32[2,3,8,128]{3,2,1,0:T(8,128)S(1)}, f32[2,3,8,128]{3,2,1,0:T(8,128)S(1)}, u32[]{:S(2)}, u32[]{:S(2)}) %collective-permute-start.12) | collective-permute-done | bytes 24608 | tf_op jit(solution)/shard_map/ppermute | solution.py:369
  45.4 0.0 collective-permute-done.13.refs_1_.rb
  45.4 1.3 %collective-permute-start.14 = (f32[2,3,8,128]{3,2,1,0:T(8,128)S(1)}, f32[2,3,8,128]{3,2,1,0:T(8,128)S(1)}, u32[]{:S(2)}, u32[]{:S(2)}) collective-permute-start(f32[2,3,8,128]{3,2,1,0:T(8,128)S(1)} %get-tuple-element.86), channel_id=1, source_target_pairs={{0,1},{1,0},{2,3},{3,2},{4,5},{5,4},{6,7},{7,6},{8,9},{9,8},{10,11... | collective-permute-start | bytes 73736 | tf_op jit(solution)/shard_map/ppermute | solution.py:374
  46.7 1.2 %collective-permute-start.15 = (f32[2,3,8,128]{3,2,1,0:T(8,128)S(1)}, f32[2,3,8,128]{3,2,1,0:T(8,128)S(1)}, u32[]{:S(2)}, u32[]{:S(2)}) collective-permute-start(f32[2,3,8,128]{3,2,1,0:T(8,128)S(1)} %get-tuple-element.87), channel_id=1, source_target_pairs={{0,3},{1,2},{2,1},{3,0},{4,7},{5,6},{6,5},{7,4},{8,11},{9,10},{10,... | collective-permute-start | bytes 73736 | tf_op jit(solution)/shard_map/ppermute | solution.py:374
  47.9 0.0 collective-permute-done.14.qe
  47.9 2.1 %collective-permute-done.15.qo = f32[2,3,8,128]{3,2,1,0:T(8,128)S(1)} collective-permute-done((f32[2,3,8,128]{3,2,1,0:T(8,128)S(1)}, f32[2,3,8,128]{3,2,1,0:T(8,128)S(1)}, u32[]{:S(2)}, u32[]{:S(2)}) %collective-permute-start.15) | collective-permute-done | bytes 24608 | tf_op jit(solution)/shard_map/ppermute | solution.py:374
  50.0 0.7 %last.1 = f32[96,128]{1,0:T(8,128)} custom-call(f32[16,8,128]{2,1,0:T(8,128)S(1)} %get-tuple-element.82.refs_2_.own, f32[16,8,128]{2,1,0:T(8,128)S(1)} %get-tuple-element.59.refs_4_.refs_14_.v_own, f32[16,8,128]{2,1,0:T(8,128)S(1)} %get-tuple-element.60.refs_5_.refs_15_.m_own, f32[2,3,8,128]{3,2,1,0:T(8,128)S(1)} %collective-permute-done.12.refs_0_.ra, ...), custom_call_target="tpu_custom_call" | custom-call | tf_op jit(solution)/shard_map/last/pallas_call | solution.py:357
  (4 shorter events, 0.0 us)
Async XLA Ops:
  5.2 3.6 %collective-permute-start = (f32[4,3,8,128]{3,2,1,0:T(8,128)S(1)}, f32[4,3,8,128]{3,2,1,0:T(8,128)S(1)}, u32[]{:S(2)}, u32[]{:S(2)}) collective-permute-start(f32[4,3,8,128]{3,2,1,0:T(8,128)S(1)} %get-tuple-element.61), channel_id=1, source_target_pairs={{0,4},{1,0},{2,6},{3,2},{4,8},{5,1},{6,10},{7,3},{8,12},{9,5},{10,... | collective-permute-start | bytes 147464 | tf_op jit(solution)/shard_map/ppermute | solution.py:369
  5.3 3.7 %collective-permute-start.1 = (f32[4,3,8,128]{3,2,1,0:T(8,128)S(1)}, f32[4,3,8,128]{3,2,1,0:T(8,128)S(1)}, u32[]{:S(2)}, u32[]{:S(2)}) collective-permute-start(f32[4,3,8,128]{3,2,1,0:T(8,128)S(1)} %get-tuple-element.62), channel_id=1, source_target_pairs={{4,0},{0,1},{6,2},{2,3},{8,4},{1,5},{10,6},{3,7},{12,8},{5,9},{14,... | collective-permute-start | bytes 147464 | tf_op jit(solution)/shard_map/ppermute | solution.py:370
  9.0 4.6 %collective-permute-start.2 = (f32[4,3,8,128]{3,2,1,0:T(8,128)S(1)}, f32[4,3,8,128]{3,2,1,0:T(8,128)S(1)}, u32[]{:S(2)}, u32[]{:S(2)}) collective-permute-start(f32[4,3,8,128]{3,2,1,0:T(8,128)S(1)} %get-tuple-element.63), channel_id=1, source_target_pairs={{0,1},{1,0},{2,3},{3,2},{4,5},{5,4},{6,7},{7,6},{8,9},{9,8},{10,11... | collective-permute-start | bytes 147464 | tf_op jit(solution)/shard_map/ppermute | solution.py:374
  12.5 3.5 %collective-permute-start.3 = (f32[4,3,8,128]{3,2,1,0:T(8,128)S(1)}, f32[4,3,8,128]{3,2,1,0:T(8,128)S(1)}, u32[]{:S(2)}, u32[]{:S(2)}) collective-permute-start(f32[4,3,8,128]{3,2,1,0:T(8,128)S(1)} %get-tuple-element.64), channel_id=1, source_target_pairs={{0,3},{1,2},{2,1},{3,0},{4,7},{5,6},{6,5},{7,4},{8,11},{9,10},{10,... | collective-permute-start | bytes 147464 | tf_op jit(solution)/shard_map/ppermute | solution.py:374
  18.8 2.7 %collective-permute-start.4 = (f32[2,3,8,128]{3,2,1,0:T(8,128)S(1)}, f32[2,3,8,128]{3,2,1,0:T(8,128)S(1)}, u32[]{:S(2)}, u32[]{:S(2)}) collective-permute-start(f32[2,3,8,128]{3,2,1,0:T(8,128)S(1)} %get-tuple-element.70), channel_id=1, source_target_pairs={{0,4},{1,0},{2,6},{3,2},{4,8},{5,1},{6,10},{7,3},{8,12},{9,5},{10,... | collective-permute-start | bytes 73736 | tf_op jit(solution)/shard_map/ppermute | solution.py:369
  18.9 2.6 %collective-permute-start.5 = (f32[2,3,8,128]{3,2,1,0:T(8,128)S(1)}, f32[2,3,8,128]{3,2,1,0:T(8,128)S(1)}, u32[]{:S(2)}, u32[]{:S(2)}) collective-permute-start(f32[2,3,8,128]{3,2,1,0:T(8,128)S(1)} %get-tuple-element.71), channel_id=1, source_target_pairs={{4,0},{0,1},{6,2},{2,3},{8,4},{1,5},{10,6},{3,7},{12,8},{5,9},{14,... | collective-permute-start | bytes 73736 | tf_op jit(solution)/shard_map/ppermute | solution.py:370
  21.6 4.0 %collective-permute-start.6 = (f32[2,3,8,128]{3,2,1,0:T(8,128)S(1)}, f32[2,3,8,128]{3,2,1,0:T(8,128)S(1)}, u32[]{:S(2)}, u32[]{:S(2)}) collective-permute-start(f32[2,3,8,128]{3,2,1,0:T(8,128)S(1)} %get-tuple-element.72), channel_id=1, source_target_pairs={{0,1},{1,0},{2,3},{3,2},{4,5},{5,4},{6,7},{7,6},{8,9},{9,8},{10,11... | collective-permute-start | bytes 73736 | tf_op jit(solution)/shard_map/ppermute | solution.py:374
  24.4 3.3 %collective-permute-start.7 = (f32[2,3,8,128]{3,2,1,0:T(8,128)S(1)}, f32[2,3,8,128]{3,2,1,0:T(8,128)S(1)}, u32[]{:S(2)}, u32[]{:S(2)}) collective-permute-start(f32[2,3,8,128]{3,2,1,0:T(8,128)S(1)} %get-tuple-element.73), channel_id=1, source_target_pairs={{0,3},{1,2},{2,1},{3,0},{4,7},{5,6},{6,5},{7,4},{8,11},{9,10},{10,... | collective-permute-start | bytes 73736 | tf_op jit(solution)/shard_map/ppermute | solution.py:374
  30.6 2.7 %collective-permute-start.8 = (f32[2,3,8,128]{3,2,1,0:T(8,128)S(1)}, f32[2,3,8,128]{3,2,1,0:T(8,128)S(1)}, u32[]{:S(2)}, u32[]{:S(2)}) collective-permute-start(f32[2,3,8,128]{3,2,1,0:T(8,128)S(1)} %get-tuple-element.77), channel_id=1, source_target_pairs={{0,4},{1,0},{2,6},{3,2},{4,8},{5,1},{6,10},{7,3},{8,12},{9,5},{10,... | collective-permute-start | bytes 73736 | tf_op jit(solution)/shard_map/ppermute | solution.py:369
  30.6 2.6 %collective-permute-start.9 = (f32[2,3,8,128]{3,2,1,0:T(8,128)S(1)}, f32[2,3,8,128]{3,2,1,0:T(8,128)S(1)}, u32[]{:S(2)}, u32[]{:S(2)}) collective-permute-start(f32[2,3,8,128]{3,2,1,0:T(8,128)S(1)} %get-tuple-element.78), channel_id=1, source_target_pairs={{4,0},{0,1},{6,2},{2,3},{8,4},{1,5},{10,6},{3,7},{12,8},{5,9},{14,... | collective-permute-start | bytes 73736 | tf_op jit(solution)/shard_map/ppermute | solution.py:370
  33.3 4.0 %collective-permute-start.10 = (f32[2,3,8,128]{3,2,1,0:T(8,128)S(1)}, f32[2,3,8,128]{3,2,1,0:T(8,128)S(1)}, u32[]{:S(2)}, u32[]{:S(2)}) collective-permute-start(f32[2,3,8,128]{3,2,1,0:T(8,128)S(1)} %get-tuple-element.79), channel_id=1, source_target_pairs={{0,1},{1,0},{2,3},{3,2},{4,5},{5,4},{6,7},{7,6},{8,9},{9,8},{10,11... | collective-permute-start | bytes 73736 | tf_op jit(solution)/shard_map/ppermute | solution.py:374
  36.1 3.3 %collective-permute-start.11 = (f32[2,3,8,128]{3,2,1,0:T(8,128)S(1)}, f32[2,3,8,128]{3,2,1,0:T(8,128)S(1)}, u32[]{:S(2)}, u32[]{:S(2)}) collective-permute-start(f32[2,3,8,128]{3,2,1,0:T(8,128)S(1)} %get-tuple-element.80), channel_id=1, source_target_pairs={{0,3},{1,2},{2,1},{3,0},{4,7},{5,6},{6,5},{7,4},{8,11},{9,10},{10,... | collective-permute-start | bytes 73736 | tf_op jit(solution)/shard_map/ppermute | solution.py:374
  42.7 2.7 %collective-permute-start.12 = (f32[2,3,8,128]{3,2,1,0:T(8,128)S(1)}, f32[2,3,8,128]{3,2,1,0:T(8,128)S(1)}, u32[]{:S(2)}, u32[]{:S(2)}) collective-permute-start(f32[2,3,8,128]{3,2,1,0:T(8,128)S(1)} %get-tuple-element.83), channel_id=1, source_target_pairs={{0,4},{1,0},{2,6},{3,2},{4,8},{5,1},{6,10},{7,3},{8,12},{9,5},{10,... | collective-permute-start | bytes 73736 | tf_op jit(solution)/shard_map/ppermute | solution.py:369
  42.8 2.6 %collective-permute-start.13 = (f32[2,3,8,128]{3,2,1,0:T(8,128)S(1)}, f32[2,3,8,128]{3,2,1,0:T(8,128)S(1)}, u32[]{:S(2)}, u32[]{:S(2)}) collective-permute-start(f32[2,3,8,128]{3,2,1,0:T(8,128)S(1)} %get-tuple-element.84), channel_id=1, source_target_pairs={{4,0},{0,1},{6,2},{2,3},{8,4},{1,5},{10,6},{3,7},{12,8},{5,9},{14,... | collective-permute-start | bytes 73736 | tf_op jit(solution)/shard_map/ppermute | solution.py:370
  45.4 2.5 %collective-permute-start.14 = (f32[2,3,8,128]{3,2,1,0:T(8,128)S(1)}, f32[2,3,8,128]{3,2,1,0:T(8,128)S(1)}, u32[]{:S(2)}, u32[]{:S(2)}) collective-permute-start(f32[2,3,8,128]{3,2,1,0:T(8,128)S(1)} %get-tuple-element.86), channel_id=1, source_target_pairs={{0,1},{1,0},{2,3},{3,2},{4,5},{5,4},{6,7},{7,6},{8,9},{9,8},{10,11... | collective-permute-start | bytes 73736 | tf_op jit(solution)/shard_map/ppermute | solution.py:374
  46.7 3.3 %collective-permute-start.15 = (f32[2,3,8,128]{3,2,1,0:T(8,128)S(1)}, f32[2,3,8,128]{3,2,1,0:T(8,128)S(1)}, u32[]{:S(2)}, u32[]{:S(2)}) collective-permute-start(f32[2,3,8,128]{3,2,1,0:T(8,128)S(1)} %get-tuple-element.87), channel_id=1, source_target_pairs={{0,3},{1,2},{2,1},{3,0},{4,7},{5,6},{6,5},{7,4},{8,11},{9,10},{10,... | collective-permute-start | bytes 73736 | tf_op jit(solution)/shard_map/ppermute | solution.py:374

commit v3 on v2

--- a/solution.py
+++ b/solution.py
@@ -86,13 +86,15 @@
     return ref[pl.ds(r, 1), :]
 
 
-def build_onehot(index_ref, onehot_ref):
-    rows = index_ref.shape[0]
-    base = lax.broadcasted_iota(jnp.int32, (NBND, LANES), 0)
+def build_onehot(index, onehot_ref):
+    rows = index.shape[0]
+    lane = (index & (NBND - 1)).astype(jnp.float32).T
+    base = lax.broadcasted_iota(jnp.int32, (LANES, NBND), 1).astype(jnp.float32).astype(jnp.bfloat16)
+    one, zero = jnp.ones((), jnp.bfloat16), jnp.zeros((), jnp.bfloat16)
     for r in range(rows):
-        q = row_of(index_ref, r) & (NBND - 1)
-        hit = (base == q).astype(jnp.float32).astype(jnp.bfloat16)
-        onehot_ref[:, r * LANES : (r + 1) * LANES] = hit
+        q = jnp.broadcast_to(lane[:, r : r + 1], (LANES, LANES)).astype(jnp.bfloat16)
+        q = jnp.concatenate([q, q], axis=1)
+        onehot_ref[r * LANES : (r + 1) * LANES, :] = jnp.where(base == q, one, zero)
 
 
 def forces(lam, jac_ref, force_ref):
@@ -125,7 +127,7 @@
 
 
 def scatter(lam, jac_a, jac_b, id_a, id_b, hot_a, hot_b, force, left_a, left_b):
-    contract = (((1,), (1,)), ((), ()))
+    contract = (((1,), (0,)), ((), ()))
     forces(lam, jac_a, force)
     spread(force, id_a, left_a, OWN_HEADS)
     sum_a = lax.dot_general(left_a[...], hot_a[...], contract, preferred_element_type=jnp.float32)
@@ -148,8 +150,8 @@
         up = (tiles[6], tiles[7], jnp.where(high, tiles[-1], 0.0))
         down = (tiles[0], tiles[1], jnp.where(high, 0.0, tiles[-1]))
         for k in range(3):
-            a_ref[p, k] = jnp.where(even, up[k], down[k])
-            b_ref[p, k] = jnp.where(even, down[k], up[k])
+            a_ref[p, k] = jnp.where(even, down[k], up[k])
+            b_ref[p, k] = jnp.where(even, up[k], down[k])
 
 
 def is_even():
@@ -167,9 +169,9 @@
         def pick(first, second):
             return lambda p, k: jnp.where(even, first[p, k], second[p, k])
 
-        self.x_low, self.x_high = pick(a_ref, b_ref), pick(b_ref, a_ref)
+        self.x_low, self.x_high = pick(b_ref, a_ref), pick(a_ref, b_ref)
         if e_ref is not None:
-            self.y_high, self.y_low = pick(e_ref, o_ref), pick(o_ref, e_ref)
+            self.y_high, self.y_low = pick(o_ref, e_ref), pick(e_ref, o_ref)
 
     def plane(self, p):
         tiles = []
@@ -196,10 +198,10 @@
     even = is_even()
     copies[0].wait()
     id_a[...] = table_index(body_a[...])
-    build_onehot(id_a, hot_a)
+    build_onehot(id_a[...], hot_a)
     copies[1].wait()
     id_b[...] = table_index(body_b[...])
-    build_onehot(id_b, hot_b)
+    build_onehot(id_b[...], hot_b)
     for copy in copies[2:6]:
         copy.wait()
     active = act[...].astype(jnp.float32)
@@ -226,8 +228,8 @@
         corner = jnp.where(lane < 2 * CORNER, came.x_high(p, 2), came.x_low(p, 2))
         for k in range(2):
             minus, plus = sources[p][2 + k], sources[p][4 + k]
-            e_ref[p, k] = jnp.where(even, plus, minus)
-            o_ref[p, k] = jnp.where(even, minus, plus)
+            e_ref[p, k] = jnp.where(even, minus, plus)
+            o_ref[p, k] = jnp.where(even, plus, minus)
         e_ref[p, 2] = corner
         o_ref[p, 2] = corner
 
@@ -236,16 +238,20 @@
 
 
 def gather(table, index, codes):
-    lane = index & (LANES - 1)
-    code = index >> 7
-    values = [jnp.zeros(index.shape, jnp.float32) for _ in range(DOF)]
-    for c, t in codes:
-        mask = code == c
+    values = [[] for _ in range(DOF)]
+    for g in range(0, index.shape[0], 8):
+        lane = index[g : g + 8] & (LANES - 1)
+        code = index[g : g + 8] >> 7
+        part = [jnp.zeros(lane.shape, jnp.float32) for _ in range(DOF)]
+        for c, t in codes:
+            mask = code == c
+            for d in range(DOF):
+                row = jnp.broadcast_to(table[t, d : d + 1, :], lane.shape)
+                got = jnp.take_along_axis(row, lane, axis=1, mode="promise_in_bounds")
+                part[d] = jnp.where(mask, got, part[d])
         for d in range(DOF):
-            row = jnp.broadcast_to(table[t, d : d + 1, :], index.shape)
-            got = jnp.take_along_axis(row, lane, axis=1, mode="promise_in_bounds")
-            values[d] = jnp.where(mask, got, values[d])
-    return values
+            values[d].append(part[d])
+    return [jnp.concatenate(v, axis=0) for v in values]
 
 
 def relative(jac, values):
@@ -318,7 +324,7 @@
     up = []
     for x in range(nx):
         for y in range(ny):
-            to = x + 1 if y % 2 == 0 else x - 1
+            to = x + 1 if y % 2 == 1 else x - 1
             goal = (to, y) if 0 <= to < nx else (x, y ^ 1)
             up.append((x * ny + y, goal[0] * ny + goal[1]))
     down = [(b, a) for a, b in up]
@@ -344,7 +350,7 @@
     vmem = pl.BlockSpec(memory_space=pltpu.VMEM)
     own_t, halo_t = arr((OWN_TILES, 8, lanes), f32), arr((HALO_TILES, 8, lanes), f32)
     lam_t = arr((ROWS, rows, lanes), f32)
-    ids_t, hot_t = arr((rows, lanes), i32), arr((NBND, contacts), bf16)
+    ids_t, hot_t = arr((rows, lanes), i32), arr((contacts, NBND), bf16)
     message = lambda p: arr((p, 3, 8, lanes), f32)
     work = [
         pltpu.VMEM((8 * rows, lanes), f32),
@@ -371,7 +377,7 @@
         ye, yo = call(
             lambda *refs: turn_kernel(planes, *refs), (message(planes), message(planes)), [], "turn", ra, rb, *sources
         )
-        return ra, rb, lax.ppermute(ye, "gy", near), lax.ppermute(yo, "gy", far)
+        return ra, rb, lax.ppermute(ye, "gy", far), lax.ppermute(yo, "gy", near)
 
     sources = (body_a, body_b, active, impulse0, jac_a, jac_b, start, minv, precond, bias, friction, sticking)
     like = lambda a: arr(a.shape, a.dtype)

time: 50.9 us -> 43.3 us (0.85)
  starting transfers between devices: 21.7 us -> 13.5 us
  waiting for transfers between devices: 13.9 us -> 18.2 us
  Pallas kernels: 14.3 us -> 10.6 us
    ppermute x8, starting transfers between devices: 15.1 us -> 6.54 us  [exchange(): return (ra, rb, lax.ppermute(ye, 'gy', far), lax.ppermute(yo, 'gy', near))]
    ppermute x4, waiting for transfers between devices: 0.2 us -> 6.98 us  [exchange(): rb = lax.ppermute(xb, ('gx', 'gy'), down)]
    ppermute x4, starting transfers between devices: 0.3 us -> 6.97 us  [exchange(): ra = lax.ppermute(xa, ('gx', 'gy'), up)]
    ppermute x4, starting transfers between devices: 6.32 us -> 0.01 us  [exchange(): rb = lax.ppermute(xb, ('gx', 'gy'), down)]
    pallas_call x9, Pallas kernels: 14.3 us -> 10.6 us  [call(): pl.pallas_call(kernel, out_shape=outs, in_specs=[pl.BlockSpec(memory_spac...]
    ppermute x8, waiting for transfers between devices: 8.63 us -> 7.26 us  [exchange(): return (ra, rb, lax.ppermute(ye, 'gy', far), lax.ppermute(yo, 'gy', near))]
    ppermute x4, waiting for transfers between devices: 5.08 us -> 4.01 us  [exchange(): ra = lax.ppermute(xa, ('gx', 'gy'), up)]
  transfers between devices with their start and end apart: 16 -> 16, of which waited for: 9 -> 12; matrix products, arithmetic and copies ran while one was open for 0% -> 0% of each run, Pallas kernels for 0% -> 0%
where the time goes in v3:
time: 43.3 us; the launch traced here: 43 us
  waiting for transfers between devices  18.2 us (42%)
  starting transfers between devices  13.5 us (31%)
  Pallas kernels  10.6 us (24%)
  between operations  0.69 us (2%)
    pallas_call x9, Pallas kernels, call(): pl.pallas_call(kernel, out_shape=outs, in_specs=[pl.BlockSpec(memory_spac...  10.6 us
    ppermute x8, waiting for transfers between devices, exchange(): return (ra, rb, lax.ppermute(ye, 'gy', far), lax.ppermute(yo, 'gy', near))  7.26 us
    ppermute x4, waiting for transfers between devices, exchange(): rb = lax.ppermute(xb, ('gx', 'gy'), down)  6.98 us
    ppermute x4, starting transfers between devices, exchange(): ra = lax.ppermute(xa, ('gx', 'gy'), up)  6.97 us
    ppermute x8, starting transfers between devices, exchange(): return (ra, rb, lax.ppermute(ye, 'gy', far), lax.ppermute(yo, 'gy', near))  6.54 us
    ppermute x4, waiting for transfers between devices, exchange(): ra = lax.ppermute(xa, ('gx', 'gy'), up)  4.01 us
  transfers between devices with their start and end apart: 16, of which 12 were waited for; matrix products, arithmetic and copies ran while one was open for 0% of the time, Pallas kernels for 0%

profile of v3, /device:TPU:1, one launch (start us, length us, event | category | flops | bytes accessed | tf_op | source)
XLA Modules:
  0.0 43.0 jit_solution(8850095644178370243)
XLA Ops:
  0.6 3.2 %first.1 = (f32[18,32,128]{2,1,0:T(8,128)S(1)}, f32[18,32,128]{2,1,0:T(8,128)S(1)}, f32[9,32,128]{2,1,0:T(8,128)S(1)}, f32[3,32,128]{2,1,0:T(8,128)S(1)}, f32[32...) custom-call(s32[32,128]{1,0:T(8,128)} %bitcast.24, ...), custom_call_target="tpu_custom_call" | custom-call | tf_op jit(solution)/shard_map/first/pallas_call | solution.py:363
  3.9 2.1 %collective-permute-start = (f32[4,3,8,128]{3,2,1,0:T(8,128)S(1)}, f32[4,3,8,128]{3,2,1,0:T(8,128)S(1)}, u32[]{:S(2)}, u32[]{:S(2)}) collective-permute-start(f32[4,3,8,128]{3,2,1,0:T(8,128)S(1)} %get-tuple-element.61), channel_id=1, source_target_pairs={{0,1},{1,5},{2,3},{3,7},{4,0},{5,9},{6,2},{7,11},{8,4},{9,13},{10,... | collective-permute-start | bytes 147464 | tf_op jit(solution)/shard_map/ppermute | solution.py:375
  6.0 0.0 collective-permute-start.1
  6.0 1.2 %collective-permute-done.refs_0_.refs_16_ = f32[4,3,8,128]{3,2,1,0:T(8,128)S(1)} collective-permute-done((f32[4,3,8,128]{3,2,1,0:T(8,128)S(1)}, f32[4,3,8,128]{3,2,1,0:T(8,128)S(1)}, u32[]{:S(2)}, u32[]{:S(2)}) %collective-permute-start) | collective-permute-done | bytes 49184 | tf_op jit(solution)/shard_map/ppermute | solution.py:375
  7.2 1.8 %collective-permute-done.1.refs_1_.refs_17_ = f32[4,3,8,128]{3,2,1,0:T(8,128)S(1)} collective-permute-done((f32[4,3,8,128]{3,2,1,0:T(8,128)S(1)}, f32[4,3,8,128]{3,2,1,0:T(8,128)S(1)}, u32[]{:S(2)}, u32[]{:S(2)}) %collective-permute-start.1) | collective-permute-done | bytes 49184 | tf_op jit(solution)/shard_map/ppermute | solution.py:376
  9.0 2.1 %collective-permute-start.2 = (f32[4,3,8,128]{3,2,1,0:T(8,128)S(1)}, f32[4,3,8,128]{3,2,1,0:T(8,128)S(1)}, u32[]{:S(2)}, u32[]{:S(2)}) collective-permute-start(f32[4,3,8,128]{3,2,1,0:T(8,128)S(1)} %get-tuple-element.63), channel_id=1, source_target_pairs={{0,3},{1,2},{2,1},{3,0},{4,7},{5,6},{6,5},{7,4},{8,11},{9,10},{10,... | collective-permute-start | bytes 147464 | tf_op jit(solution)/shard_map/ppermute | solution.py:380
  11.0 0.1 collective-permute-start.3
  11.1 1.7 %collective-permute-done.2.refs_18_ = f32[4,3,8,128]{3,2,1,0:T(8,128)S(1)} collective-permute-done((f32[4,3,8,128]{3,2,1,0:T(8,128)S(1)}, f32[4,3,8,128]{3,2,1,0:T(8,128)S(1)}, u32[]{:S(2)}, u32[]{:S(2)}) %collective-permute-start.2) | collective-permute-done | bytes 49184 | tf_op jit(solution)/shard_map/ppermute | solution.py:380
  12.8 0.0 collective-permute-done.3.refs_19_
  12.8 2.1 %middle0.1 = (f32[3,32,128]{2,1,0:T(8,128)S(1)}, f32[16,8,128]{2,1,0:T(8,128)S(1)}, f32[9,8,128]{2,1,0:T(8,128)S(1)}, f32[2,3,8,128]{3,2,1,0:T(8,128)S(1)}, f32[...) custom-call(f32[18,32,128]{2,1,0:T(8,128)S(1)} %get-tuple-element.45.refs_0_, ...), custom_call_target="tpu_custom_call" | custom-call | tf_op jit(solution)/shard_map/middle0/pallas_call | solution.py:363
  14.9 1.8 %collective-permute-start.4 = (f32[2,3,8,128]{3,2,1,0:T(8,128)S(1)}, f32[2,3,8,128]{3,2,1,0:T(8,128)S(1)}, u32[]{:S(2)}, u32[]{:S(2)}) collective-permute-start(f32[2,3,8,128]{3,2,1,0:T(8,128)S(1)} %get-tuple-element.70), channel_id=1, source_target_pairs={{0,1},{1,5},{2,3},{3,7},{4,0},{5,9},{6,2},{7,11},{8,4},{9,13},{10,... | collective-permute-start | bytes 73736 | tf_op jit(solution)/shard_map/ppermute | solution.py:375
  16.7 0.0 collective-permute-start.5
  16.7 0.9 %collective-permute-done.4.refs_0_.refs_18_ = f32[2,3,8,128]{3,2,1,0:T(8,128)S(1)} collective-permute-done((f32[2,3,8,128]{3,2,1,0:T(8,128)S(1)}, f32[2,3,8,128]{3,2,1,0:T(8,128)S(1)}, u32[]{:S(2)}, u32[]{:S(2)}) %collective-permute-start.4) | collective-permute-done | bytes 24608 | tf_op jit(solution)/shard_map/ppermute | solution.py:375
  17.6 1.7 %collective-permute-done.5.refs_1_.refs_19_ = f32[2,3,8,128]{3,2,1,0:T(8,128)S(1)} collective-permute-done((f32[2,3,8,128]{3,2,1,0:T(8,128)S(1)}, f32[2,3,8,128]{3,2,1,0:T(8,128)S(1)}, u32[]{:S(2)}, u32[]{:S(2)}) %collective-permute-start.5) | collective-permute-done | bytes 24608 | tf_op jit(solution)/shard_map/ppermute | solution.py:376
  19.4 1.4 %collective-permute-start.6 = (f32[2,3,8,128]{3,2,1,0:T(8,128)S(1)}, f32[2,3,8,128]{3,2,1,0:T(8,128)S(1)}, u32[]{:S(2)}, u32[]{:S(2)}) collective-permute-start(f32[2,3,8,128]{3,2,1,0:T(8,128)S(1)} %get-tuple-element.72), channel_id=1, source_target_pairs={{0,3},{1,2},{2,1},{3,0},{4,7},{5,6},{6,5},{7,4},{8,11},{9,10},{10,... | collective-permute-start | bytes 73736 | tf_op jit(solution)/shard_map/ppermute | solution.py:380
  20.8 0.3 collective-permute-start.7
  21.1 1.6 %collective-permute-done.6.refs_20_ = f32[2,3,8,128]{3,2,1,0:T(8,128)S(1)} collective-permute-done((f32[2,3,8,128]{3,2,1,0:T(8,128)S(1)}, f32[2,3,8,128]{3,2,1,0:T(8,128)S(1)}, u32[]{:S(2)}, u32[]{:S(2)}) %collective-permute-start.6) | collective-permute-done | bytes 24608 | tf_op jit(solution)/shard_map/ppermute | solution.py:380
  22.7 0.0 collective-permute-done.7.refs_21_
  22.7 2.1 %middle.2 = (f32[3,32,128]{2,1,0:T(8,128)S(1)}, f32[16,8,128]{2,1,0:T(8,128)S(1)}, f32[9,8,128]{2,1,0:T(8,128)S(1)}, f32[2,3,8,128]{3,2,1,0:T(8,128)S(1)}, f32[2,3,8,128]{3,2,1,0:T(8,128)S(1)}) custom-call(f32[18,32,128]{2,1,0:T(8,128)S(1)} %get-tuple-element.45.refs_0_, f32[18,32,128]{2,1,0:T(8,128)S(1)} %get-tuple-element.46.refs_1_, ...), custom_call_target="tpu_custom_call" | custom-call | tf_op jit(solution)/shard_map/middle/pallas_call | solution.py:363
  24.7 1.5 %collective-permute-start.8 = (f32[2,3,8,128]{3,2,1,0:T(8,128)S(1)}, f32[2,3,8,128]{3,2,1,0:T(8,128)S(1)}, u32[]{:S(2)}, u32[]{:S(2)}) collective-permute-start(f32[2,3,8,128]{3,2,1,0:T(8,128)S(1)} %get-tuple-element.77), channel_id=1, source_target_pairs={{0,1},{1,5},{2,3},{3,7},{4,0},{5,9},{6,2},{7,11},{8,4},{9,13},{10,... | collective-permute-start | bytes 73736 | tf_op jit(solution)/shard_map/ppermute | solution.py:375
  26.2 0.0 collective-permute-start.9
  26.2 0.9 %collective-permute-done.8.refs_0_.refs_18_ = f32[2,3,8,128]{3,2,1,0:T(8,128)S(1)} collective-permute-done((f32[2,3,8,128]{3,2,1,0:T(8,128)S(1)}, f32[2,3,8,128]{3,2,1,0:T(8,128)S(1)}, u32[]{:S(2)}, u32[]{:S(2)}) %collective-permute-start.8) | collective-permute-done | bytes 24608 | tf_op jit(solution)/shard_map/ppermute | solution.py:375
  27.2 1.7 %collective-permute-done.9.refs_1_.refs_19_ = f32[2,3,8,128]{3,2,1,0:T(8,128)S(1)} collective-permute-done((f32[2,3,8,128]{3,2,1,0:T(8,128)S(1)}, f32[2,3,8,128]{3,2,1,0:T(8,128)S(1)}, u32[]{:S(2)}, u32[]{:S(2)}) %collective-permute-start.9) | collective-permute-done | bytes 24608 | tf_op jit(solution)/shard_map/ppermute | solution.py:376
  28.9 1.1 %collective-permute-start.10 = (f32[2,3,8,128]{3,2,1,0:T(8,128)S(1)}, f32[2,3,8,128]{3,2,1,0:T(8,128)S(1)}, u32[]{:S(2)}, u32[]{:S(2)}) collective-permute-start(f32[2,3,8,128]{3,2,1,0:T(8,128)S(1)} %get-tuple-element.79), channel_id=1, source_target_pairs={{0,3},{1,2},{2,1},{3,0},{4,7},{5,6},{6,5},{7,4},{8,11},{9,10},{10,... | collective-permute-start | bytes 73736 | tf_op jit(solution)/shard_map/ppermute | solution.py:380
  30.0 0.7 %collective-permute-start.11 = (f32[2,3,8,128]{3,2,1,0:T(8,128)S(1)}, f32[2,3,8,128]{3,2,1,0:T(8,128)S(1)}, u32[]{:S(2)}, u32[]{:S(2)}) collective-permute-start(f32[2,3,8,128]{3,2,1,0:T(8,128)S(1)} %get-tuple-element.80), channel_id=1, source_target_pairs={{0,1},{1,0},{2,3},{3,2},{4,5},{5,4},{6,7},{7,6},{8,9},{9,8},{10,11... | collective-permute-start | bytes 73736 | tf_op jit(solution)/shard_map/ppermute | solution.py:380
  30.7 1.5 %collective-permute-done.10.refs_20_ = f32[2,3,8,128]{3,2,1,0:T(8,128)S(1)} collective-permute-done((f32[2,3,8,128]{3,2,1,0:T(8,128)S(1)}, f32[2,3,8,128]{3,2,1,0:T(8,128)S(1)}, u32[]{:S(2)}, u32[]{:S(2)}) %collective-permute-start.10) | collective-permute-done | bytes 24608 | tf_op jit(solution)/shard_map/ppermute | solution.py:380
  32.2 0.0 collective-permute-done.11.refs_21_
  32.2 2.5 %middle.3 = (f32[3,32,128]{2,1,0:T(8,128)}, f32[16,8,128]{2,1,0:T(8,128)S(1)}, f32[9,8,128]{2,1,0:T(8,128)S(1)}, f32[2,3,8,128]{3,2,1,0:T(8,128)S(1)}, f32[2,3,8,128]{3,2,1,0:T(8,128)S(1)}) custom-call(f32[18,32,128]{2,1,0:T(8,128)S(1)} %get-tuple-element.45.refs_0_, f32[18,32,128]{2,1,0:T(8,128)S(1)} %get-tuple-element.46.refs_1_, ...), custom_call_target="tpu_custom_call" | custom-call | tf_op jit(solution)/shard_map/middle/pallas_call | solution.py:363
  34.7 1.6 %collective-permute-start.12 = (f32[2,3,8,128]{3,2,1,0:T(8,128)S(1)}, f32[2,3,8,128]{3,2,1,0:T(8,128)S(1)}, u32[]{:S(2)}, u32[]{:S(2)}) collective-permute-start(f32[2,3,8,128]{3,2,1,0:T(8,128)S(1)} %get-tuple-element.83), channel_id=1, source_target_pairs={{0,1},{1,5},{2,3},{3,7},{4,0},{5,9},{6,2},{7,11},{8,4},{9,13},{10,... | collective-permute-start | bytes 73736 | tf_op jit(solution)/shard_map/ppermute | solution.py:375
  36.3 0.0 collective-permute-start.13
  36.3 0.9 %collective-permute-done.12.refs_0_.ra = f32[2,3,8,128]{3,2,1,0:T(8,128)S(1)} collective-permute-done((f32[2,3,8,128]{3,2,1,0:T(8,128)S(1)}, f32[2,3,8,128]{3,2,1,0:T(8,128)S(1)}, u32[]{:S(2)}, u32[]{:S(2)}) %collective-permute-start.12) | collective-permute-done | bytes 24608 | tf_op jit(solution)/shard_map/ppermute | solution.py:375
  37.2 1.8 %collective-permute-done.13.refs_1_.rb = f32[2,3,8,128]{3,2,1,0:T(8,128)S(1)} collective-permute-done((f32[2,3,8,128]{3,2,1,0:T(8,128)S(1)}, f32[2,3,8,128]{3,2,1,0:T(8,128)S(1)}, u32[]{:S(2)}, u32[]{:S(2)}) %collective-permute-start.13) | collective-permute-done | bytes 24608 | tf_op jit(solution)/shard_map/ppermute | solution.py:376
  39.0 0.8 %collective-permute-start.14 = (f32[2,3,8,128]{3,2,1,0:T(8,128)S(1)}, f32[2,3,8,128]{3,2,1,0:T(8,128)S(1)}, u32[]{:S(2)}, u32[]{:S(2)}) collective-permute-start(f32[2,3,8,128]{3,2,1,0:T(8,128)S(1)} %get-tuple-element.86), channel_id=1, source_target_pairs={{0,3},{1,2},{2,1},{3,0},{4,7},{5,6},{6,5},{7,4},{8,11},{9,10},{10,... | collective-permute-start | bytes 73736 | tf_op jit(solution)/shard_map/ppermute | solution.py:380
  39.8 0.0 collective-permute-start.15
  39.8 2.5 %collective-permute-done.14.qe = f32[2,3,8,128]{3,2,1,0:T(8,128)S(1)} collective-permute-done((f32[2,3,8,128]{3,2,1,0:T(8,128)S(1)}, f32[2,3,8,128]{3,2,1,0:T(8,128)S(1)}, u32[]{:S(2)}, u32[]{:S(2)}) %collective-permute-start.14) | collective-permute-done | bytes 24608 | tf_op jit(solution)/shard_map/ppermute | solution.py:380
  42.3 0.0 collective-permute-done.15.qo
  42.3 0.7 %last.1 = f32[96,128]{1,0:T(8,128)} custom-call(f32[16,8,128]{2,1,0:T(8,128)S(1)} %get-tuple-element.82.refs_2_.own, f32[16,8,128]{2,1,0:T(8,128)S(1)} %get-tuple-element.59.refs_4_.refs_14_.v_own, f32[16,8,128]{2,1,0:T(8,128)S(1)} %get-tuple-element.60.refs_5_.refs_15_.m_own, f32[2,3,8,128]{3,2,1,0:T(8,128)S(1)} %collective-permute-done.12.refs_0_.ra, ...), custom_call_target="tpu_custom_call" | custom-call | tf_op jit(solution)/shard_map/last/pallas_call | solution.py:363
  (4 shorter events, 0.0 us)
Async XLA Ops:
  3.9 3.3 %collective-permute-start = (f32[4,3,8,128]{3,2,1,0:T(8,128)S(1)}, f32[4,3,8,128]{3,2,1,0:T(8,128)S(1)}, u32[]{:S(2)}, u32[]{:S(2)}) collective-permute-start(f32[4,3,8,128]{3,2,1,0:T(8,128)S(1)} %get-tuple-element.61), channel_id=1, source_target_pairs={{0,1},{1,5},{2,3},{3,7},{4,0},{5,9},{6,2},{7,11},{8,4},{9,13},{10,... | collective-permute-start | bytes 147464 | tf_op jit(solution)/shard_map/ppermute | solution.py:375
  6.0 2.9 %collective-permute-start.1 = (f32[4,3,8,128]{3,2,1,0:T(8,128)S(1)}, f32[4,3,8,128]{3,2,1,0:T(8,128)S(1)}, u32[]{:S(2)}, u32[]{:S(2)}) collective-permute-start(f32[4,3,8,128]{3,2,1,0:T(8,128)S(1)} %get-tuple-element.62), channel_id=1, source_target_pairs={{1,0},{5,1},{3,2},{7,3},{0,4},{9,5},{2,6},{11,7},{4,8},{13,9},{6,1... | collective-permute-start | bytes 147464 | tf_op jit(solution)/shard_map/ppermute | solution.py:376
  9.0 3.8 %collective-permute-start.2 = (f32[4,3,8,128]{3,2,1,0:T(8,128)S(1)}, f32[4,3,8,128]{3,2,1,0:T(8,128)S(1)}, u32[]{:S(2)}, u32[]{:S(2)}) collective-permute-start(f32[4,3,8,128]{3,2,1,0:T(8,128)S(1)} %get-tuple-element.63), channel_id=1, source_target_pairs={{0,3},{1,2},{2,1},{3,0},{4,7},{5,6},{6,5},{7,4},{8,11},{9,10},{10,... | collective-permute-start | bytes 147464 | tf_op jit(solution)/shard_map/ppermute | solution.py:380
  11.0 1.8 %collective-permute-start.3 = (f32[4,3,8,128]{3,2,1,0:T(8,128)S(1)}, f32[4,3,8,128]{3,2,1,0:T(8,128)S(1)}, u32[]{:S(2)}, u32[]{:S(2)}) collective-permute-start(f32[4,3,8,128]{3,2,1,0:T(8,128)S(1)} %get-tuple-element.64), channel_id=1, source_target_pairs={{0,1},{1,0},{2,3},{3,2},{4,5},{5,4},{6,7},{7,6},{8,9},{9,8},{10,11... | collective-permute-start | bytes 147464 | tf_op jit(solution)/shard_map/ppermute | solution.py:380
  14.9 2.7 %collective-permute-start.4 = (f32[2,3,8,128]{3,2,1,0:T(8,128)S(1)}, f32[2,3,8,128]{3,2,1,0:T(8,128)S(1)}, u32[]{:S(2)}, u32[]{:S(2)}) collective-permute-start(f32[2,3,8,128]{3,2,1,0:T(8,128)S(1)} %get-tuple-element.70), channel_id=1, source_target_pairs={{0,1},{1,5},{2,3},{3,7},{4,0},{5,9},{6,2},{7,11},{8,4},{9,13},{10,... | collective-permute-start | bytes 73736 | tf_op jit(solution)/shard_map/ppermute | solution.py:375
  16.7 2.7 %collective-permute-start.5 = (f32[2,3,8,128]{3,2,1,0:T(8,128)S(1)}, f32[2,3,8,128]{3,2,1,0:T(8,128)S(1)}, u32[]{:S(2)}, u32[]{:S(2)}) collective-permute-start(f32[2,3,8,128]{3,2,1,0:T(8,128)S(1)} %get-tuple-element.71), channel_id=1, source_target_pairs={{1,0},{5,1},{3,2},{7,3},{0,4},{9,5},{2,6},{11,7},{4,8},{13,9},{6,1... | collective-permute-start | bytes 73736 | tf_op jit(solution)/shard_map/ppermute | solution.py:376
  19.4 3.3 %collective-permute-start.6 = (f32[2,3,8,128]{3,2,1,0:T(8,128)S(1)}, f32[2,3,8,128]{3,2,1,0:T(8,128)S(1)}, u32[]{:S(2)}, u32[]{:S(2)}) collective-permute-start(f32[2,3,8,128]{3,2,1,0:T(8,128)S(1)} %get-tuple-element.72), channel_id=1, source_target_pairs={{0,3},{1,2},{2,1},{3,0},{4,7},{5,6},{6,5},{7,4},{8,11},{9,10},{10,... | collective-permute-start | bytes 73736 | tf_op jit(solution)/shard_map/ppermute | solution.py:380
  20.8 1.9 %collective-permute-start.7 = (f32[2,3,8,128]{3,2,1,0:T(8,128)S(1)}, f32[2,3,8,128]{3,2,1,0:T(8,128)S(1)}, u32[]{:S(2)}, u32[]{:S(2)}) collective-permute-start(f32[2,3,8,128]{3,2,1,0:T(8,128)S(1)} %get-tuple-element.73), channel_id=1, source_target_pairs={{0,1},{1,0},{2,3},{3,2},{4,5},{5,4},{6,7},{7,6},{8,9},{9,8},{10,11... | collective-permute-start | bytes 73736 | tf_op jit(solution)/shard_map/ppermute | solution.py:380
  24.7 2.4 %collective-permute-start.8 = (f32[2,3,8,128]{3,2,1,0:T(8,128)S(1)}, f32[2,3,8,128]{3,2,1,0:T(8,128)S(1)}, u32[]{:S(2)}, u32[]{:S(2)}) collective-permute-start(f32[2,3,8,128]{3,2,1,0:T(8,128)S(1)} %get-tuple-element.77), channel_id=1, source_target_pairs={{0,1},{1,5},{2,3},{3,7},{4,0},{5,9},{6,2},{7,11},{8,4},{9,13},{10,... | collective-permute-start | bytes 73736 | tf_op jit(solution)/shard_map/ppermute | solution.py:375
  26.2 2.7 %collective-permute-start.9 = (f32[2,3,8,128]{3,2,1,0:T(8,128)S(1)}, f32[2,3,8,128]{3,2,1,0:T(8,128)S(1)}, u32[]{:S(2)}, u32[]{:S(2)}) collective-permute-start(f32[2,3,8,128]{3,2,1,0:T(8,128)S(1)} %get-tuple-element.78), channel_id=1, source_target_pairs={{1,0},{5,1},{3,2},{7,3},{0,4},{9,5},{2,6},{11,7},{4,8},{13,9},{6,1... | collective-permute-start | bytes 73736 | tf_op jit(solution)/shard_map/ppermute | solution.py:376
  28.9 3.3 %collective-permute-start.10 = (f32[2,3,8,128]{3,2,1,0:T(8,128)S(1)}, f32[2,3,8,128]{3,2,1,0:T(8,128)S(1)}, u32[]{:S(2)}, u32[]{:S(2)}) collective-permute-start(f32[2,3,8,128]{3,2,1,0:T(8,128)S(1)} %get-tuple-element.79), channel_id=1, source_target_pairs={{0,3},{1,2},{2,1},{3,0},{4,7},{5,6},{6,5},{7,4},{8,11},{9,10},{10,... | collective-permute-start | bytes 73736 | tf_op jit(solution)/shard_map/ppermute | solution.py:380
  30.0 2.2 %collective-permute-start.11 = (f32[2,3,8,128]{3,2,1,0:T(8,128)S(1)}, f32[2,3,8,128]{3,2,1,0:T(8,128)S(1)}, u32[]{:S(2)}, u32[]{:S(2)}) collective-permute-start(f32[2,3,8,128]{3,2,1,0:T(8,128)S(1)} %get-tuple-element.80), channel_id=1, source_target_pairs={{0,1},{1,0},{2,3},{3,2},{4,5},{5,4},{6,7},{7,6},{8,9},{9,8},{10,11... | collective-permute-start | bytes 73736 | tf_op jit(solution)/shard_map/ppermute | solution.py:380
  34.7 2.5 %collective-permute-start.12 = (f32[2,3,8,128]{3,2,1,0:T(8,128)S(1)}, f32[2,3,8,128]{3,2,1,0:T(8,128)S(1)}, u32[]{:S(2)}, u32[]{:S(2)}) collective-permute-start(f32[2,3,8,128]{3,2,1,0:T(8,128)S(1)} %get-tuple-element.83), channel_id=1, source_target_pairs={{0,1},{1,5},{2,3},{3,7},{4,0},{5,9},{6,2},{7,11},{8,4},{9,13},{10,... | collective-permute-start | bytes 73736 | tf_op jit(solution)/shard_map/ppermute | solution.py:375
  36.3 2.7 %collective-permute-start.13 = (f32[2,3,8,128]{3,2,1,0:T(8,128)S(1)}, f32[2,3,8,128]{3,2,1,0:T(8,128)S(1)}, u32[]{:S(2)}, u32[]{:S(2)}) collective-permute-start(f32[2,3,8,128]{3,2,1,0:T(8,128)S(1)} %get-tuple-element.84), channel_id=1, source_target_pairs={{1,0},{5,1},{3,2},{7,3},{0,4},{9,5},{2,6},{11,7},{4,8},{13,9},{6,1... | collective-permute-start | bytes 73736 | tf_op jit(solution)/shard_map/ppermute | solution.py:376
  39.0 3.3 %collective-permute-start.14 = (f32[2,3,8,128]{3,2,1,0:T(8,128)S(1)}, f32[2,3,8,128]{3,2,1,0:T(8,128)S(1)}, u32[]{:S(2)}, u32[]{:S(2)}) collective-permute-start(f32[2,3,8,128]{3,2,1,0:T(8,128)S(1)} %get-tuple-element.86), channel_id=1, source_target_pairs={{0,3},{1,2},{2,1},{3,0},{4,7},{5,6},{6,5},{7,4},{8,11},{9,10},{10,... | collective-permute-start | bytes 73736 | tf_op jit(solution)/shard_map/ppermute | solution.py:380
  39.8 2.5 %collective-permute-start.15 = (f32[2,3,8,128]{3,2,1,0:T(8,128)S(1)}, f32[2,3,8,128]{3,2,1,0:T(8,128)S(1)}, u32[]{:S(2)}, u32[]{:S(2)}) collective-permute-start(f32[2,3,8,128]{3,2,1,0:T(8,128)S(1)} %get-tuple-element.87), channel_id=1, source_target_pairs={{0,1},{1,0},{2,3},{3,2},{4,5},{5,4},{6,7},{7,6},{8,9},{9,8},{10,11... | collective-permute-start | bytes 73736 | tf_op jit(solution)/shard_map/ppermute | solution.py:380

commit v4 on v3

--- a/solution.py
+++ b/solution.py
@@ -144,46 +144,88 @@
     return own, halo
 
 
-def put_x(even, planes, a_ref, b_ref):
-    high = lane_iota() >= 2 * CORNER
-    for p, tiles in enumerate(planes):
-        up = (tiles[6], tiles[7], jnp.where(high, tiles[-1], 0.0))
-        down = (tiles[0], tiles[1], jnp.where(high, 0.0, tiles[-1]))
-        for k in range(3):
-            a_ref[p, k] = jnp.where(even, down[k], up[k])
-            b_ref[p, k] = jnp.where(even, up[k], down[k])
-
-
 def is_even():
     return lax.rem(lax.axis_index("gy"), 2) == 0
 
 
-def corners_in(y_low, y_high, p):
-    lane = lane_iota()
-    odd = (lane & CORNER) != 0
-    return jnp.where(odd, pltpu.roll(y_high(p, 2), 96, 1), pltpu.roll(y_low(p, 2), 32, 1))
+GROUP = 32
+LAST_GROUP = 24
+
+
+def put_tiles(ref, base, tiles, end):
+    for k, tile in enumerate(tiles):
+        ref[base + DOF * k : base + DOF * (k + 1), :] = tile[:DOF]
+    rest = DOF * len(tiles)
+    ref[base + rest : base + end, :] = jnp.zeros((end - rest, LANES), jnp.float32)
+
+
+def put_x(even, groups, a_ref, b_ref):
+    high = lane_iota() >= 2 * CORNER
+    for g, (first, second) in enumerate(groups):
+        half = jnp.zeros_like(second[-1]) if first is None else first[-1]
+        up = [second[6], second[7], jnp.where(high, second[-1], pltpu.roll(half, 2 * CORNER, 1))]
+        down = [second[0], second[1], jnp.where(high, pltpu.roll(second[-1], 2 * CORNER, 1), half)]
+        if first is not None:
+            up, down = [first[6], first[7]] + up, [first[0], first[1]] + down
+        rows = a_ref.shape[0] // len(groups)
+        put_tiles(a_ref, g * rows, [jnp.where(even, d, u) for u, d in zip(up, down)], rows)
+        put_tiles(b_ref, g * rows, [jnp.where(even, u, d) for u, d in zip(up, down)], rows)
 
 
 class Received:
-    def __init__(self, even, a_ref, b_ref, e_ref, o_ref):
-        def pick(first, second):
-            return lambda p, k: jnp.where(even, first[p, k], second[p, k])
-
+    def __init__(self, even, a_ref, b_ref, e_ref=None, o_ref=None):
+        def pick(when, other):
+            def tile(row):
+                return jnp.where(even, when[pl.ds(row, 8), :], other[pl.ds(row, 8), :])
+
+            return tile
+
+        self.rows = GROUP if a_ref.shape[0] % GROUP == 0 else LAST_GROUP
+        self.tiles = 5 if self.rows == GROUP else 3
         self.x_low, self.x_high = pick(b_ref, a_ref), pick(a_ref, b_ref)
         if e_ref is not None:
-            self.y_high, self.y_low = pick(o_ref, e_ref), pick(e_ref, o_ref)
-
-    def plane(self, p):
-        tiles = []
-        for side in (self.x_low, self.y_low, self.y_high, self.x_high):
-            tiles += [side(p, 0), side(p, 1)]
-        return tiles + [corners_in(self.y_low, self.y_high, p)]
-
-
-def add_own(own, came):
-    out = [own[t] + came[t] for t in range(8)]
-    out += [own[t] for t in range(8, CORNER_TILE)]
-    return out + [own[CORNER_TILE] + came[HALO_CORNER]]
+            self.y_low, self.y_high = pick(e_ref, o_ref), pick(o_ref, e_ref)
+
+    def edge(self, side, plane):
+        place = 2 * (plane % 2) if self.tiles == 5 else 0
+        base = self.rows * (plane // 2) + DOF * place
+        return [side(base), side(base + DOF)]
+
+    def corner_row(self, plane):
+        return self.rows * (plane // 2) + DOF * (self.tiles - 1)
+
+    def x_corner(self, plane):
+        lane = lane_iota()
+        low, high = self.x_low(self.corner_row(plane)), self.x_high(self.corner_row(plane))
+        left = lane < 2 * CORNER
+        first = jnp.where(left, high, pltpu.roll(low, 2 * CORNER, 1))
+        second = jnp.where(left, pltpu.roll(high, 2 * CORNER, 1), low)
+        odd = (lane & CORNER) != 0
+        minus = jnp.where(odd, pltpu.roll(second, CORNER, 1), first)
+        plus = jnp.where(odd, first, pltpu.roll(second, 3 * CORNER, 1))
+        return minus, plus
+
+    def corner(self, plane):
+        odd = (lane_iota() & CORNER) != 0
+        low, high = self.y_low(self.corner_row(plane)), self.y_high(self.corner_row(plane))
+        if plane % 2:
+            return pltpu.roll(jnp.where(odd, high, low), 2 * CORNER, 1)
+        return jnp.where(odd, pltpu.roll(high, 3 * CORNER, 1), pltpu.roll(low, CORNER, 1))
+
+
+X_EDGES = (0, 1, 6, 7)
+Y_EDGES = (2, 3, 4, 5)
+INTERIOR = tuple(range(8, CORNER_TILE))
+
+
+def x_plane(came, plane):
+    low, high = came.edge(came.x_low, plane), came.edge(came.x_high, plane)
+    return dict(zip(X_EDGES, low + high))
+
+
+def y_plane(came, plane):
+    low, high = came.edge(came.y_low, plane), came.edge(came.y_high, plane)
+    return dict(zip(Y_EDGES, low + high))
 
 
 def first_kernel(*refs):
@@ -214,35 +256,35 @@
         own[t], v_own[t], m_own[t] = sums[t], v[t], m[t]
     for t in range(HALO_TILES):
         halo[t] = sums_halo[t]
-    put_x(even, [sums, sums_halo, v, m], xa, xb)
+    put_x(even, [(sums, sums_halo), (v, m)], xa, xb)
     for copy in copies[8:]:
         copy.wait()
 
 
-def turn_kernel(planes, ra, rb, *refs):
+def turn_kernel(ra, rb, *refs):
     sources, (e_ref, o_ref) = refs[:-2], refs[-2:]
     even = is_even()
-    came = Received(even, ra, rb, None, None)
-    lane = lane_iota()
-    for p in range(planes):
-        corner = jnp.where(lane < 2 * CORNER, came.x_high(p, 2), came.x_low(p, 2))
-        for k in range(2):
-            minus, plus = sources[p][2 + k], sources[p][4 + k]
-            e_ref[p, k] = jnp.where(even, minus, plus)
-            o_ref[p, k] = jnp.where(even, plus, minus)
-        e_ref[p, 2] = corner
-        o_ref[p, 2] = corner
-
-
-TILE_CODES = tuple((t, t) for t in range(24)) + ((31, 24),)
-
-
-def gather(table, index, codes):
+    came = Received(even, ra, rb)
+    groups = ra.shape[0] // came.rows
+    for g in range(groups):
+        planes = sources[2 * g : 2 * g + 2] if len(sources) > 1 else sources
+        minus = [p[t] for p in planes for t in (2, 3)]
+        plus = [p[t] for p in planes for t in (4, 5)]
+        corner = came.x_corner(2 * g)
+        minus, plus = minus + [corner[0]], plus + [corner[1]]
+        put_tiles(e_ref, g * came.rows, [jnp.where(even, m, p) for m, p in zip(minus, plus)], came.rows)
+        put_tiles(o_ref, g * came.rows, [jnp.where(even, p, m) for m, p in zip(minus, plus)], came.rows)
+
+
+def gather(table, index, codes, start=None):
     values = [[] for _ in range(DOF)]
     for g in range(0, index.shape[0], 8):
         lane = index[g : g + 8] & (LANES - 1)
         code = index[g : g + 8] >> 7
-        part = [jnp.zeros(lane.shape, jnp.float32) for _ in range(DOF)]
+        if start is None:
+            part = [jnp.zeros(lane.shape, jnp.float32) for _ in range(DOF)]
+        else:
+            part = [start[d, g : g + 8, :] for d in range(DOF)]
         for c, t in codes:
             mask = code == c
             for d in range(DOF):
@@ -254,6 +296,42 @@
     return [jnp.concatenate(v, axis=0) for v in values]
 
 
+def own_codes(tiles):
+    return tuple((t, t) for t in tiles)
+
+
+def halo_codes(tiles):
+    return tuple((OWN_TILES + (15 if t == HALO_CORNER else t), OWN_TILES + t) for t in tiles)
+
+
+def gather_both(table, id_a, id_b, own_tiles, halo_tiles, out, start):
+    part = (None, None) if start is None else (start.at[:DOF], start.at[DOF:])
+    for ref, ids, codes, first, base in (
+        (out, id_a, own_codes(own_tiles), part[0], 0),
+        (out, id_b, own_codes(own_tiles) + halo_codes(halo_tiles), part[1], DOF),
+    ):
+        for d, value in enumerate(gather(table, ids[...], codes, first)):
+            ref[base + d] = value
+
+
+def inner_kernel(own, v_own, m_own, id_a, id_b, out, table):
+    for t in INTERIOR:
+        table[t] = v_own[t] + m_own[t] * own[t]
+    gather_both(table, id_a, id_b, INTERIOR, (), out, None)
+
+
+def side_kernel(first, own, halo, v_own, m_own, id_a, id_b, part, ra, rb, *refs):
+    v_halo, m_halo, (out, table) = (None, None, refs) if first else (refs[0], refs[1], refs[2:])
+    came = Received(is_even(), ra, rb)
+    theirs, ours = x_plane(came, 0), x_plane(came, 1)
+    if first:
+        v_halo, m_halo = x_plane(came, 2), x_plane(came, 3)
+    for t in X_EDGES:
+        table[t] = v_own[t] + m_own[t] * (own[t] + ours[t])
+        table[OWN_TILES + t] = v_halo[t] + m_halo[t] * (halo[t] + theirs[t])
+    gather_both(table, id_a, id_b, X_EDGES, X_EDGES, out, part)
+
+
 def relative(jac, values):
     out = []
     for k in range(ROWS):
@@ -265,28 +343,32 @@
 
 
 def middle_kernel(
-    first, jac_a, jac_b, precond, bias, mu, stick, act, lam_in,
-    id_a, id_b, hot_a, hot_b, own, halo, v_own, m_own, *refs,
+    first, last, jac_a, jac_b, precond, bias, mu, stick, act, lam_in,
+    id_a, id_b, hot_a, hot_b, own, halo, v_own, m_own, part, ra, rb, qe, qo, *refs,
 ):
     if first:
-        ra, rb, qe, qo, lam_out, own_out, halo_out, xa, xb, v_halo, m_halo = refs[:11]
+        lam_out, own_out, halo_out, xa, xb, v_halo, m_halo = refs[:7]
     else:
-        v_halo, m_halo, ra, rb, qe, qo, lam_out, own_out, halo_out, xa, xb = refs[:11]
-    table, force, left_a, left_b = refs[11:]
+        v_halo, m_halo, lam_out, own_out, halo_out, xa, xb = refs[:7]
+    table, force, left_a, left_b = refs[7:]
     even = is_even()
     came = Received(even, ra, rb, qe, qo)
     if first:
         for ref, p in ((v_halo, 2), (m_halo, 3)):
-            for t, value in enumerate(came.plane(p)):
+            for t, value in (x_plane(came, p) | y_plane(came, p)).items():
                 ref[t] = value
-    total = add_own(own, came.plane(1))
-    total_halo = [a + b for a, b in zip([halo[t] for t in range(HALO_TILES)], came.plane(0))]
-    for t in range(OWN_TILES):
-        table[t] = v_own[t] + m_own[t] * total[t]
-    for t in range(HALO_TILES):
-        table[OWN_TILES + t] = v_halo[t] + m_halo[t] * total_halo[t]
-    u_a = relative(jac_a, gather(table, id_a[...], TILE_CODES[:OWN_TILES]))
-    u_b = relative(jac_b, gather(table, id_b[...], TILE_CODES))
+            ref[HALO_CORNER] = came.corner(p)
+    theirs, ours = y_plane(came, 0), y_plane(came, 1)
+    theirs[HALO_CORNER], ours[CORNER_TILE] = came.corner(0), came.corner(1)
+    for t, value in ours.items():
+        table[t] = v_own[t] + m_own[t] * (own[t] + value)
+    for t, value in theirs.items():
+        table[OWN_TILES + t] = v_halo[t] + m_halo[t] * (halo[t] + value)
+    late, late_halo = own_codes(ours), halo_codes(theirs)
+    v_a = gather(table, id_a[...], late, part.at[:DOF])
+    v_b = gather(table, id_b[...], late + late_halo, part.at[DOF:])
+    u_a = relative(jac_a, v_a)
+    u_b = relative(jac_b, v_b)
     target = [u_a[k] + u_b[k] + bias[k] for k in range(ROWS)]
     active = act[...].astype(jnp.float32)
     if first:
@@ -311,12 +393,20 @@
         own_out[t] = sums[t]
     for t in range(HALO_TILES):
         halo_out[t] = sums_halo[t]
-    put_x(even, [sums, sums_halo], xa, xb)
+    put_x(even, [(None if last else sums, sums_halo)], xa, xb)
+
+
+def keep_kernel(lam, out, sem):
+    copy = pltpu.make_async_copy(lam, out, sem)
+    copy.start()
+    copy.wait()
 
 
 def last_kernel(own, v_own, m_own, ra, rb, qe, qo, out):
     came = Received(is_even(), ra, rb, qe, qo)
-    total = add_own(own, came.plane(1))
+    ours = x_plane(came, 1) | y_plane(came, 1)
+    ours[CORNER_TILE] = came.corner(1)
+    total = [own[t] + ours[t] if t in ours else own[t] for t in range(OWN_TILES)]
     from_tables([v_own[t] + m_own[t] * total[t] for t in range(OWN_TILES)], out)
 
 
@@ -351,7 +441,7 @@
     own_t, halo_t = arr((OWN_TILES, 8, lanes), f32), arr((HALO_TILES, 8, lanes), f32)
     lam_t = arr((ROWS, rows, lanes), f32)
     ids_t, hot_t = arr((rows, lanes), i32), arr((contacts, NBND), bf16)
-    message = lambda p: arr((p, 3, 8, lanes), f32)
+    message = lambda r: arr((r, lanes), f32)
     work = [
         pltpu.VMEM((8 * rows, lanes), f32),
         pltpu.VMEM((16 * len(OWN_HEADS), contacts), bf16),
@@ -359,25 +449,24 @@
     ]
     table = [pltpu.VMEM((OWN_TILES + HALO_TILES, 8, lanes), f32)]
 
-    def call(kernel, outs, scratch, name, *operands, space=pltpu.VMEM):
+    def call(kernel, outs, scratch, name, *operands, space=pltpu.VMEM, out_space=pltpu.VMEM):
         return pl.pallas_call(
             kernel,
             out_shape=outs,
             in_specs=[pl.BlockSpec(memory_space=space)] * len(operands),
-            out_specs=jax.tree.map(lambda _: vmem, outs),
+            out_specs=jax.tree.map(lambda _: pl.BlockSpec(memory_space=out_space), outs),
             scratch_shapes=scratch,
             compiler_params=pltpu.CompilerParams(vmem_limit_bytes=32 * 1024 * 1024),
             name=name,
         )(*operands)
 
-    def exchange(xa, xb, sources):
-        planes = xa.shape[0]
-        ra = lax.ppermute(xa, ("gx", "gy"), up)
-        rb = lax.ppermute(xb, ("gx", "gy"), down)
-        ye, yo = call(
-            lambda *refs: turn_kernel(planes, *refs), (message(planes), message(planes)), [], "turn", ra, rb, *sources
-        )
-        return ra, rb, lax.ppermute(ye, "gy", far), lax.ppermute(yo, "gy", near)
+    def along_x(xa, xb):
+        return lax.ppermute(xa, ("gx", "gy"), up), lax.ppermute(xb, ("gx", "gy"), down)
+
+    def along_y(ra, rb, sources):
+        like = arr(ra.shape, f32)
+        ye, yo = call(turn_kernel, (like, like), [], "turn", ra, rb, *sources)
+        return lax.ppermute(ye, "gy", far), lax.ppermute(yo, "gy", near)
 
     sources = (body_a, body_b, active, impulse0, jac_a, jac_b, start, minv, precond, bias, friction, sticking)
     like = lambda a: arr(a.shape, a.dtype)
@@ -385,7 +474,7 @@
     sources = [pltpu.with_memory_space_constraint(a, pltpu.HBM) for a in sources]
     made = call(
         first_kernel,
-        (*map(like, kept), ids_t, ids_t, hot_t, hot_t, own_t, halo_t, own_t, own_t, message(4), message(4)),
+        (*map(like, kept), ids_t, ids_t, hot_t, hot_t, own_t, halo_t, own_t, own_t, message(2 * GROUP), message(2 * GROUP)),
         [pltpu.VMEM(a.shape, a.dtype) for a in (body_a, body_b, start, minv)]
         + work
         + [pltpu.SemaphoreType.DMA((len(sources),))],
@@ -395,23 +484,28 @@
     )
     fixed, lam = made[:7], made[7]
     id_a, id_b, hot_a, hot_b, own, halo, v_own, m_own, xa, xb = made[8:]
+    part_t = arr((2 * DOF, rows, lanes), f32)
+    halo_tables = ()
     for step in range(ITERS):
-        first = step == 0
-        sources = (own, halo, v_own, m_own) if first else (own, halo)
-        received = exchange(xa, xb, sources)
-        ins = (*fixed, lam, id_a, id_b, hot_a, hot_b, own, halo, v_own, m_own)
-        outs = (lam_t, own_t, halo_t, message(2), message(2))
-        kernel = lambda *refs, first=first: middle_kernel(first, *refs)
-        if first:
-            lam, own, halo, xa, xb, v_halo, m_halo = call(
-                kernel, outs + (halo_t, halo_t), table + work, "middle0", *ins, *received
-            )
-        else:
-            lam, own, halo, xa, xb = call(
-                kernel, outs, table + work, "middle", *ins, v_halo, m_halo, *received
-            )
-    received = exchange(xa, xb, (own, halo))
-    out = call(last_kernel, arr(start.shape, f32), [], "last", own, v_own, m_own, *received)
+        first, last = step == 0, step == ITERS - 1
+        came_x = along_x(xa, xb)
+        part = call(inner_kernel, part_t, table, "inner", own, v_own, m_own, id_a, id_b)
+        came_y = along_y(*came_x, (own, halo, v_own, m_own) if first else (own, halo))
+        part = call(
+            lambda *refs, first=first: side_kernel(first, *refs), part_t, table, "side",
+            own, halo, v_own, m_own, id_a, id_b, part, *came_x, *halo_tables,
+        )
+        sent = message(LAST_GROUP if last else GROUP)
+        outs = (lam_t, own_t, halo_t, sent, sent) + ((halo_t, halo_t) if first else ())
+        lam, own, halo, xa, xb, *made = call(
+            lambda *refs, first=first, last=last: middle_kernel(first, last, *refs), outs, table + work, "middle",
+            *fixed, lam, id_a, id_b, hot_a, hot_b, own, halo, v_own, m_own, part, *came_x, *came_y, *halo_tables,
+        )
+        halo_tables = tuple(made) or halo_tables
+    came_x = along_x(xa, xb)
+    lam = call(keep_kernel, lam_t, [pltpu.SemaphoreType.DMA], "keep", lam, out_space=pltpu.HBM)
+    came_y = along_y(*came_x, (halo,))
+    out = call(last_kernel, arr(start.shape, f32), [], "last", own, v_own, m_own, *came_x, *came_y)
     return lam.reshape(ROWS, 1, 1, rows, lanes), out.reshape(velocity0.shape)
 
 

time: 43.3 us -> 40.7 us (0.940)
  waiting for transfers between devices: 18.2 us -> 14.4 us
  Pallas kernels: 10.6 us -> 12.6 us
  starting transfers between devices: 13.5 us -> 12.7 us
    ppermute x16, waiting for transfers between devices: 18.2 us -> 14.4 us  [the longest x4 7.08 us: along_x(): lax.ppermute(xb, ('gx', 'gy'), down)]
    pallas_call x9 -> x16, Pallas kernels: 10.6 us -> 12.6 us  [call(): pl.pallas_call(kernel, out_shape=outs, in_specs=[pl.BlockSpec(memory_spac...]
    ppermute x16, starting transfers between devices: 13.5 us -> 12.7 us  [the longest x4 6.79 us: along_x(): lax.ppermute(xa, ('gx', 'gy'), up)]
  transfers between devices with their start and end apart: 16 -> 16, of which waited for: 12 -> 12; matrix products, arithmetic and copies ran while one was open for 0% -> 0% of each run, Pallas kernels for 0% -> 8%
where the time goes in v4:
time: 40.7 us; the launch traced here: 40.4 us
  waiting for transfers between devices  14.4 us (35%)
  starting transfers between devices  12.7 us (31%)
  Pallas kernels  12.6 us (31%)
  between operations  0.71 us (2%)
    pallas_call x16, Pallas kernels, call(): pl.pallas_call(kernel, out_shape=outs, in_specs=[pl.BlockSpec(memory_spac...  12.6 us
    ppermute x4, waiting for transfers between devices, along_x(): lax.ppermute(xb, ('gx', 'gy'), down)  7.08 us
    ppermute x4, starting transfers between devices, along_x(): lax.ppermute(xa, ('gx', 'gy'), up)  6.79 us
    ppermute x8, starting transfers between devices, along_y(): return (lax.ppermute(ye, 'gy', far), lax.ppermute(yo, 'gy', near))  5.88 us
    ppermute x8, waiting for transfers between devices, along_y(): return (lax.ppermute(ye, 'gy', far), lax.ppermute(yo, 'gy', near))  3.76 us
    ppermute x4, waiting for transfers between devices, along_x(): lax.ppermute(xa, ('gx', 'gy'), up)  3.58 us
  transfers between devices with their start and end apart: 16, of which 12 were waited for; matrix products, arithmetic and copies ran while one was open for 0% of the time, Pallas kernels for 8%

profile of v4, /device:TPU:1, one launch (start us, length us, event | category | flops | bytes accessed | tf_op | source)
XLA Modules:
  0.0 40.4 jit_solution(15122059621540070102)
XLA Ops:
  0.6 3.2 %first.1 = (f32[18,32,128]{2,1,0:T(8,128)S(1)}, f32[18,32,128]{2,1,0:T(8,128)S(1)}, f32[9,32,128]{2,1,0:T(8,128)S(1)}, f32[3,32,128]{2,1,0:T(8,128)S(1)}, f32[32...) custom-call(s32[32,128]{1,0:T(8,128)} %bitcast.25, ...), custom_call_target="tpu_custom_call" | custom-call | tf_op jit(solution)/shard_map/first/pallas_call | solution.py:453
  3.9 2.1 %collective-permute-start = (f32[64,128]{1,0:T(8,128)S(1)}, f32[64,128]{1,0:T(8,128)S(1)}, u32[]{:S(2)}, u32[]{:S(2)}) collective-permute-start(f32[64,128]{1,0:T(8,128)S(1)} %get-tuple-element.61), channel_id=1, source_target_pairs={{0,1},{1,5},{2,3},{3,7},{4,0},{5,9},{6,2},{7,11},{8,4},{9,13},{10,... | collective-permute-start | bytes 98312 | tf_op jit(solution)/shard_map/ppermute | solution.py:464
  6.0 0.0 collective-permute-start.1
  6.0 1.0 %collective-permute-done.refs_7_.ra.refs_17_ = f32[64,128]{1,0:T(8,128)S(1)} collective-permute-done((f32[64,128]{1,0:T(8,128)S(1)}, f32[64,128]{1,0:T(8,128)S(1)}, u32[]{:S(2)}, u32[]{:S(2)}) %collective-permute-start) | collective-permute-done | bytes 32800 | tf_op jit(solution)/shard_map/ppermute | solution.py:464
  7.0 1.7 %collective-permute-done.1.refs_8_.rb.refs_18_ = f32[64,128]{1,0:T(8,128)S(1)} collective-permute-done((f32[64,128]{1,0:T(8,128)S(1)}, f32[64,128]{1,0:T(8,128)S(1)}, u32[]{:S(2)}, u32[]{:S(2)}) %collective-permute-start.1) | collective-permute-done | bytes 32800 | tf_op jit(solution)/shard_map/ppermute | solution.py:464
  8.8 0.1 turn.4
  8.9 1.8 %collective-permute-start.2 = (f32[64,128]{1,0:T(8,128)S(1)}, f32[64,128]{1,0:T(8,128)S(1)}, u32[]{:S(2)}, u32[]{:S(2)}) collective-permute-start(f32[64,128]{1,0:T(8,128)S(1)} %get-tuple-element.63), channel_id=1, source_target_pairs={{0,3},{1,2},{2,1},{3,0},{4,7},{5,6},{6,5},{7,4},{8,11},{9,10},{10,... | collective-permute-start | bytes 98312 | tf_op jit(solution)/shard_map/ppermute | solution.py:469
  10.7 0.1 collective-permute-start.3
  10.8 0.4 %inner.3.refs_6_ = f32[12,32,128]{2,1,0:T(8,128)S(1)} custom-call(f32[16,8,128]{2,1,0:T(8,128)S(1)} %get-tuple-element.57.own.refs_0_.refs_12_, f32[16,8,128]{2,1,0:T(8,128)S(1)} %get-tuple-element.59.v_own.refs_2_.refs_14_, f32[16,8,128]{2,1,0:T(8,128)S(1)} %get-tuple-element.60.m_own.refs_3_.refs_15_, ...), custom_call_target="tpu_custom_call" | custom-call | tf_op jit(solution)/shard_map/inner/pallas_call | solution.py:453
  11.3 0.4 %side.3.refs_16_ = f32[12,32,128]{2,1,0:T(8,128)S(1)} custom-call(f32[16,8,128]{2,1,0:T(8,128)S(1)} %get-tuple-element.57.own.refs_0_.refs_12_, f32[9,8,128]{2,1,0:T(8,128)S(1)} %get-tuple-element.58.refs_1_.refs_13_, f32[16,8,128]{2,1,0:T(8,128)S(1)} %get-tuple-element.59.v_own.refs_2_.refs_14_, f32[16,8,128]{2,1,0:T(8,128)S(1)} %get-tuple-element.60.m_own.refs_3_.refs_15_, ...), custom_call_target="tpu_custom_call" | custom-call | tf_op jit(solution)/shard_map/side/pallas_call | solution.py:453
  11.7 0.6 %collective-permute-done.2.refs_19_ = f32[64,128]{1,0:T(8,128)S(1)} collective-permute-done((f32[64,128]{1,0:T(8,128)S(1)}, f32[64,128]{1,0:T(8,128)S(1)}, u32[]{:S(2)}, u32[]{:S(2)}) %collective-permute-start.2) | collective-permute-done | bytes 32800 | tf_op jit(solution)/shard_map/ppermute | solution.py:469
  12.3 0.0 collective-permute-done.3.refs_20_
  12.3 1.6 %middle.3 = (f32[3,32,128]{2,1,0:T(8,128)S(1)}, f32[16,8,128]{2,1,0:T(8,128)S(1)}, f32[9,8,128]{2,1,0:T(8,128)S(1)}, f32[32,128]{1,0:T(8,128)S(1)}, f32[32,128]{...) custom-call(f32[18,32,128]{2,1,0:T(8,128)S(1)} %get-tuple-element.45.refs_0_, ...), custom_call_target="tpu_custom_call" | custom-call | tf_op jit(solution)/shard_map/middle/pallas_call | solution.py:453
  14.0 1.6 %collective-permute-start.4 = (f32[32,128]{1,0:T(8,128)S(1)}, f32[32,128]{1,0:T(8,128)S(1)}, u32[]{:S(2)}, u32[]{:S(2)}) collective-permute-start(f32[32,128]{1,0:T(8,128)S(1)} %get-tuple-element.68), channel_id=1, source_target_pairs={{0,1},{1,5},{2,3},{3,7},{4,0},{5,9},{6,2},{7,11},{8,4},{9,13},{10,... | collective-permute-start | bytes 49160 | tf_op jit(solution)/shard_map/ppermute | solution.py:464
  15.6 0.0 collective-permute-start.5
  15.6 0.9 %collective-permute-done.4.refs_7_.ra.refs_17_ = f32[32,128]{1,0:T(8,128)S(1)} collective-permute-done((f32[32,128]{1,0:T(8,128)S(1)}, f32[32,128]{1,0:T(8,128)S(1)}, u32[]{:S(2)}, u32[]{:S(2)}) %collective-permute-start.4) | collective-permute-done | bytes 16416 | tf_op jit(solution)/shard_map/ppermute | solution.py:464
  16.5 1.9 %collective-permute-done.5.refs_8_.rb.refs_18_ = f32[32,128]{1,0:T(8,128)S(1)} collective-permute-done((f32[32,128]{1,0:T(8,128)S(1)}, f32[32,128]{1,0:T(8,128)S(1)}, u32[]{:S(2)}, u32[]{:S(2)}) %collective-permute-start.5) | collective-permute-done | bytes 16416 | tf_op jit(solution)/shard_map/ppermute | solution.py:464
  18.4 0.1 turn.5
  18.5 1.2 %collective-permute-start.6 = (f32[32,128]{1,0:T(8,128)S(1)}, f32[32,128]{1,0:T(8,128)S(1)}, u32[]{:S(2)}, u32[]{:S(2)}) collective-permute-start(f32[32,128]{1,0:T(8,128)S(1)} %get-tuple-element.72), channel_id=1, source_target_pairs={{0,3},{1,2},{2,1},{3,0},{4,7},{5,6},{6,5},{7,4},{8,11},{9,10},{10,... | collective-permute-start | bytes 49160 | tf_op jit(solution)/shard_map/ppermute | solution.py:469
  19.7 0.6 %collective-permute-start.7 = (f32[32,128]{1,0:T(8,128)S(1)}, f32[32,128]{1,0:T(8,128)S(1)}, u32[]{:S(2)}, u32[]{:S(2)}) collective-permute-start(f32[32,128]{1,0:T(8,128)S(1)} %get-tuple-element.73), channel_id=1, source_target_pairs={{0,1},{1,0},{2,3},{3,2},{4,5},{5,4},{6,7},{7,6},{8,9},{9,8},{10,11... | collective-permute-start | bytes 49160 | tf_op jit(solution)/shard_map/ppermute | solution.py:469
  20.3 0.4 %inner.4.refs_6_ = f32[12,32,128]{2,1,0:T(8,128)S(1)} custom-call(f32[16,8,128]{2,1,0:T(8,128)S(1)} %get-tuple-element.66.own.refs_0_.refs_12_, f32[16,8,128]{2,1,0:T(8,128)S(1)} %get-tuple-element.59.v_own.refs_2_.refs_14_, f32[16,8,128]{2,1,0:T(8,128)S(1)} %get-tuple-element.60.m_own.refs_3_.refs_15_, ...), custom_call_target="tpu_custom_call" | custom-call | tf_op jit(solution)/shard_map/inner/pallas_call | solution.py:453
  20.7 0.4 %side.4.refs_16_ = f32[12,32,128]{2,1,0:T(8,128)S(1)} custom-call(f32[16,8,128]{2,1,0:T(8,128)S(1)} %get-tuple-element.66.own.refs_0_.refs_12_, f32[9,8,128]{2,1,0:T(8,128)S(1)} %get-tuple-element.67.refs_1_.refs_13_, f32[16,8,128]{2,1,0:T(8,128)S(1)} %get-tuple-element.59.v_own.refs_2_.refs_14_, f32[16,8,128]{2,1,0:T(8,128)S(1)} %get-tuple-element.60.m_own.refs_3_.refs_15_, ...), custom_call_target="tpu_custom_call" | custom-call | tf_op jit(solution)/shard_map/side/pallas_call | solution.py:453
  21.1 0.5 %collective-permute-done.6.refs_19_ = f32[32,128]{1,0:T(8,128)S(1)} collective-permute-done((f32[32,128]{1,0:T(8,128)S(1)}, f32[32,128]{1,0:T(8,128)S(1)}, u32[]{:S(2)}, u32[]{:S(2)}) %collective-permute-start.6) | collective-permute-done | bytes 16416 | tf_op jit(solution)/shard_map/ppermute | solution.py:469
  21.7 0.0 collective-permute-done.7.refs_20_
  21.7 1.6 %middle.4 = (f32[3,32,128]{2,1,0:T(8,128)S(1)}, f32[16,8,128]{2,1,0:T(8,128)S(1)}, f32[9,8,128]{2,1,0:T(8,128)S(1)}, f32[32,128]{1,0:T(8,128)S(1)}, f32[32,128]{1,0:T(8,128)S(1)}) custom-call(f32[18,32,128]{2,1,0:T(8,128)S(1)} %get-tuple-element.45.refs_0_, f32[18,32,128]{2,1,0:T(8,128)S(1)} %get-tuple-element.46.refs_1_, ...), custom_call_target="tpu_custom_call" | custom-call | tf_op jit(solution)/shard_map/middle/pallas_call | solution.py:453
  23.3 1.5 %collective-permute-start.8 = (f32[32,128]{1,0:T(8,128)S(1)}, f32[32,128]{1,0:T(8,128)S(1)}, u32[]{:S(2)}, u32[]{:S(2)}) collective-permute-start(f32[32,128]{1,0:T(8,128)S(1)} %get-tuple-element.77), channel_id=1, source_target_pairs={{0,1},{1,5},{2,3},{3,7},{4,0},{5,9},{6,2},{7,11},{8,4},{9,13},{10,... | collective-permute-start | bytes 49160 | tf_op jit(solution)/shard_map/ppermute | solution.py:464
  24.8 0.0 collective-permute-start.9
  24.8 0.9 %collective-permute-done.8.refs_7_.ra.refs_17_ = f32[32,128]{1,0:T(8,128)S(1)} collective-permute-done((f32[32,128]{1,0:T(8,128)S(1)}, f32[32,128]{1,0:T(8,128)S(1)}, u32[]{:S(2)}, u32[]{:S(2)}) %collective-permute-start.8) | collective-permute-done | bytes 16416 | tf_op jit(solution)/shard_map/ppermute | solution.py:464
  25.7 1.7 %collective-permute-done.9.refs_8_.rb.refs_18_ = f32[32,128]{1,0:T(8,128)S(1)} collective-permute-done((f32[32,128]{1,0:T(8,128)S(1)}, f32[32,128]{1,0:T(8,128)S(1)}, u32[]{:S(2)}, u32[]{:S(2)}) %collective-permute-start.9) | collective-permute-done | bytes 16416 | tf_op jit(solution)/shard_map/ppermute | solution.py:464
  27.4 0.1 turn.6
  27.5 0.9 %collective-permute-start.10 = (f32[32,128]{1,0:T(8,128)S(1)}, f32[32,128]{1,0:T(8,128)S(1)}, u32[]{:S(2)}, u32[]{:S(2)}) collective-permute-start(f32[32,128]{1,0:T(8,128)S(1)} %get-tuple-element.79), channel_id=1, source_target_pairs={{0,3},{1,2},{2,1},{3,0},{4,7},{5,6},{6,5},{7,4},{8,11},{9,10},{10,... | collective-permute-start | bytes 49160 | tf_op jit(solution)/shard_map/ppermute | solution.py:469
  28.4 0.8 %collective-permute-start.11 = (f32[32,128]{1,0:T(8,128)S(1)}, f32[32,128]{1,0:T(8,128)S(1)}, u32[]{:S(2)}, u32[]{:S(2)}) collective-permute-start(f32[32,128]{1,0:T(8,128)S(1)} %get-tuple-element.80), channel_id=1, source_target_pairs={{0,1},{1,0},{2,3},{3,2},{4,5},{5,4},{6,7},{7,6},{8,9},{9,8},{10,11... | collective-permute-start | bytes 49160 | tf_op jit(solution)/shard_map/ppermute | solution.py:469
  29.1 0.4 %inner.5.refs_6_ = f32[12,32,128]{2,1,0:T(8,128)S(1)} custom-call(f32[16,8,128]{2,1,0:T(8,128)S(1)} %get-tuple-element.75.own.refs_0_.refs_12_, f32[16,8,128]{2,1,0:T(8,128)S(1)} %get-tuple-element.59.v_own.refs_2_.refs_14_, f32[16,8,128]{2,1,0:T(8,128)S(1)} %get-tuple-element.60.m_own.refs_3_.refs_15_, ...), custom_call_target="tpu_custom_call" | custom-call | tf_op jit(solution)/shard_map/inner/pallas_call | solution.py:453
  29.6 0.4 %side.5.refs_16_ = f32[12,32,128]{2,1,0:T(8,128)S(1)} custom-call(f32[16,8,128]{2,1,0:T(8,128)S(1)} %get-tuple-element.75.own.refs_0_.refs_12_, f32[9,8,128]{2,1,0:T(8,128)S(1)} %get-tuple-element.76.refs_1_.refs_13_, f32[16,8,128]{2,1,0:T(8,128)S(1)} %get-tuple-element.59.v_own.refs_2_.refs_14_, f32[16,8,128]{2,1,0:T(8,128)S(1)} %get-tuple-element.60.m_own.refs_3_.refs_15_, ...), custom_call_target="tpu_custom_call" | custom-call | tf_op jit(solution)/shard_map/side/pallas_call | solution.py:453
  30.0 0.7 %collective-permute-done.10.refs_19_ = f32[32,128]{1,0:T(8,128)S(1)} collective-permute-done((f32[32,128]{1,0:T(8,128)S(1)}, f32[32,128]{1,0:T(8,128)S(1)}, u32[]{:S(2)}, u32[]{:S(2)}) %collective-permute-start.10) | collective-permute-done | bytes 16416 | tf_op jit(solution)/shard_map/ppermute | solution.py:469
  30.7 0.0 collective-permute-done.11.refs_20_
  30.7 1.6 %middle.5 = (f32[3,32,128]{2,1,0:T(8,128)S(1)}, f32[16,8,128]{2,1,0:T(8,128)S(1)}, f32[9,8,128]{2,1,0:T(8,128)S(1)}, f32[24,128]{1,0:T(8,128)S(1)}, f32[24,128]{1,0:T(8,128)S(1)}) custom-call(f32[18,32,128]{2,1,0:T(8,128)S(1)} %get-tuple-element.45.refs_0_, f32[18,32,128]{2,1,0:T(8,128)S(1)} %get-tuple-element.46.refs_1_, ...), custom_call_target="tpu_custom_call" | custom-call | tf_op jit(solution)/shard_map/middle/pallas_call | solution.py:453
  32.3 1.6 %collective-permute-start.12 = (f32[24,128]{1,0:T(8,128)S(1)}, f32[24,128]{1,0:T(8,128)S(1)}, u32[]{:S(2)}, u32[]{:S(2)}) collective-permute-start(f32[24,128]{1,0:T(8,128)S(1)} %get-tuple-element.83), channel_id=1, source_target_pairs={{0,1},{1,5},{2,3},{3,7},{4,0},{5,9},{6,2},{7,11},{8,4},{9,13},{10,... | collective-permute-start | bytes 36872 | tf_op jit(solution)/shard_map/ppermute | solution.py:464
  33.9 0.0 collective-permute-start.13
  33.9 0.8 %collective-permute-done.12.ra = f32[24,128]{1,0:T(8,128)S(1)} collective-permute-done((f32[24,128]{1,0:T(8,128)S(1)}, f32[24,128]{1,0:T(8,128)S(1)}, u32[]{:S(2)}, u32[]{:S(2)}) %collective-permute-start.12) | collective-permute-done | bytes 12320 | tf_op jit(solution)/shard_map/ppermute | solution.py:464
  34.7 1.7 %collective-permute-done.13.rb = f32[24,128]{1,0:T(8,128)S(1)} collective-permute-done((f32[24,128]{1,0:T(8,128)S(1)}, f32[24,128]{1,0:T(8,128)S(1)}, u32[]{:S(2)}, u32[]{:S(2)}) %collective-permute-start.13) | collective-permute-done | bytes 12320 | tf_op jit(solution)/shard_map/ppermute | solution.py:464
  36.5 0.1 turn.7
  36.6 0.4 %collective-permute-start.14 = (f32[24,128]{1,0:T(8,128)S(1)}, f32[24,128]{1,0:T(8,128)S(1)}, u32[]{:S(2)}, u32[]{:S(2)}) collective-permute-start(f32[24,128]{1,0:T(8,128)S(1)} %get-tuple-element.86), channel_id=1, source_target_pairs={{0,3},{1,2},{2,1},{3,0},{4,7},{5,6},{6,5},{7,4},{8,11},{9,10},{10,... | collective-permute-start | bytes 36872 | tf_op jit(solution)/shard_map/ppermute | solution.py:469
  37.0 0.1 collective-permute-start.15
  37.2 0.6 %keep.1 = f32[3,32,128]{2,1,0:T(8,128)} custom-call(f32[3,32,128]{2,1,0:T(8,128)S(1)} %get-tuple-element.81.lam), custom_call_target="tpu_custom_call" | custom-call | tf_op jit(solution)/shard_map/keep/pallas_call | solution.py:453
  37.8 1.9 %collective-permute-done.14.qe = f32[24,128]{1,0:T(8,128)S(1)} collective-permute-done((f32[24,128]{1,0:T(8,128)S(1)}, f32[24,128]{1,0:T(8,128)S(1)}, u32[]{:S(2)}, u32[]{:S(2)}) %collective-permute-start.14) | collective-permute-done | bytes 12320 | tf_op jit(solution)/shard_map/ppermute | solution.py:469
  39.7 0.0 collective-permute-done.15.qo
  39.7 0.7 %last.1 = f32[96,128]{1,0:T(8,128)} custom-call(f32[16,8,128]{2,1,0:T(8,128)S(1)} %get-tuple-element.82.own, f32[16,8,128]{2,1,0:T(8,128)S(1)} %get-tuple-element.59.v_own.refs_2_.refs_14_, f32[16,8,128]{2,1,0:T(8,128)S(1)} %get-tuple-element.60.m_own.refs_3_.refs_15_, f32[24,128]{1,0:T(8,128)S(1)} %collective-permute-done.12.ra, ...), custom_call_target="tpu_custom_call" | custom-call | tf_op jit(solution)/shard_map/last/pallas_call | solution.py:453
Async XLA Ops:
  3.9 3.2 %collective-permute-start = (f32[64,128]{1,0:T(8,128)S(1)}, f32[64,128]{1,0:T(8,128)S(1)}, u32[]{:S(2)}, u32[]{:S(2)}) collective-permute-start(f32[64,128]{1,0:T(8,128)S(1)} %get-tuple-element.61), channel_id=1, source_target_pairs={{0,1},{1,5},{2,3},{3,7},{4,0},{5,9},{6,2},{7,11},{8,4},{9,13},{10,... | collective-permute-start | bytes 98312 | tf_op jit(solution)/shard_map/ppermute | solution.py:464
  6.0 2.8 %collective-permute-start.1 = (f32[64,128]{1,0:T(8,128)S(1)}, f32[64,128]{1,0:T(8,128)S(1)}, u32[]{:S(2)}, u32[]{:S(2)}) collective-permute-start(f32[64,128]{1,0:T(8,128)S(1)} %get-tuple-element.62), channel_id=1, source_target_pairs={{1,0},{5,1},{3,2},{7,3},{0,4},{9,5},{2,6},{11,7},{4,8},{13,9},{6,1... | collective-permute-start | bytes 98312 | tf_op jit(solution)/shard_map/ppermute | solution.py:464
  8.9 3.4 %collective-permute-start.2 = (f32[64,128]{1,0:T(8,128)S(1)}, f32[64,128]{1,0:T(8,128)S(1)}, u32[]{:S(2)}, u32[]{:S(2)}) collective-permute-start(f32[64,128]{1,0:T(8,128)S(1)} %get-tuple-element.63), channel_id=1, source_target_pairs={{0,3},{1,2},{2,1},{3,0},{4,7},{5,6},{6,5},{7,4},{8,11},{9,10},{10,... | collective-permute-start | bytes 98312 | tf_op jit(solution)/shard_map/ppermute | solution.py:469
  10.7 1.6 %collective-permute-start.3 = (f32[64,128]{1,0:T(8,128)S(1)}, f32[64,128]{1,0:T(8,128)S(1)}, u32[]{:S(2)}, u32[]{:S(2)}) collective-permute-start(f32[64,128]{1,0:T(8,128)S(1)} %get-tuple-element.64), channel_id=1, source_target_pairs={{0,1},{1,0},{2,3},{3,2},{4,5},{5,4},{6,7},{7,6},{8,9},{9,8},{10,11... | collective-permute-start | bytes 98312 | tf_op jit(solution)/shard_map/ppermute | solution.py:469
  14.0 2.5 %collective-permute-start.4 = (f32[32,128]{1,0:T(8,128)S(1)}, f32[32,128]{1,0:T(8,128)S(1)}, u32[]{:S(2)}, u32[]{:S(2)}) collective-permute-start(f32[32,128]{1,0:T(8,128)S(1)} %get-tuple-element.68), channel_id=1, source_target_pairs={{0,1},{1,5},{2,3},{3,7},{4,0},{5,9},{6,2},{7,11},{8,4},{9,13},{10,... | collective-permute-start | bytes 49160 | tf_op jit(solution)/shard_map/ppermute | solution.py:464
  15.6 2.8 %collective-permute-start.5 = (f32[32,128]{1,0:T(8,128)S(1)}, f32[32,128]{1,0:T(8,128)S(1)}, u32[]{:S(2)}, u32[]{:S(2)}) collective-permute-start(f32[32,128]{1,0:T(8,128)S(1)} %get-tuple-element.69), channel_id=1, source_target_pairs={{1,0},{5,1},{3,2},{7,3},{0,4},{9,5},{2,6},{11,7},{4,8},{13,9},{6,1... | collective-permute-start | bytes 49160 | tf_op jit(solution)/shard_map/ppermute | solution.py:464
  18.5 3.2 %collective-permute-start.6 = (f32[32,128]{1,0:T(8,128)S(1)}, f32[32,128]{1,0:T(8,128)S(1)}, u32[]{:S(2)}, u32[]{:S(2)}) collective-permute-start(f32[32,128]{1,0:T(8,128)S(1)} %get-tuple-element.72), channel_id=1, source_target_pairs={{0,3},{1,2},{2,1},{3,0},{4,7},{5,6},{6,5},{7,4},{8,11},{9,10},{10,... | collective-permute-start | bytes 49160 | tf_op jit(solution)/shard_map/ppermute | solution.py:469
  19.7 2.0 %collective-permute-start.7 = (f32[32,128]{1,0:T(8,128)S(1)}, f32[32,128]{1,0:T(8,128)S(1)}, u32[]{:S(2)}, u32[]{:S(2)}) collective-permute-start(f32[32,128]{1,0:T(8,128)S(1)} %get-tuple-element.73), channel_id=1, source_target_pairs={{0,1},{1,0},{2,3},{3,2},{4,5},{5,4},{6,7},{7,6},{8,9},{9,8},{10,11... | collective-permute-start | bytes 49160 | tf_op jit(solution)/shard_map/ppermute | solution.py:469
  23.3 2.3 %collective-permute-start.8 = (f32[32,128]{1,0:T(8,128)S(1)}, f32[32,128]{1,0:T(8,128)S(1)}, u32[]{:S(2)}, u32[]{:S(2)}) collective-permute-start(f32[32,128]{1,0:T(8,128)S(1)} %get-tuple-element.77), channel_id=1, source_target_pairs={{0,1},{1,5},{2,3},{3,7},{4,0},{5,9},{6,2},{7,11},{8,4},{9,13},{10,... | collective-permute-start | bytes 49160 | tf_op jit(solution)/shard_map/ppermute | solution.py:464
  24.8 2.6 %collective-permute-start.9 = (f32[32,128]{1,0:T(8,128)S(1)}, f32[32,128]{1,0:T(8,128)S(1)}, u32[]{:S(2)}, u32[]{:S(2)}) collective-permute-start(f32[32,128]{1,0:T(8,128)S(1)} %get-tuple-element.78), channel_id=1, source_target_pairs={{1,0},{5,1},{3,2},{7,3},{0,4},{9,5},{2,6},{11,7},{4,8},{13,9},{6,1... | collective-permute-start | bytes 49160 | tf_op jit(solution)/shard_map/ppermute | solution.py:464
  27.5 3.2 %collective-permute-start.10 = (f32[32,128]{1,0:T(8,128)S(1)}, f32[32,128]{1,0:T(8,128)S(1)}, u32[]{:S(2)}, u32[]{:S(2)}) collective-permute-start(f32[32,128]{1,0:T(8,128)S(1)} %get-tuple-element.79), channel_id=1, source_target_pairs={{0,3},{1,2},{2,1},{3,0},{4,7},{5,6},{6,5},{7,4},{8,11},{9,10},{10,... | collective-permute-start | bytes 49160 | tf_op jit(solution)/shard_map/ppermute | solution.py:469
  28.4 2.3 %collective-permute-start.11 = (f32[32,128]{1,0:T(8,128)S(1)}, f32[32,128]{1,0:T(8,128)S(1)}, u32[]{:S(2)}, u32[]{:S(2)}) collective-permute-start(f32[32,128]{1,0:T(8,128)S(1)} %get-tuple-element.80), channel_id=1, source_target_pairs={{0,1},{1,0},{2,3},{3,2},{4,5},{5,4},{6,7},{7,6},{8,9},{9,8},{10,11... | collective-permute-start | bytes 49160 | tf_op jit(solution)/shard_map/ppermute | solution.py:469
  32.3 2.4 %collective-permute-start.12 = (f32[24,128]{1,0:T(8,128)S(1)}, f32[24,128]{1,0:T(8,128)S(1)}, u32[]{:S(2)}, u32[]{:S(2)}) collective-permute-start(f32[24,128]{1,0:T(8,128)S(1)} %get-tuple-element.83), channel_id=1, source_target_pairs={{0,1},{1,5},{2,3},{3,7},{4,0},{5,9},{6,2},{7,11},{8,4},{9,13},{10,... | collective-permute-start | bytes 36872 | tf_op jit(solution)/shard_map/ppermute | solution.py:464
  33.9 2.5 %collective-permute-start.13 = (f32[24,128]{1,0:T(8,128)S(1)}, f32[24,128]{1,0:T(8,128)S(1)}, u32[]{:S(2)}, u32[]{:S(2)}) collective-permute-start(f32[24,128]{1,0:T(8,128)S(1)} %get-tuple-element.84), channel_id=1, source_target_pairs={{1,0},{5,1},{3,2},{7,3},{0,4},{9,5},{2,6},{11,7},{4,8},{13,9},{6,1... | collective-permute-start | bytes 36872 | tf_op jit(solution)/shard_map/ppermute | solution.py:464
  36.6 3.1 %collective-permute-start.14 = (f32[24,128]{1,0:T(8,128)S(1)}, f32[24,128]{1,0:T(8,128)S(1)}, u32[]{:S(2)}, u32[]{:S(2)}) collective-permute-start(f32[24,128]{1,0:T(8,128)S(1)} %get-tuple-element.86), channel_id=1, source_target_pairs={{0,3},{1,2},{2,1},{3,0},{4,7},{5,6},{6,5},{7,4},{8,11},{9,10},{10,... | collective-permute-start | bytes 36872 | tf_op jit(solution)/shard_map/ppermute | solution.py:469
  37.0 2.7 %collective-permute-start.15 = (f32[24,128]{1,0:T(8,128)S(1)}, f32[24,128]{1,0:T(8,128)S(1)}, u32[]{:S(2)}, u32[]{:S(2)}) collective-permute-start(f32[24,128]{1,0:T(8,128)S(1)} %get-tuple-element.87), channel_id=1, source_target_pairs={{0,1},{1,0},{2,3},{3,2},{4,5},{5,4},{6,7},{7,6},{8,9},{9,8},{10,11... | collective-permute-start | bytes 36872 | tf_op jit(solution)/shard_map/ppermute | solution.py:469

commit v5 on v4

--- a/solution.py
+++ b/solution.py
@@ -122,25 +122,39 @@
             ).astype(jnp.bfloat16)
 
 
-OWN_HEADS = tuple(range(8))
-ALL_HEADS = OWN_HEADS + (8, 9, 10, 11, 15)
-
-
-def scatter(lam, jac_a, jac_b, id_a, id_b, hot_a, hot_b, force, left_a, left_b):
+X_HEADS = (0, 3, 7)
+REST_HEADS = (1, 2, 4, 5, 6)
+
+
+def with_halo(heads):
+    return heads + tuple(h + 8 for h in heads if h < 4 or h == 7)
+
+
+def scatter(lam, jac_a, jac_b, id_a, id_b, hot_a, hot_b, force, left_a, left_b, heads):
     contract = (((1,), (0,)), ((), ()))
+    both = with_halo(heads)
+    left_a, left_b = left_a.at[: 16 * len(heads)], left_b.at[: 16 * len(both)]
     forces(lam, jac_a, force)
-    spread(force, id_a, left_a, OWN_HEADS)
+    spread(force, id_a, left_a, heads)
     sum_a = lax.dot_general(left_a[...], hot_a[...], contract, preferred_element_type=jnp.float32)
     forces(lam, jac_b, force)
-    spread(force, id_b, left_b, ALL_HEADS)
+    spread(force, id_b, left_b, both)
     sum_b = lax.dot_general(left_b[...], hot_b[...], contract, preferred_element_type=jnp.float32)
 
     def tile(s, k, j):
         lanes = slice(j * LANES, (j + 1) * LANES)
         return s[16 * k : 16 * k + 8, lanes] + s[16 * k + 8 : 16 * k + 16, lanes]
 
-    own = [tile(sum_a, t // 2, t % 2) + tile(sum_b, t // 2, t % 2) for t in range(OWN_TILES)]
-    halo = [tile(sum_b, 8 + t // 2, t % 2) for t in range(8)] + [tile(sum_b, 12, 1)]
+    own, halo = {}, {}
+    for k, h in enumerate(both):
+        for j in range(2):
+            if h < 8:
+                own[2 * h + j] = tile(sum_a, k, j) + tile(sum_b, k, j)
+            elif h < 12:
+                halo[2 * (h - 8) + j] = tile(sum_b, k, j)
+    halo_corner = both.index(15) if 15 in both else None
+    if halo_corner is not None:
+        halo[HALO_CORNER] = tile(sum_b, halo_corner, 1)
     return own, halo
 
 
@@ -152,24 +166,37 @@
 LAST_GROUP = 24
 
 
-def put_tiles(ref, base, tiles, end):
-    for k, tile in enumerate(tiles):
-        ref[base + DOF * k : base + DOF * (k + 1), :] = tile[:DOF]
-    rest = DOF * len(tiles)
-    ref[base + rest : base + end, :] = jnp.zeros((end - rest, LANES), jnp.float32)
+def put_edges(even, group, minus, plus, a_ref, b_ref):
+    for k, (m, p) in enumerate(zip(minus, plus)):
+        rows = slice(group + DOF * k, group + DOF * (k + 1))
+        a_ref[rows, :] = jnp.where(even, m[:DOF], p[:DOF])
+        b_ref[rows, :] = jnp.where(even, p[:DOF], m[:DOF])
+
+
+def blocks(tiles):
+    block = lane_iota() // CORNER
+    out = tiles[3]
+    for k in range(3):
+        out = jnp.where(block == k, tiles[k], out)
+    return out
 
 
 def put_x(even, groups, a_ref, b_ref):
-    high = lane_iota() >= 2 * CORNER
+    size = a_ref.shape[0] // len(groups)
     for g, (first, second) in enumerate(groups):
-        half = jnp.zeros_like(second[-1]) if first is None else first[-1]
-        up = [second[6], second[7], jnp.where(high, second[-1], pltpu.roll(half, 2 * CORNER, 1))]
-        down = [second[0], second[1], jnp.where(high, pltpu.roll(second[-1], 2 * CORNER, 1), half)]
+        up, down = [second[6], second[7]], [second[0], second[1]]
         if first is not None:
             up, down = [first[6], first[7]] + up, [first[0], first[1]] + down
-        rows = a_ref.shape[0] // len(groups)
-        put_tiles(a_ref, g * rows, [jnp.where(even, d, u) for u, d in zip(up, down)], rows)
-        put_tiles(b_ref, g * rows, [jnp.where(even, u, d) for u, d in zip(up, down)], rows)
+        theirs = second[CORNER_TILE] if CORNER_TILE in second else second[HALO_CORNER]
+        ours = jnp.zeros_like(theirs) if first is None else first[CORNER_TILE]
+        ours_on, theirs_on = pltpu.roll(ours, CORNER, 1), pltpu.roll(theirs, CORNER, 1)
+        theirs_half = pltpu.roll(theirs, 2 * CORNER, 1)
+        corner_down = blocks([ours, theirs_on, ours_on, theirs_half])
+        corner_up = blocks([ours_on, theirs_half, ours, theirs_on])
+        put_edges(even, g * size, down, up, a_ref, b_ref)
+        last = slice((g + 1) * size - 8, (g + 1) * size)
+        a_ref[last, :] = jnp.where(even, corner_down, corner_up)
+        b_ref[last, :] = jnp.where(even, corner_up, corner_down)
 
 
 class Received:
@@ -181,36 +208,22 @@
             return tile
 
         self.rows = GROUP if a_ref.shape[0] % GROUP == 0 else LAST_GROUP
-        self.tiles = 5 if self.rows == GROUP else 3
         self.x_low, self.x_high = pick(b_ref, a_ref), pick(a_ref, b_ref)
         if e_ref is not None:
             self.y_low, self.y_high = pick(e_ref, o_ref), pick(o_ref, e_ref)
 
     def edge(self, side, plane):
-        place = 2 * (plane % 2) if self.tiles == 5 else 0
+        place = 2 * (plane % 2) if self.rows == GROUP else 0
         base = self.rows * (plane // 2) + DOF * place
         return [side(base), side(base + DOF)]
 
-    def corner_row(self, plane):
-        return self.rows * (plane // 2) + DOF * (self.tiles - 1)
-
-    def x_corner(self, plane):
-        lane = lane_iota()
-        low, high = self.x_low(self.corner_row(plane)), self.x_high(self.corner_row(plane))
-        left = lane < 2 * CORNER
-        first = jnp.where(left, high, pltpu.roll(low, 2 * CORNER, 1))
-        second = jnp.where(left, pltpu.roll(high, 2 * CORNER, 1), low)
-        odd = (lane & CORNER) != 0
-        minus = jnp.where(odd, pltpu.roll(second, CORNER, 1), first)
-        plus = jnp.where(odd, first, pltpu.roll(second, 3 * CORNER, 1))
-        return minus, plus
-
     def corner(self, plane):
         odd = (lane_iota() & CORNER) != 0
-        low, high = self.y_low(self.corner_row(plane)), self.y_high(self.corner_row(plane))
+        row = self.rows * (plane // 2) + self.rows - 8
+        low, high = self.y_low(row), self.y_high(row)
         if plane % 2:
-            return pltpu.roll(jnp.where(odd, high, low), 2 * CORNER, 1)
-        return jnp.where(odd, pltpu.roll(high, 3 * CORNER, 1), pltpu.roll(low, CORNER, 1))
+            return jnp.where(odd, pltpu.roll(high, 2 * CORNER, 1), pltpu.roll(low, 3 * CORNER, 1))
+        return jnp.where(odd, pltpu.roll(high, 3 * CORNER, 1), low)
 
 
 X_EDGES = (0, 1, 6, 7)
@@ -226,6 +239,11 @@
 def y_plane(came, plane):
     low, high = came.edge(came.y_low, plane), came.edge(came.y_high, plane)
     return dict(zip(Y_EDGES, low + high))
+
+
+def put_dict(ref, tiles):
+    for t, value in tiles.items():
+        ref[t] = value
 
 
 def first_kernel(*refs):
@@ -248,32 +266,31 @@
         copy.wait()
     active = act[...].astype(jnp.float32)
     lam = [active * lam0[k] for k in range(ROWS)]
-    sums, sums_halo = scatter(lam, jac_a, jac_b, id_a, id_b, hot_a, hot_b, force, left_a, left_b)
+    for k in range(ROWS):
+        lam0[k] = lam[k]
+    sums, sums_halo = scatter(lam, jac_a, jac_b, id_a, id_b, hot_a, hot_b, force, left_a, left_b, X_HEADS)
     for copy in copies[6:8]:
         copy.wait()
     v, m = to_tables(start), to_tables(minv)
     for t in range(OWN_TILES):
-        own[t], v_own[t], m_own[t] = sums[t], v[t], m[t]
-    for t in range(HALO_TILES):
-        halo[t] = sums_halo[t]
-    put_x(even, [(sums, sums_halo), (v, m)], xa, xb)
+        v_own[t], m_own[t] = v[t], m[t]
+    put_dict(own, sums)
+    put_dict(halo, sums_halo)
+    put_x(even, [(sums, sums_halo), (dict(enumerate(v)), dict(enumerate(m)))], xa, xb)
     for copy in copies[8:]:
         copy.wait()
 
 
-def turn_kernel(ra, rb, *refs):
-    sources, (e_ref, o_ref) = refs[:-2], refs[-2:]
+def turn_kernel(ra, rb, e_in, o_in, e_ref, o_ref):
     even = is_even()
     came = Received(even, ra, rb)
-    groups = ra.shape[0] // came.rows
-    for g in range(groups):
-        planes = sources[2 * g : 2 * g + 2] if len(sources) > 1 else sources
-        minus = [p[t] for p in planes for t in (2, 3)]
-        plus = [p[t] for p in planes for t in (4, 5)]
-        corner = came.x_corner(2 * g)
-        minus, plus = minus + [corner[0]], plus + [corner[1]]
-        put_tiles(e_ref, g * came.rows, [jnp.where(even, m, p) for m, p in zip(minus, plus)], came.rows)
-        put_tiles(o_ref, g * came.rows, [jnp.where(even, p, m) for m, p in zip(minus, plus)], came.rows)
+    left = lane_iota() < 2 * CORNER
+    for g in range(0, ra.shape[0], came.rows):
+        row = g + came.rows - 8
+        low, high = came.x_low(row), came.x_high(row)
+        minus, plus = jnp.where(left, high, low), jnp.where(left, low, high)
+        e_ref[row : row + 8, :] = jnp.where(even, minus, plus)
+        o_ref[row : row + 8, :] = jnp.where(even, plus, minus)
 
 
 def gather(table, index, codes, start=None):
@@ -314,9 +331,30 @@
             ref[base + d] = value
 
 
-def inner_kernel(own, v_own, m_own, id_a, id_b, out, table):
+def window_kernel(first, last, jac_a, jac_b, lam, id_a, id_b, hot_a, hot_b, v_own, m_own, own_x, *refs):
+    own, e_ref, o_ref, out = refs[:4]
+    halo, work = (None, refs[4:]) if last else (refs[4], refs[5:])
+    force, left_a, left_b, table, *sem = work
+    if last:
+        copy = pltpu.make_async_copy(lam, out, sem[0])
+        copy.start()
+    even = is_even()
+    values = [lam[k] for k in range(ROWS)]
+    sums, sums_halo = scatter(values, jac_a, jac_b, id_a, id_b, hot_a, hot_b, force, left_a, left_b, REST_HEADS)
+    put_dict(own, sums)
+    if not last:
+        put_dict(halo, sums_halo)
+    planes = [(sums_halo,)] if last else [(sums, sums_halo)] + [(v_own, m_own)] * first
+    size = e_ref.shape[0] // len(planes)
+    for g, pair in enumerate(planes):
+        minus = [p[t] for p in pair for t in (2, 3)]
+        plus = [p[t] for p in pair for t in (4, 5)]
+        put_edges(even, g * size, minus, plus, e_ref, o_ref)
+    if last:
+        copy.wait()
+        return
     for t in INTERIOR:
-        table[t] = v_own[t] + m_own[t] * own[t]
+        table[t] = v_own[t] + m_own[t] * (sums[t] if t in sums else own_x[t])
     gather_both(table, id_a, id_b, INTERIOR, (), out, None)
 
 
@@ -344,13 +382,14 @@
 
 def middle_kernel(
     first, last, jac_a, jac_b, precond, bias, mu, stick, act, lam_in,
-    id_a, id_b, hot_a, hot_b, own, halo, v_own, m_own, part, ra, rb, qe, qo, *refs,
+    id_a, id_b, hot_a, hot_b, own_x, halo_x, own, halo, v_own, m_own, part, ra, rb, qe, qo, *refs,
 ):
+    if not first:
+        v_halo, m_halo, *refs = refs
+    lam_out, own_out, xa, xb, *made = refs[:-4]
+    table, force, left_a, left_b = refs[-4:]
     if first:
-        lam_out, own_out, halo_out, xa, xb, v_halo, m_halo = refs[:7]
-    else:
-        v_halo, m_halo, lam_out, own_out, halo_out, xa, xb = refs[:7]
-    table, force, left_a, left_b = refs[7:]
+        v_halo, m_halo = made[1:]
     even = is_even()
     came = Received(even, ra, rb, qe, qo)
     if first:
@@ -361,9 +400,11 @@
     theirs, ours = y_plane(came, 0), y_plane(came, 1)
     theirs[HALO_CORNER], ours[CORNER_TILE] = came.corner(0), came.corner(1)
     for t, value in ours.items():
-        table[t] = v_own[t] + m_own[t] * (own[t] + value)
+        mine = own_x if t == CORNER_TILE else own
+        table[t] = v_own[t] + m_own[t] * (mine[t] + value)
     for t, value in theirs.items():
-        table[OWN_TILES + t] = v_halo[t] + m_halo[t] * (halo[t] + value)
+        mine = halo_x if t == HALO_CORNER else halo
+        table[OWN_TILES + t] = v_halo[t] + m_halo[t] * (mine[t] + value)
     late, late_halo = own_codes(ours), halo_codes(theirs)
     v_a = gather(table, id_a[...], late, part.at[:DOF])
     v_b = gather(table, id_b[...], late + late_halo, part.at[DOF:])
@@ -371,10 +412,7 @@
     u_b = relative(jac_b, v_b)
     target = [u_a[k] + u_b[k] + bias[k] for k in range(ROWS)]
     active = act[...].astype(jnp.float32)
-    if first:
-        lam = [active * lam_in[k] for k in range(ROWS)]
-    else:
-        lam = [lam_in[k] for k in range(ROWS)]
+    lam = [lam_in[k] for k in range(ROWS)]
     raw = []
     for k in range(ROWS):
         w = precond[k * ROWS] * target[0]
@@ -388,25 +426,19 @@
     lam = [active * normal, active * (raw[1] * scale), active * (raw[2] * scale)]
     for k in range(ROWS):
         lam_out[k] = lam[k]
-    sums, sums_halo = scatter(lam, jac_a, jac_b, id_a, id_b, hot_a, hot_b, force, left_a, left_b)
-    for t in range(OWN_TILES):
-        own_out[t] = sums[t]
-    for t in range(HALO_TILES):
-        halo_out[t] = sums_halo[t]
+    sums, sums_halo = scatter(lam, jac_a, jac_b, id_a, id_b, hot_a, hot_b, force, left_a, left_b, X_HEADS)
+    put_dict(own_out, sums)
+    if not last:
+        put_dict(made[0], sums_halo)
     put_x(even, [(None if last else sums, sums_halo)], xa, xb)
 
 
-def keep_kernel(lam, out, sem):
-    copy = pltpu.make_async_copy(lam, out, sem)
-    copy.start()
-    copy.wait()
-
-
-def last_kernel(own, v_own, m_own, ra, rb, qe, qo, out):
+def last_kernel(own_x, own, v_own, m_own, ra, rb, qe, qo, out):
     came = Received(is_even(), ra, rb, qe, qo)
     ours = x_plane(came, 1) | y_plane(came, 1)
     ours[CORNER_TILE] = came.corner(1)
-    total = [own[t] + ours[t] if t in ours else own[t] for t in range(OWN_TILES)]
+    mine = [(own_x if t // 2 in X_HEADS else own)[t] for t in range(OWN_TILES)]
+    total = [mine[t] + ours[t] if t in ours else mine[t] for t in range(OWN_TILES)]
     from_tables([v_own[t] + m_own[t] * total[t] for t in range(OWN_TILES)], out)
 
 
@@ -444,28 +476,31 @@
     message = lambda r: arr((r, lanes), f32)
     work = [
         pltpu.VMEM((8 * rows, lanes), f32),
-        pltpu.VMEM((16 * len(OWN_HEADS), contacts), bf16),
-        pltpu.VMEM((16 * len(ALL_HEADS), contacts), bf16),
+        pltpu.VMEM((16 * len(REST_HEADS), contacts), bf16),
+        pltpu.VMEM((16 * len(with_halo(REST_HEADS)), contacts), bf16),
     ]
     table = [pltpu.VMEM((OWN_TILES + HALO_TILES, 8, lanes), f32)]
 
-    def call(kernel, outs, scratch, name, *operands, space=pltpu.VMEM, out_space=pltpu.VMEM):
+    def call(kernel, outs, scratch, name, *operands, space=pltpu.VMEM, out_spaces=None, aliases={}, flops=0):
+        spaces = out_spaces or jax.tree.map(lambda _: pltpu.VMEM, outs)
         return pl.pallas_call(
             kernel,
             out_shape=outs,
             in_specs=[pl.BlockSpec(memory_space=space)] * len(operands),
-            out_specs=jax.tree.map(lambda _: pl.BlockSpec(memory_space=out_space), outs),
+            out_specs=jax.tree.map(lambda m: pl.BlockSpec(memory_space=m), spaces),
             scratch_shapes=scratch,
+            input_output_aliases=aliases,
             compiler_params=pltpu.CompilerParams(vmem_limit_bytes=32 * 1024 * 1024),
+            cost_estimate=pl.CostEstimate(flops=flops, bytes_accessed=0, transcendentals=0) if flops else None,
             name=name,
         )(*operands)
 
     def along_x(xa, xb):
         return lax.ppermute(xa, ("gx", "gy"), up), lax.ppermute(xb, ("gx", "gy"), down)
 
-    def along_y(ra, rb, sources):
-        like = arr(ra.shape, f32)
-        ye, yo = call(turn_kernel, (like, like), [], "turn", ra, rb, *sources)
+    def along_y(ra, rb, ye, yo):
+        like = arr(ye.shape, f32)
+        ye, yo = call(turn_kernel, (like, like), [], "turn", ra, rb, ye, yo, aliases={2: 0, 3: 1})
         return lax.ppermute(ye, "gy", far), lax.ppermute(yo, "gy", near)
 
     sources = (body_a, body_b, active, impulse0, jac_a, jac_b, start, minv, precond, bias, friction, sticking)
@@ -483,29 +518,44 @@
         space=pltpu.HBM,
     )
     fixed, lam = made[:7], made[7]
-    id_a, id_b, hot_a, hot_b, own, halo, v_own, m_own, xa, xb = made[8:]
+    id_a, id_b, hot_a, hot_b, own_x, halo_x, v_own, m_own, xa, xb = made[8:]
     part_t = arr((2 * DOF, rows, lanes), f32)
     halo_tables = ()
+    ids = (id_a, id_b)
+    hots = (hot_a, hot_b)
     for step in range(ITERS):
         first, last = step == 0, step == ITERS - 1
         came_x = along_x(xa, xb)
-        part = call(inner_kernel, part_t, table, "inner", own, v_own, m_own, id_a, id_b)
-        came_y = along_y(*came_x, (own, halo, v_own, m_own) if first else (own, halo))
+        sent = message(GROUP * (2 if first else 1))
+        own, ye, yo, part, halo = call(
+            lambda *refs, first=first: window_kernel(first, False, *refs),
+            (own_t, sent, sent, part_t, halo_t), work + table, "window",
+            *fixed[:2], lam, *ids, *hots, v_own, m_own, own_x,
+        )
+        came_y = along_y(*came_x, ye, yo)
         part = call(
             lambda *refs, first=first: side_kernel(first, *refs), part_t, table, "side",
-            own, halo, v_own, m_own, id_a, id_b, part, *came_x, *halo_tables,
+            own_x, halo_x, v_own, m_own, *ids, part, *came_x, *halo_tables,
         )
         sent = message(LAST_GROUP if last else GROUP)
-        outs = (lam_t, own_t, halo_t, sent, sent) + ((halo_t, halo_t) if first else ())
-        lam, own, halo, xa, xb, *made = call(
+        outs = (lam_t, own_t, sent, sent) + (halo_t,) * (3 if first else 0 if last else 1)
+        lam, own_x, xa, xb, *made = call(
             lambda *refs, first=first, last=last: middle_kernel(first, last, *refs), outs, table + work, "middle",
-            *fixed, lam, id_a, id_b, hot_a, hot_b, own, halo, v_own, m_own, part, *came_x, *came_y, *halo_tables,
+            *fixed, lam, *ids, *hots, own_x, halo_x, own, halo, v_own, m_own, part, *came_x, *came_y, *halo_tables,
         )
-        halo_tables = tuple(made) or halo_tables
+        if not last:
+            halo_x = made[0]
+        if first:
+            halo_tables = tuple(made[1:])
     came_x = along_x(xa, xb)
-    lam = call(keep_kernel, lam_t, [pltpu.SemaphoreType.DMA], "keep", lam, out_space=pltpu.HBM)
-    came_y = along_y(*came_x, (halo,))
-    out = call(last_kernel, arr(start.shape, f32), [], "last", own, v_own, m_own, *came_x, *came_y)
+    own, ye, yo, lam = call(
+        lambda *refs: window_kernel(False, True, *refs),
+        (own_t, sent, sent, lam_t), work + table + [pltpu.SemaphoreType.DMA], "window",
+        *fixed[:2], lam, *ids, *hots, v_own, m_own, own_x,
+        out_spaces=(pltpu.VMEM,) * 3 + (pltpu.HBM,),
+    )
+    came_y = along_y(*came_x, ye, yo)
+    out = call(last_kernel, arr(start.shape, f32), [], "last", own_x, own, v_own, m_own, *came_x, *came_y)
     return lam.reshape(ROWS, 1, 1, rows, lanes), out.reshape(velocity0.shape)
 
 

time: 40.7 us -> 39.3 us (0.966)
  waiting for transfers between devices: 14.4 us -> 10.4 us
  Pallas kernels: 12.6 us -> 15 us
    ppermute x4, waiting for transfers between devices: 3.58 us -> 0.01 us  [along_x(): lax.ppermute(xa, ('gx', 'gy'), up)]
    pallas_call x16, Pallas kernels: 12.6 us -> 15 us  [call(): pl.pallas_call(kernel, out_shape=outs, in_specs=[pl.BlockSpec(memory_spac...]
    ppermute x4, waiting for transfers between devices: 7.08 us -> 4.74 us  [along_x(): lax.ppermute(xb, ('gx', 'gy'), down)]
    ppermute x8, waiting for transfers between devices: 3.76 us -> 5.65 us  [along_y(): return (lax.ppermute(ye, 'gy', far), lax.ppermute(yo, 'gy', near))]
  transfers between devices with their start and end apart: 16 -> 16, of which waited for: 12 -> 8; matrix products, arithmetic and copies ran while one was open for 0% -> 0% of each run, Pallas kernels for 8% -> 18%
where the time goes in v5:
time: 39.3 us; the launch traced here: 39 us
  Pallas kernels  15 us (38%)
  starting transfers between devices  12.9 us (33%)
  waiting for transfers between devices  10.4 us (26%)
  between operations  0.73 us (2%)
    pallas_call x16, Pallas kernels, call(): pl.pallas_call(kernel, out_shape=outs, in_specs=[pl.BlockSpec(memory_spac...  15 us
    ppermute x4, starting transfers between devices, along_x(): lax.ppermute(xa, ('gx', 'gy'), up)  6.81 us
    ppermute x8, starting transfers between devices, along_y(): return (lax.ppermute(ye, 'gy', far), lax.ppermute(yo, 'gy', near))  6.06 us
    ppermute x8, waiting for transfers between devices, along_y(): return (lax.ppermute(ye, 'gy', far), lax.ppermute(yo, 'gy', near))  5.65 us
    ppermute x4, waiting for transfers between devices, along_x(): lax.ppermute(xb, ('gx', 'gy'), down)  4.74 us
  transfers between devices with their start and end apart: 16, of which 8 were waited for; matrix products, arithmetic and copies ran while one was open for 0% of the time, Pallas kernels for 18%

profile of v5, /device:TPU:1, one launch (start us, length us, event | category | flops | bytes accessed | tf_op | source)
XLA Modules:
  0.0 39.0 jit_solution(17207489724113966596)
XLA Ops:
  0.6 3.1 %first.1 = (f32[18,32,128]{2,1,0:T(8,128)S(1)}, f32[18,32,128]{2,1,0:T(8,128)S(1)}, f32[9,32,128]{2,1,0:T(8,128)S(1)}, f32[3,32,128]{2,1,0:T(8,128)S(1)}, f32[32...) custom-call(s32[32,128]{1,0:T(8,128)} %bitcast.24, ...), custom_call_target="tpu_custom_call" | custom-call | tf_op jit(solution)/shard_map/first/pallas_call | solution.py:486
  3.7 2.1 %collective-permute-start = (f32[64,128]{1,0:T(8,128)S(1)}, f32[64,128]{1,0:T(8,128)S(1)}, u32[]{:S(2)}, u32[]{:S(2)}) collective-permute-start(f32[64,128]{1,0:T(8,128)S(1)} %get-tuple-element.82), channel_id=1, source_target_pairs={{0,1},{1,5},{2,3},{3,7},{4,0},{5,9},{6,2},{7,11},{8,4},{9,13},{10,... | collective-permute-start | bytes 98312 | tf_op jit(solution)/shard_map/ppermute | solution.py:499
  5.9 0.0 collective-permute-start.1
  5.9 1.6 %window.4 = (f32[16,8,128]{2,1,0:T(8,128)S(1)}, f32[64,128]{1,0:T(8,128)S(1)}, f32[64,128]{1,0:T(8,128)S(1)}, f32[12,32,128]{2,1,0:T(8,128)S(1)}, f32[9,8,128]{2,1,0:T(8,128)S(1)}) custom-call(f32[18,32,128]{2,1,0:T(8,128)S(1)} %get-tuple-element.63.refs_0_, f32[18,32,128]{2,1,0:T(8,128)S(1)} %get-tuple-element.64.refs_1_, ...), custom_call_target="tpu_custom_call" | custom-call | tf_op jit(solution)/shard_map/window/pallas_call | solution.py:486
  7.4 0.0 collective-permute-done.refs_7_.ra.refs_19_
  7.4 1.2 %collective-permute-done.1.refs_8_.rb.refs_20_ = f32[64,128]{1,0:T(8,128)S(1)} collective-permute-done((f32[64,128]{1,0:T(8,128)S(1)}, f32[64,128]{1,0:T(8,128)S(1)}, u32[]{:S(2)}, u32[]{:S(2)}) %collective-permute-start.1) | collective-permute-done | bytes 32800 | tf_op jit(solution)/shard_map/ppermute | solution.py:499
  8.6 1.9 %collective-permute-start.2 = (f32[64,128]{1,0:T(8,128)S(1)}, f32[64,128]{1,0:T(8,128)S(1)}, u32[]{:S(2)}, u32[]{:S(2)}) collective-permute-start(f32[64,128]{1,0:T(8,128)S(1)} %get-tuple-element.86), channel_id=1, source_target_pairs={{0,3},{1,2},{2,1},{3,0},{4,7},{5,6},{6,5},{7,4},{8,11},{9,10},{10,... | collective-permute-start | bytes 98312 | tf_op jit(solution)/shard_map/ppermute | solution.py:504
  10.5 0.1 collective-permute-start.3
  10.6 0.4 %side.3.refs_18_ = f32[12,32,128]{2,1,0:T(8,128)S(1)} custom-call(f32[16,8,128]{2,1,0:T(8,128)S(1)} %get-tuple-element.75.refs_9_.refs_0_.refs_12_, f32[9,8,128]{2,1,0:T(8,128)S(1)} %get-tuple-element.76.refs_1_.refs_13_, f32[16,8,128]{2,1,0:T(8,128)S(1)} %get-tuple-element.77.refs_7_.refs_2_.refs_16_.v_own, ...), custom_call_target="tpu_custom_call" | custom-call | tf_op jit(solution)/shard_map/side/pallas_call | solution.py:486
  11.0 1.1 %collective-permute-done.2.refs_21_ = f32[64,128]{1,0:T(8,128)S(1)} collective-permute-done((f32[64,128]{1,0:T(8,128)S(1)}, f32[64,128]{1,0:T(8,128)S(1)}, u32[]{:S(2)}, u32[]{:S(2)}) %collective-permute-start.2) | collective-permute-done | bytes 32800 | tf_op jit(solution)/shard_map/ppermute | solution.py:504
  12.1 0.0 collective-permute-done.3.refs_22_
  12.1 1.4 %middle.3 = (f32[3,32,128]{2,1,0:T(8,128)S(1)}, f32[16,8,128]{2,1,0:T(8,128)S(1)}, f32[32,128]{1,0:T(8,128)S(1)}, f32[32,128]{1,0:T(8,128)S(1)}, f32[9,8,128]{2,...) custom-call(f32[18,32,128]{2,1,0:T(8,128)S(1)} %get-tuple-element.63.refs_0_, ...), custom_call_target="tpu_custom_call" | custom-call | tf_op jit(solution)/shard_map/middle/pallas_call | solution.py:486
  13.5 1.6 %collective-permute-start.4 = (f32[32,128]{1,0:T(8,128)S(1)}, f32[32,128]{1,0:T(8,128)S(1)}, u32[]{:S(2)}, u32[]{:S(2)}) collective-permute-start(f32[32,128]{1,0:T(8,128)S(1)} %get-tuple-element.94), channel_id=1, source_target_pairs={{0,1},{1,5},{2,3},{3,7},{4,0},{5,9},{6,2},{7,11},{8,4},{9,13},{10,... | collective-permute-start | bytes 49160 | tf_op jit(solution)/shard_map/ppermute | solution.py:499
  15.1 0.0 collective-permute-start.5
  15.1 1.6 %window.5 = (f32[16,8,128]{2,1,0:T(8,128)S(1)}, f32[32,128]{1,0:T(8,128)S(1)}, f32[32,128]{1,0:T(8,128)S(1)}, f32[12,32,128]{2,1,0:T(8,128)S(1)}, f32[9,8,128]{2,1,0:T(8,128)S(1)}) custom-call(f32[18,32,128]{2,1,0:T(8,128)S(1)} %get-tuple-element.63.refs_0_, f32[18,32,128]{2,1,0:T(8,128)S(1)} %get-tuple-element.64.refs_1_, ...), custom_call_target="tpu_custom_call" | custom-call | tf_op jit(solution)/shard_map/window/pallas_call | solution.py:486
  16.7 0.0 collective-permute-done.4.refs_7_.ra.refs_19_
  16.7 1.2 %collective-permute-done.5.refs_8_.rb.refs_20_ = f32[32,128]{1,0:T(8,128)S(1)} collective-permute-done((f32[32,128]{1,0:T(8,128)S(1)}, f32[32,128]{1,0:T(8,128)S(1)}, u32[]{:S(2)}, u32[]{:S(2)}) %collective-permute-start.5) | collective-permute-done | bytes 16416 | tf_op jit(solution)/shard_map/ppermute | solution.py:499
  17.9 1.2 %collective-permute-start.6 = (f32[32,128]{1,0:T(8,128)S(1)}, f32[32,128]{1,0:T(8,128)S(1)}, u32[]{:S(2)}, u32[]{:S(2)}) collective-permute-start(f32[32,128]{1,0:T(8,128)S(1)} %get-tuple-element.100), channel_id=1, source_target_pairs={{0,3},{1,2},{2,1},{3,0},{4,7},{5,6},{6,5},{7,4},{8,11},{9,10},{10,... | collective-permute-start | bytes 49160 | tf_op jit(solution)/shard_map/ppermute | solution.py:504
  19.1 0.5 %collective-permute-start.7 = (f32[32,128]{1,0:T(8,128)S(1)}, f32[32,128]{1,0:T(8,128)S(1)}, u32[]{:S(2)}, u32[]{:S(2)}) collective-permute-start(f32[32,128]{1,0:T(8,128)S(1)} %get-tuple-element.101), channel_id=1, source_target_pairs={{0,1},{1,0},{2,3},{3,2},{4,5},{5,4},{6,7},{7,6},{8,9},{9,8},{10,11... | collective-permute-start | bytes 49160 | tf_op jit(solution)/shard_map/ppermute | solution.py:504
  19.7 0.4 %side.4.refs_18_ = f32[12,32,128]{2,1,0:T(8,128)S(1)} custom-call(f32[16,8,128]{2,1,0:T(8,128)S(1)} %get-tuple-element.89.refs_9_.refs_0_.refs_12_, f32[9,8,128]{2,1,0:T(8,128)S(1)} %get-tuple-element.90.refs_1_.refs_13_, f32[16,8,128]{2,1,0:T(8,128)S(1)} %get-tuple-element.77.refs_7_.refs_2_.refs_16_.v_own, ...), custom_call_target="tpu_custom_call" | custom-call | tf_op jit(solution)/shard_map/side/pallas_call | solution.py:486
  20.1 1.0 %collective-permute-done.6.refs_21_ = f32[32,128]{1,0:T(8,128)S(1)} collective-permute-done((f32[32,128]{1,0:T(8,128)S(1)}, f32[32,128]{1,0:T(8,128)S(1)}, u32[]{:S(2)}, u32[]{:S(2)}) %collective-permute-start.6) | collective-permute-done | bytes 16416 | tf_op jit(solution)/shard_map/ppermute | solution.py:504
  21.1 0.0 collective-permute-done.7.refs_22_
  21.1 1.4 %middle.4 = (f32[3,32,128]{2,1,0:T(8,128)S(1)}, f32[16,8,128]{2,1,0:T(8,128)S(1)}, f32[32,128]{1,0:T(8,128)S(1)}, f32[32,128]{1,0:T(8,128)S(1)}, f32[9,8,128]{2,1,0:T(8,128)S(1)}) custom-call(f32[18,32,128]{2,1,0:T(8,128)S(1)} %get-tuple-element.63.refs_0_, f32[18,32,128]{2,1,0:T(8,128)S(1)} %get-tuple-element.64.refs_1_, ...), custom_call_target="tpu_custom_call" | custom-call | tf_op jit(solution)/shard_map/middle/pallas_call | solution.py:486
  22.4 1.5 %collective-permute-start.8 = (f32[32,128]{1,0:T(8,128)S(1)}, f32[32,128]{1,0:T(8,128)S(1)}, u32[]{:S(2)}, u32[]{:S(2)}) collective-permute-start(f32[32,128]{1,0:T(8,128)S(1)} %get-tuple-element.108), channel_id=1, source_target_pairs={{0,1},{1,5},{2,3},{3,7},{4,0},{5,9},{6,2},{7,11},{8,4},{9,13},{10,... | collective-permute-start | bytes 49160 | tf_op jit(solution)/shard_map/ppermute | solution.py:499
  23.9 0.0 collective-permute-start.9
  23.9 1.6 %window.6 = (f32[16,8,128]{2,1,0:T(8,128)S(1)}, f32[32,128]{1,0:T(8,128)S(1)}, f32[32,128]{1,0:T(8,128)S(1)}, f32[12,32,128]{2,1,0:T(8,128)S(1)}, f32[9,8,128]{2,1,0:T(8,128)S(1)}) custom-call(f32[18,32,128]{2,1,0:T(8,128)S(1)} %get-tuple-element.63.refs_0_, f32[18,32,128]{2,1,0:T(8,128)S(1)} %get-tuple-element.64.refs_1_, ...), custom_call_target="tpu_custom_call" | custom-call | tf_op jit(solution)/shard_map/window/pallas_call | solution.py:486
  25.5 0.0 collective-permute-done.8.refs_7_.ra.refs_19_
  25.5 1.0 %collective-permute-done.9.refs_8_.rb.refs_20_ = f32[32,128]{1,0:T(8,128)S(1)} collective-permute-done((f32[32,128]{1,0:T(8,128)S(1)}, f32[32,128]{1,0:T(8,128)S(1)}, u32[]{:S(2)}, u32[]{:S(2)}) %collective-permute-start.9) | collective-permute-done | bytes 16416 | tf_op jit(solution)/shard_map/ppermute | solution.py:499
  26.5 1.0 %collective-permute-start.10 = (f32[32,128]{1,0:T(8,128)S(1)}, f32[32,128]{1,0:T(8,128)S(1)}, u32[]{:S(2)}, u32[]{:S(2)}) collective-permute-start(f32[32,128]{1,0:T(8,128)S(1)} %get-tuple-element.112), channel_id=1, source_target_pairs={{0,3},{1,2},{2,1},{3,0},{4,7},{5,6},{6,5},{7,4},{8,11},{9,10},{10,... | collective-permute-start | bytes 49160 | tf_op jit(solution)/shard_map/ppermute | solution.py:504
  27.5 0.6 %collective-permute-start.11 = (f32[32,128]{1,0:T(8,128)S(1)}, f32[32,128]{1,0:T(8,128)S(1)}, u32[]{:S(2)}, u32[]{:S(2)}) collective-permute-start(f32[32,128]{1,0:T(8,128)S(1)} %get-tuple-element.113), channel_id=1, source_target_pairs={{0,1},{1,0},{2,3},{3,2},{4,5},{5,4},{6,7},{7,6},{8,9},{9,8},{10,11... | collective-permute-start | bytes 49160 | tf_op jit(solution)/shard_map/ppermute | solution.py:504
  28.1 0.4 %side.5.refs_18_ = f32[12,32,128]{2,1,0:T(8,128)S(1)} custom-call(f32[16,8,128]{2,1,0:T(8,128)S(1)} %get-tuple-element.103.refs_9_.refs_0_.refs_12_, f32[9,8,128]{2,1,0:T(8,128)S(1)} %get-tuple-element.104.refs_1_.refs_13_, f32[16,8,128]{2,1,0:T(8,128)S(1)} %get-tuple-element.77.refs_7_.refs_2_.refs_16_.v_own, ...), custom_call_target="tpu_custom_call" | custom-call | tf_op jit(solution)/shard_map/side/pallas_call | solution.py:486
  28.5 1.1 %collective-permute-done.10.refs_21_ = f32[32,128]{1,0:T(8,128)S(1)} collective-permute-done((f32[32,128]{1,0:T(8,128)S(1)}, f32[32,128]{1,0:T(8,128)S(1)}, u32[]{:S(2)}, u32[]{:S(2)}) %collective-permute-start.10) | collective-permute-done | bytes 16416 | tf_op jit(solution)/shard_map/ppermute | solution.py:504
  29.7 0.0 collective-permute-done.11.refs_22_
  29.7 1.4 %middle.5 = (f32[3,32,128]{2,1,0:T(8,128)S(1)}, f32[16,8,128]{2,1,0:T(8,128)S(1)}, f32[24,128]{1,0:T(8,128)S(1)}, f32[24,128]{1,0:T(8,128)S(1)}) custom-call(f32[18,32,128]{2,1,0:T(8,128)S(1)} %get-tuple-element.63.refs_0_, f32[18,32,128]{2,1,0:T(8,128)S(1)} %get-tuple-element.64.refs_1_, f32[9,32,128]{2,1,0:T(8,128)S(1)} %get-tuple-element.65.refs_2_, ...), custom_call_target="tpu_custom_call" | custom-call | tf_op jit(solution)/shard_map/middle/pallas_call | solution.py:486
  31.1 1.6 %collective-permute-start.12 = (f32[24,128]{1,0:T(8,128)S(1)}, f32[24,128]{1,0:T(8,128)S(1)}, u32[]{:S(2)}, u32[]{:S(2)}) collective-permute-start(f32[24,128]{1,0:T(8,128)S(1)} %get-tuple-element.118), channel_id=1, source_target_pairs={{0,1},{1,5},{2,3},{3,7},{4,0},{5,9},{6,2},{7,11},{8,4},{9,13},{10,... | collective-permute-start | bytes 36872 | tf_op jit(solution)/shard_map/ppermute | solution.py:499
  32.6 0.0 collective-permute-start.13
  32.7 1.1 %window.7 = (f32[16,8,128]{2,1,0:T(8,128)S(1)}, f32[24,128]{1,0:T(8,128)S(1)}, f32[24,128]{1,0:T(8,128)S(1)}, f32[3,32,128]{2,1,0:T(8,128)}) custom-call(f32[18,32,128]{2,1,0:T(8,128)S(1)} %get-tuple-element.63.refs_0_, f32[18,32,128]{2,1,0:T(8,128)S(1)} %get-tuple-element.64.refs_1_, f32[3,32,128]{2,1,0:T(8,128)S(1)} %get-tuple-element.114.refs_2_, ...), custom_call_target="tpu_custom_call" | custom-call | tf_op jit(solution)/shard_map/window/pallas_call | solution.py:486
  33.8 0.0 collective-permute-done.12.ra
  33.8 1.4 %collective-permute-done.13.rb = f32[24,128]{1,0:T(8,128)S(1)} collective-permute-done((f32[24,128]{1,0:T(8,128)S(1)}, f32[24,128]{1,0:T(8,128)S(1)}, u32[]{:S(2)}, u32[]{:S(2)}) %collective-permute-start.13) | collective-permute-done | bytes 12320 | tf_op jit(solution)/shard_map/ppermute | solution.py:499
  35.2 0.7 %collective-permute-start.14 = (f32[24,128]{1,0:T(8,128)S(1)}, f32[24,128]{1,0:T(8,128)S(1)}, u32[]{:S(2)}, u32[]{:S(2)}) collective-permute-start(f32[24,128]{1,0:T(8,128)S(1)} %get-tuple-element.122), channel_id=1, source_target_pairs={{0,3},{1,2},{2,1},{3,0},{4,7},{5,6},{6,5},{7,4},{8,11},{9,10},{10,... | collective-permute-start | bytes 36872 | tf_op jit(solution)/shard_map/ppermute | solution.py:504
  35.9 0.0 collective-permute-start.15
  35.9 2.4 %collective-permute-done.14.qe = f32[24,128]{1,0:T(8,128)S(1)} collective-permute-done((f32[24,128]{1,0:T(8,128)S(1)}, f32[24,128]{1,0:T(8,128)S(1)}, u32[]{:S(2)}, u32[]{:S(2)}) %collective-permute-start.14) | collective-permute-done | bytes 12320 | tf_op jit(solution)/shard_map/ppermute | solution.py:504
  38.3 0.0 collective-permute-done.15.qo
  38.3 0.7 %last.1 = f32[96,128]{1,0:T(8,128)} custom-call(f32[16,8,128]{2,1,0:T(8,128)S(1)} %get-tuple-element.115.refs_9_.own_x, f32[16,8,128]{2,1,0:T(8,128)S(1)} %get-tuple-element.117.own, f32[16,8,128]{2,1,0:T(8,128)S(1)} %get-tuple-element.77.refs_7_.refs_2_.refs_16_.v_own, f32[16,8,128]{2,1,0:T(8,128)S(1)} %get-tuple-element.78.refs_8_.refs_3_.refs_17_.m_own, ...), custom_call_target="tpu_custom_call" | custom-call | tf_op jit(solution)/shard_map/last/pallas_call | solution.py:486
  (4 shorter events, 0.0 us)
Async XLA Ops:
  3.7 3.7 %collective-permute-start = (f32[64,128]{1,0:T(8,128)S(1)}, f32[64,128]{1,0:T(8,128)S(1)}, u32[]{:S(2)}, u32[]{:S(2)}) collective-permute-start(f32[64,128]{1,0:T(8,128)S(1)} %get-tuple-element.82), channel_id=1, source_target_pairs={{0,1},{1,5},{2,3},{3,7},{4,0},{5,9},{6,2},{7,11},{8,4},{9,13},{10,... | collective-permute-start | bytes 98312 | tf_op jit(solution)/shard_map/ppermute | solution.py:499
  5.9 2.8 %collective-permute-start.1 = (f32[64,128]{1,0:T(8,128)S(1)}, f32[64,128]{1,0:T(8,128)S(1)}, u32[]{:S(2)}, u32[]{:S(2)}) collective-permute-start(f32[64,128]{1,0:T(8,128)S(1)} %get-tuple-element.83), channel_id=1, source_target_pairs={{1,0},{5,1},{3,2},{7,3},{0,4},{9,5},{2,6},{11,7},{4,8},{13,9},{6,1... | collective-permute-start | bytes 98312 | tf_op jit(solution)/shard_map/ppermute | solution.py:499
  8.6 3.5 %collective-permute-start.2 = (f32[64,128]{1,0:T(8,128)S(1)}, f32[64,128]{1,0:T(8,128)S(1)}, u32[]{:S(2)}, u32[]{:S(2)}) collective-permute-start(f32[64,128]{1,0:T(8,128)S(1)} %get-tuple-element.86), channel_id=1, source_target_pairs={{0,3},{1,2},{2,1},{3,0},{4,7},{5,6},{6,5},{7,4},{8,11},{9,10},{10,... | collective-permute-start | bytes 98312 | tf_op jit(solution)/shard_map/ppermute | solution.py:504
  10.5 1.6 %collective-permute-start.3 = (f32[64,128]{1,0:T(8,128)S(1)}, f32[64,128]{1,0:T(8,128)S(1)}, u32[]{:S(2)}, u32[]{:S(2)}) collective-permute-start(f32[64,128]{1,0:T(8,128)S(1)} %get-tuple-element.87), channel_id=1, source_target_pairs={{0,1},{1,0},{2,3},{3,2},{4,5},{5,4},{6,7},{7,6},{8,9},{9,8},{10,11... | collective-permute-start | bytes 98312 | tf_op jit(solution)/shard_map/ppermute | solution.py:504
  13.5 3.2 %collective-permute-start.4 = (f32[32,128]{1,0:T(8,128)S(1)}, f32[32,128]{1,0:T(8,128)S(1)}, u32[]{:S(2)}, u32[]{:S(2)}) collective-permute-start(f32[32,128]{1,0:T(8,128)S(1)} %get-tuple-element.94), channel_id=1, source_target_pairs={{0,1},{1,5},{2,3},{3,7},{4,0},{5,9},{6,2},{7,11},{8,4},{9,13},{10,... | collective-permute-start | bytes 49160 | tf_op jit(solution)/shard_map/ppermute | solution.py:499
  15.1 2.8 %collective-permute-start.5 = (f32[32,128]{1,0:T(8,128)S(1)}, f32[32,128]{1,0:T(8,128)S(1)}, u32[]{:S(2)}, u32[]{:S(2)}) collective-permute-start(f32[32,128]{1,0:T(8,128)S(1)} %get-tuple-element.95), channel_id=1, source_target_pairs={{1,0},{5,1},{3,2},{7,3},{0,4},{9,5},{2,6},{11,7},{4,8},{13,9},{6,1... | collective-permute-start | bytes 49160 | tf_op jit(solution)/shard_map/ppermute | solution.py:499
  17.9 3.2 %collective-permute-start.6 = (f32[32,128]{1,0:T(8,128)S(1)}, f32[32,128]{1,0:T(8,128)S(1)}, u32[]{:S(2)}, u32[]{:S(2)}) collective-permute-start(f32[32,128]{1,0:T(8,128)S(1)} %get-tuple-element.100), channel_id=1, source_target_pairs={{0,3},{1,2},{2,1},{3,0},{4,7},{5,6},{6,5},{7,4},{8,11},{9,10},{10,... | collective-permute-start | bytes 49160 | tf_op jit(solution)/shard_map/ppermute | solution.py:504
  19.1 1.9 %collective-permute-start.7 = (f32[32,128]{1,0:T(8,128)S(1)}, f32[32,128]{1,0:T(8,128)S(1)}, u32[]{:S(2)}, u32[]{:S(2)}) collective-permute-start(f32[32,128]{1,0:T(8,128)S(1)} %get-tuple-element.101), channel_id=1, source_target_pairs={{0,1},{1,0},{2,3},{3,2},{4,5},{5,4},{6,7},{7,6},{8,9},{9,8},{10,11... | collective-permute-start | bytes 49160 | tf_op jit(solution)/shard_map/ppermute | solution.py:504
  22.4 3.1 %collective-permute-start.8 = (f32[32,128]{1,0:T(8,128)S(1)}, f32[32,128]{1,0:T(8,128)S(1)}, u32[]{:S(2)}, u32[]{:S(2)}) collective-permute-start(f32[32,128]{1,0:T(8,128)S(1)} %get-tuple-element.108), channel_id=1, source_target_pairs={{0,1},{1,5},{2,3},{3,7},{4,0},{5,9},{6,2},{7,11},{8,4},{9,13},{10,... | collective-permute-start | bytes 49160 | tf_op jit(solution)/shard_map/ppermute | solution.py:499
  23.9 2.6 %collective-permute-start.9 = (f32[32,128]{1,0:T(8,128)S(1)}, f32[32,128]{1,0:T(8,128)S(1)}, u32[]{:S(2)}, u32[]{:S(2)}) collective-permute-start(f32[32,128]{1,0:T(8,128)S(1)} %get-tuple-element.109), channel_id=1, source_target_pairs={{1,0},{5,1},{3,2},{7,3},{0,4},{9,5},{2,6},{11,7},{4,8},{13,9},{6,1... | collective-permute-start | bytes 49160 | tf_op jit(solution)/shard_map/ppermute | solution.py:499
  26.5 3.2 %collective-permute-start.10 = (f32[32,128]{1,0:T(8,128)S(1)}, f32[32,128]{1,0:T(8,128)S(1)}, u32[]{:S(2)}, u32[]{:S(2)}) collective-permute-start(f32[32,128]{1,0:T(8,128)S(1)} %get-tuple-element.112), channel_id=1, source_target_pairs={{0,3},{1,2},{2,1},{3,0},{4,7},{5,6},{6,5},{7,4},{8,11},{9,10},{10,... | collective-permute-start | bytes 49160 | tf_op jit(solution)/shard_map/ppermute | solution.py:504
  27.5 2.2 %collective-permute-start.11 = (f32[32,128]{1,0:T(8,128)S(1)}, f32[32,128]{1,0:T(8,128)S(1)}, u32[]{:S(2)}, u32[]{:S(2)}) collective-permute-start(f32[32,128]{1,0:T(8,128)S(1)} %get-tuple-element.113), channel_id=1, source_target_pairs={{0,1},{1,0},{2,3},{3,2},{4,5},{5,4},{6,7},{7,6},{8,9},{9,8},{10,11... | collective-permute-start | bytes 49160 | tf_op jit(solution)/shard_map/ppermute | solution.py:504
  31.1 2.7 %collective-permute-start.12 = (f32[24,128]{1,0:T(8,128)S(1)}, f32[24,128]{1,0:T(8,128)S(1)}, u32[]{:S(2)}, u32[]{:S(2)}) collective-permute-start(f32[24,128]{1,0:T(8,128)S(1)} %get-tuple-element.118), channel_id=1, source_target_pairs={{0,1},{1,5},{2,3},{3,7},{4,0},{5,9},{6,2},{7,11},{8,4},{9,13},{10,... | collective-permute-start | bytes 36872 | tf_op jit(solution)/shard_map/ppermute | solution.py:499
  32.6 2.5 %collective-permute-start.13 = (f32[24,128]{1,0:T(8,128)S(1)}, f32[24,128]{1,0:T(8,128)S(1)}, u32[]{:S(2)}, u32[]{:S(2)}) collective-permute-start(f32[24,128]{1,0:T(8,128)S(1)} %get-tuple-element.119), channel_id=1, source_target_pairs={{1,0},{5,1},{3,2},{7,3},{0,4},{9,5},{2,6},{11,7},{4,8},{13,9},{6,1... | collective-permute-start | bytes 36872 | tf_op jit(solution)/shard_map/ppermute | solution.py:499
  35.2 3.1 %collective-permute-start.14 = (f32[24,128]{1,0:T(8,128)S(1)}, f32[24,128]{1,0:T(8,128)S(1)}, u32[]{:S(2)}, u32[]{:S(2)}) collective-permute-start(f32[24,128]{1,0:T(8,128)S(1)} %get-tuple-element.122), channel_id=1, source_target_pairs={{0,3},{1,2},{2,1},{3,0},{4,7},{5,6},{6,5},{7,4},{8,11},{9,10},{10,... | collective-permute-start | bytes 36872 | tf_op jit(solution)/shard_map/ppermute | solution.py:504
  35.9 2.5 %collective-permute-start.15 = (f32[24,128]{1,0:T(8,128)S(1)}, f32[24,128]{1,0:T(8,128)S(1)}, u32[]{:S(2)}, u32[]{:S(2)}) collective-permute-start(f32[24,128]{1,0:T(8,128)S(1)} %get-tuple-element.123), channel_id=1, source_target_pairs={{0,1},{1,0},{2,3},{3,2},{4,5},{5,4},{6,7},{7,6},{8,9},{9,8},{10,11... | collective-permute-start | bytes 36872 | tf_op jit(solution)/shard_map/ppermute | solution.py:504

commit v6 on v5

--- a/solution.py
+++ b/solution.py
@@ -114,12 +114,11 @@
         f = force_ref[pl.ds(r, 8, stride=rows), :]
         hi = f.astype(jnp.bfloat16).astype(jnp.float32)
         lo = f - hi
-        both = jnp.concatenate([hi, lo], axis=0)
-        head = jnp.broadcast_to(row_of(index_ref, r) >> 8, (16, LANES))
+        head = jnp.broadcast_to(row_of(index_ref, r) >> 8, (8, LANES))
         for k, h in enumerate(heads):
-            left_ref[16 * k : 16 * (k + 1), r * LANES : (r + 1) * LANES] = jnp.where(
-                head == h, both, 0.0
-            ).astype(jnp.bfloat16)
+            mask = head == h
+            both = jnp.concatenate([jnp.where(mask, hi, 0.0), jnp.where(mask, lo, 0.0)], axis=0)
+            left_ref[16 * k : 16 * (k + 1), r * LANES : (r + 1) * LANES] = both.astype(jnp.bfloat16)
 
 
 X_HEADS = (0, 3, 7)
@@ -130,31 +129,36 @@
     return heads + tuple(h + 8 for h in heads if h < 4 or h == 7)
 
 
-def scatter(lam, jac_a, jac_b, id_a, id_b, hot_a, hot_b, force, left_a, left_b, heads):
-    contract = (((1,), (0,)), ((), ()))
+def scatter(lam, jac_a, jac_b, id_a, id_b, hot, force, left, heads, between=None):
+    contacts = hot.shape[0] // 2
     both = with_halo(heads)
-    left_a, left_b = left_a.at[: 16 * len(heads)], left_b.at[: 16 * len(both)]
+    rows, own_rows = 16 * len(both), 16 * len(heads)
     forces(lam, jac_a, force)
-    spread(force, id_a, left_a, heads)
-    sum_a = lax.dot_general(left_a[...], hot_a[...], contract, preferred_element_type=jnp.float32)
+    spread(force, id_a, left.at[:own_rows, :contacts], heads)
+    left[own_rows:rows, :contacts] = jnp.zeros((rows - own_rows, contacts), jnp.bfloat16)
+    if between is not None:
+        sums = jnp.dot(left[:rows, :contacts], hot[:contacts, :], preferred_element_type=jnp.float32)
+        between()
     forces(lam, jac_b, force)
-    spread(force, id_b, left_b, both)
-    sum_b = lax.dot_general(left_b[...], hot_b[...], contract, preferred_element_type=jnp.float32)
-
-    def tile(s, k, j):
+    spread(force, id_b, left.at[:rows, contacts:], both)
+    if between is None:
+        sums = jnp.dot(left[:rows, :], hot[...], preferred_element_type=jnp.float32)
+    else:
+        sums = sums + jnp.dot(left[:rows, contacts:], hot[contacts:, :], preferred_element_type=jnp.float32)
+
+    def tile(k, j):
         lanes = slice(j * LANES, (j + 1) * LANES)
-        return s[16 * k : 16 * k + 8, lanes] + s[16 * k + 8 : 16 * k + 16, lanes]
+        return sums[16 * k : 16 * k + 8, lanes] + sums[16 * k + 8 : 16 * k + 16, lanes]
 
     own, halo = {}, {}
     for k, h in enumerate(both):
         for j in range(2):
             if h < 8:
-                own[2 * h + j] = tile(sum_a, k, j) + tile(sum_b, k, j)
+                own[2 * h + j] = tile(k, j)
             elif h < 12:
-                halo[2 * (h - 8) + j] = tile(sum_b, k, j)
-    halo_corner = both.index(15) if 15 in both else None
-    if halo_corner is not None:
-        halo[HALO_CORNER] = tile(sum_b, halo_corner, 1)
+                halo[2 * (h - 8) + j] = tile(k, j)
+    if 15 in both:
+        halo[HALO_CORNER] = tile(both.index(15), 1)
     return own, halo
 
 
@@ -247,9 +251,9 @@
 
 
 def first_kernel(*refs):
-    sources, kept, outs = refs[:12], refs[12:20], refs[20:30]
-    body_a, body_b, start, minv, force, left_a, left_b, sems = refs[30:]
-    id_a, id_b, hot_a, hot_b, own, halo, v_own, m_own, xa, xb = outs
+    sources, kept, outs = refs[:12], refs[12:20], refs[20:29]
+    body_a, body_b, start, minv, force, left, sems = refs[29:]
+    id_a, id_b, hot, own, halo, v_own, m_own, xa, xb = outs
     jac_a, jac_b, precond, bias, mu, stick, act, lam0 = kept
     goals = (body_a, body_b, act, lam0, jac_a, jac_b, start, minv, precond, bias, mu, stick)
     copies = [pltpu.make_async_copy(s, g, sems.at[k]) for k, (s, g) in enumerate(zip(sources, goals))]
@@ -258,17 +262,19 @@
     even = is_even()
     copies[0].wait()
     id_a[...] = table_index(body_a[...])
-    build_onehot(id_a[...], hot_a)
+    build_onehot(id_a[...], hot.at[: hot.shape[0] // 2])
     copies[1].wait()
     id_b[...] = table_index(body_b[...])
-    build_onehot(id_b[...], hot_b)
     for copy in copies[2:6]:
         copy.wait()
     active = act[...].astype(jnp.float32)
     lam = [active * lam0[k] for k in range(ROWS)]
     for k in range(ROWS):
         lam0[k] = lam[k]
-    sums, sums_halo = scatter(lam, jac_a, jac_b, id_a, id_b, hot_a, hot_b, force, left_a, left_b, X_HEADS)
+    sums, sums_halo = scatter(
+        lam, jac_a, jac_b, id_a, id_b, hot, force, left, X_HEADS,
+        between=lambda: build_onehot(id_b[...], hot.at[hot.shape[0] // 2 :]),
+    )
     for copy in copies[6:8]:
         copy.wait()
     v, m = to_tables(start), to_tables(minv)
@@ -331,16 +337,16 @@
             ref[base + d] = value
 
 
-def window_kernel(first, last, jac_a, jac_b, lam, id_a, id_b, hot_a, hot_b, v_own, m_own, own_x, *refs):
+def window_kernel(first, last, jac_a, jac_b, lam, id_a, id_b, hot, v_own, m_own, own_x, *refs):
     own, e_ref, o_ref, out = refs[:4]
     halo, work = (None, refs[4:]) if last else (refs[4], refs[5:])
-    force, left_a, left_b, table, *sem = work
+    force, left, table, *sem = work
     if last:
         copy = pltpu.make_async_copy(lam, out, sem[0])
         copy.start()
     even = is_even()
     values = [lam[k] for k in range(ROWS)]
-    sums, sums_halo = scatter(values, jac_a, jac_b, id_a, id_b, hot_a, hot_b, force, left_a, left_b, REST_HEADS)
+    sums, sums_halo = scatter(values, jac_a, jac_b, id_a, id_b, hot, force, left, REST_HEADS)
     put_dict(own, sums)
     if not last:
         put_dict(halo, sums_halo)
@@ -382,12 +388,12 @@
 
 def middle_kernel(
     first, last, jac_a, jac_b, precond, bias, mu, stick, act, lam_in,
-    id_a, id_b, hot_a, hot_b, own_x, halo_x, own, halo, v_own, m_own, part, ra, rb, qe, qo, *refs,
+    id_a, id_b, hot, own_x, halo_x, own, halo, v_own, m_own, part, ra, rb, qe, qo, *refs,
 ):
     if not first:
         v_halo, m_halo, *refs = refs
-    lam_out, own_out, xa, xb, *made = refs[:-4]
-    table, force, left_a, left_b = refs[-4:]
+    lam_out, own_out, xa, xb, *made = refs[:-3]
+    table, force, left = refs[-3:]
     if first:
         v_halo, m_halo = made[1:]
     even = is_even()
@@ -426,7 +432,7 @@
     lam = [active * normal, active * (raw[1] * scale), active * (raw[2] * scale)]
     for k in range(ROWS):
         lam_out[k] = lam[k]
-    sums, sums_halo = scatter(lam, jac_a, jac_b, id_a, id_b, hot_a, hot_b, force, left_a, left_b, X_HEADS)
+    sums, sums_halo = scatter(lam, jac_a, jac_b, id_a, id_b, hot, force, left, X_HEADS)
     put_dict(own_out, sums)
     if not last:
         put_dict(made[0], sums_halo)
@@ -472,12 +478,11 @@
     vmem = pl.BlockSpec(memory_space=pltpu.VMEM)
     own_t, halo_t = arr((OWN_TILES, 8, lanes), f32), arr((HALO_TILES, 8, lanes), f32)
     lam_t = arr((ROWS, rows, lanes), f32)
-    ids_t, hot_t = arr((rows, lanes), i32), arr((contacts, NBND), bf16)
+    ids_t, hot_t = arr((rows, lanes), i32), arr((2 * contacts, NBND), bf16)
     message = lambda r: arr((r, lanes), f32)
     work = [
         pltpu.VMEM((8 * rows, lanes), f32),
-        pltpu.VMEM((16 * len(REST_HEADS), contacts), bf16),
-        pltpu.VMEM((16 * len(with_halo(REST_HEADS)), contacts), bf16),
+        pltpu.VMEM((16 * len(with_halo(REST_HEADS)), 2 * contacts), bf16),
     ]
     table = [pltpu.VMEM((OWN_TILES + HALO_TILES, 8, lanes), f32)]
 
@@ -509,7 +514,7 @@
     sources = [pltpu.with_memory_space_constraint(a, pltpu.HBM) for a in sources]
     made = call(
         first_kernel,
-        (*map(like, kept), ids_t, ids_t, hot_t, hot_t, own_t, halo_t, own_t, own_t, message(2 * GROUP), message(2 * GROUP)),
+        (*map(like, kept), ids_t, ids_t, hot_t, own_t, halo_t, own_t, own_t, message(2 * GROUP), message(2 * GROUP)),
         [pltpu.VMEM(a.shape, a.dtype) for a in (body_a, body_b, start, minv)]
         + work
         + [pltpu.SemaphoreType.DMA((len(sources),))],
@@ -518,11 +523,10 @@
         space=pltpu.HBM,
     )
     fixed, lam = made[:7], made[7]
-    id_a, id_b, hot_a, hot_b, own_x, halo_x, v_own, m_own, xa, xb = made[8:]
+    id_a, id_b, hot, own_x, halo_x, v_own, m_own, xa, xb = made[8:]
     part_t = arr((2 * DOF, rows, lanes), f32)
     halo_tables = ()
     ids = (id_a, id_b)
-    hots = (hot_a, hot_b)
     for step in range(ITERS):
         first, last = step == 0, step == ITERS - 1
         came_x = along_x(xa, xb)
@@ -530,7 +534,7 @@
         own, ye, yo, part, halo = call(
             lambda *refs, first=first: window_kernel(first, False, *refs),
             (own_t, sent, sent, part_t, halo_t), work + table, "window",
-            *fixed[:2], lam, *ids, *hots, v_own, m_own, own_x,
+            *fixed[:2], lam, *ids, hot, v_own, m_own, own_x,
         )
         came_y = along_y(*came_x, ye, yo)
         part = call(
@@ -541,7 +545,7 @@
         outs = (lam_t, own_t, sent, sent) + (halo_t,) * (3 if first else 0 if last else 1)
         lam, own_x, xa, xb, *made = call(
             lambda *refs, first=first, last=last: middle_kernel(first, last, *refs), outs, table + work, "middle",
-            *fixed, lam, *ids, *hots, own_x, halo_x, own, halo, v_own, m_own, part, *came_x, *came_y, *halo_tables,
+            *fixed, lam, *ids, hot, own_x, halo_x, own, halo, v_own, m_own, part, *came_x, *came_y, *halo_tables,
         )
         if not last:
             halo_x = made[0]
@@ -551,7 +555,7 @@
     own, ye, yo, lam = call(
         lambda *refs: window_kernel(False, True, *refs),
         (own_t, sent, sent, lam_t), work + table + [pltpu.SemaphoreType.DMA], "window",
-        *fixed[:2], lam, *ids, *hots, v_own, m_own, own_x,
+        *fixed[:2], lam, *ids, hot, v_own, m_own, own_x,
         out_spaces=(pltpu.VMEM,) * 3 + (pltpu.HBM,),
     )
     came_y = along_y(*came_x, ye, yo)

time: 39.3 us -> 39 us (level)
  Pallas kernels: 15 us -> 14.6 us
    pallas_call x16, Pallas kernels: 15 us -> 14.6 us  [call(): pl.pallas_call(kernel, out_shape=outs, in_specs=[pl.BlockSpec(memory_spac...]
where the time goes in v6:
time: 39 us; the launch traced here: 38.7 us
  Pallas kernels  14.6 us (37%)
  starting transfers between devices  12.9 us (33%)
  waiting for transfers between devices  10.5 us (27%)
  between operations  0.73 us (2%)
    pallas_call x16, Pallas kernels, call(): pl.pallas_call(kernel, out_shape=outs, in_specs=[pl.BlockSpec(memory_spac...  14.6 us
    ppermute x4, starting transfers between devices, along_x(): lax.ppermute(xa, ('gx', 'gy'), up)  6.81 us
    ppermute x8, starting transfers between devices, along_y(): return (lax.ppermute(ye, 'gy', far), lax.ppermute(yo, 'gy', near))  6.07 us
    ppermute x8, waiting for transfers between devices, along_y(): return (lax.ppermute(ye, 'gy', far), lax.ppermute(yo, 'gy', near))  5.65 us
    ppermute x4, waiting for transfers between devices, along_x(): lax.ppermute(xb, ('gx', 'gy'), down)  4.83 us
  transfers between devices with their start and end apart: 16, of which 8 were waited for; matrix products, arithmetic and copies ran while one was open for 0% of the time, Pallas kernels for 18%

profile of v6, /device:TPU:1, one launch (start us, length us, event | category | flops | bytes accessed | tf_op | source)
XLA Modules:
  0.0 38.7 jit_solution(13483125880058193841)
XLA Ops:
  0.6 2.8 %first.1 = (f32[18,32,128]{2,1,0:T(8,128)S(1)}, f32[18,32,128]{2,1,0:T(8,128)S(1)}, f32[9,32,128]{2,1,0:T(8,128)S(1)}, f32[3,32,128]{2,1,0:T(8,128)S(1)}, f32[32...) custom-call(s32[32,128]{1,0:T(8,128)} %bitcast.24, ...), custom_call_target="tpu_custom_call" | custom-call | tf_op jit(solution)/shard_map/first/pallas_call | solution.py:491
  3.4 2.1 %collective-permute-start = (f32[64,128]{1,0:T(8,128)S(1)}, f32[64,128]{1,0:T(8,128)S(1)}, u32[]{:S(2)}, u32[]{:S(2)}) collective-permute-start(f32[64,128]{1,0:T(8,128)S(1)} %get-tuple-element.80), channel_id=1, source_target_pairs={{0,1},{1,5},{2,3},{3,7},{4,0},{5,9},{6,2},{7,11},{8,4},{9,13},{10,... | collective-permute-start | bytes 98312 | tf_op jit(solution)/shard_map/ppermute | solution.py:504
  5.6 0.0 collective-permute-start.1
  5.6 1.6 %window.4 = (f32[16,8,128]{2,1,0:T(8,128)S(1)}, f32[64,128]{1,0:T(8,128)S(1)}, f32[64,128]{1,0:T(8,128)S(1)}, f32[12,32,128]{2,1,0:T(8,128)S(1)}, f32[9,8,128]{2,1,0:T(8,128)S(1)}) custom-call(f32[18,32,128]{2,1,0:T(8,128)S(1)} %get-tuple-element.62.refs_0_, f32[18,32,128]{2,1,0:T(8,128)S(1)} %get-tuple-element.63.refs_1_, ...), custom_call_target="tpu_custom_call" | custom-call | tf_op jit(solution)/shard_map/window/pallas_call | solution.py:491
  7.1 0.0 collective-permute-done.refs_7_.ra.refs_18_
  7.1 1.2 %collective-permute-done.1.refs_8_.rb.refs_19_ = f32[64,128]{1,0:T(8,128)S(1)} collective-permute-done((f32[64,128]{1,0:T(8,128)S(1)}, f32[64,128]{1,0:T(8,128)S(1)}, u32[]{:S(2)}, u32[]{:S(2)}) %collective-permute-start.1) | collective-permute-done | bytes 32800 | tf_op jit(solution)/shard_map/ppermute | solution.py:504
  8.3 1.9 %collective-permute-start.2 = (f32[64,128]{1,0:T(8,128)S(1)}, f32[64,128]{1,0:T(8,128)S(1)}, u32[]{:S(2)}, u32[]{:S(2)}) collective-permute-start(f32[64,128]{1,0:T(8,128)S(1)} %get-tuple-element.84), channel_id=1, source_target_pairs={{0,3},{1,2},{2,1},{3,0},{4,7},{5,6},{6,5},{7,4},{8,11},{9,10},{10,... | collective-permute-start | bytes 98312 | tf_op jit(solution)/shard_map/ppermute | solution.py:509
  10.2 0.1 collective-permute-start.3
  10.3 0.4 %side.3.refs_17_ = f32[12,32,128]{2,1,0:T(8,128)S(1)} custom-call(f32[16,8,128]{2,1,0:T(8,128)S(1)} %get-tuple-element.73.refs_8_.refs_0_.refs_11_, f32[9,8,128]{2,1,0:T(8,128)S(1)} %get-tuple-element.74.refs_1_.refs_12_, f32[16,8,128]{2,1,0:T(8,128)S(1)} %get-tuple-element.75.refs_6_.refs_2_.refs_15_.v_own, ...), custom_call_target="tpu_custom_call" | custom-call | tf_op jit(solution)/shard_map/side/pallas_call | solution.py:491
  10.7 1.1 %collective-permute-done.2.refs_20_ = f32[64,128]{1,0:T(8,128)S(1)} collective-permute-done((f32[64,128]{1,0:T(8,128)S(1)}, f32[64,128]{1,0:T(8,128)S(1)}, u32[]{:S(2)}, u32[]{:S(2)}) %collective-permute-start.2) | collective-permute-done | bytes 32800 | tf_op jit(solution)/shard_map/ppermute | solution.py:509
  11.8 0.0 collective-permute-done.3.refs_21_
  11.8 1.4 %middle.3 = (f32[3,32,128]{2,1,0:T(8,128)S(1)}, f32[16,8,128]{2,1,0:T(8,128)S(1)}, f32[32,128]{1,0:T(8,128)S(1)}, f32[32,128]{1,0:T(8,128)S(1)}, f32[9,8,128]{2,...) custom-call(f32[18,32,128]{2,1,0:T(8,128)S(1)} %get-tuple-element.62.refs_0_, ...), custom_call_target="tpu_custom_call" | custom-call | tf_op jit(solution)/shard_map/middle/pallas_call | solution.py:491
  13.2 1.6 %collective-permute-start.4 = (f32[32,128]{1,0:T(8,128)S(1)}, f32[32,128]{1,0:T(8,128)S(1)}, u32[]{:S(2)}, u32[]{:S(2)}) collective-permute-start(f32[32,128]{1,0:T(8,128)S(1)} %get-tuple-element.92), channel_id=1, source_target_pairs={{0,1},{1,5},{2,3},{3,7},{4,0},{5,9},{6,2},{7,11},{8,4},{9,13},{10,... | collective-permute-start | bytes 49160 | tf_op jit(solution)/shard_map/ppermute | solution.py:504
  14.8 0.0 collective-permute-start.5
  14.8 1.6 %window.5 = (f32[16,8,128]{2,1,0:T(8,128)S(1)}, f32[32,128]{1,0:T(8,128)S(1)}, f32[32,128]{1,0:T(8,128)S(1)}, f32[12,32,128]{2,1,0:T(8,128)S(1)}, f32[9,8,128]{2,1,0:T(8,128)S(1)}) custom-call(f32[18,32,128]{2,1,0:T(8,128)S(1)} %get-tuple-element.62.refs_0_, f32[18,32,128]{2,1,0:T(8,128)S(1)} %get-tuple-element.63.refs_1_, ...), custom_call_target="tpu_custom_call" | custom-call | tf_op jit(solution)/shard_map/window/pallas_call | solution.py:491
  16.4 0.0 collective-permute-done.4.refs_7_.ra.refs_18_
  16.4 1.2 %collective-permute-done.5.refs_8_.rb.refs_19_ = f32[32,128]{1,0:T(8,128)S(1)} collective-permute-done((f32[32,128]{1,0:T(8,128)S(1)}, f32[32,128]{1,0:T(8,128)S(1)}, u32[]{:S(2)}, u32[]{:S(2)}) %collective-permute-start.5) | collective-permute-done | bytes 16416 | tf_op jit(solution)/shard_map/ppermute | solution.py:504
  17.6 1.2 %collective-permute-start.6 = (f32[32,128]{1,0:T(8,128)S(1)}, f32[32,128]{1,0:T(8,128)S(1)}, u32[]{:S(2)}, u32[]{:S(2)}) collective-permute-start(f32[32,128]{1,0:T(8,128)S(1)} %get-tuple-element.98), channel_id=1, source_target_pairs={{0,3},{1,2},{2,1},{3,0},{4,7},{5,6},{6,5},{7,4},{8,11},{9,10},{10,... | collective-permute-start | bytes 49160 | tf_op jit(solution)/shard_map/ppermute | solution.py:509
  18.9 0.5 %collective-permute-start.7 = (f32[32,128]{1,0:T(8,128)S(1)}, f32[32,128]{1,0:T(8,128)S(1)}, u32[]{:S(2)}, u32[]{:S(2)}) collective-permute-start(f32[32,128]{1,0:T(8,128)S(1)} %get-tuple-element.99), channel_id=1, source_target_pairs={{0,1},{1,0},{2,3},{3,2},{4,5},{5,4},{6,7},{7,6},{8,9},{9,8},{10,11... | collective-permute-start | bytes 49160 | tf_op jit(solution)/shard_map/ppermute | solution.py:509
  19.4 0.4 %side.4.refs_17_ = f32[12,32,128]{2,1,0:T(8,128)S(1)} custom-call(f32[16,8,128]{2,1,0:T(8,128)S(1)} %get-tuple-element.87.refs_8_.refs_0_.refs_11_, f32[9,8,128]{2,1,0:T(8,128)S(1)} %get-tuple-element.88.refs_1_.refs_12_, f32[16,8,128]{2,1,0:T(8,128)S(1)} %get-tuple-element.75.refs_6_.refs_2_.refs_15_.v_own, ...), custom_call_target="tpu_custom_call" | custom-call | tf_op jit(solution)/shard_map/side/pallas_call | solution.py:491
  19.8 1.0 %collective-permute-done.6.refs_20_ = f32[32,128]{1,0:T(8,128)S(1)} collective-permute-done((f32[32,128]{1,0:T(8,128)S(1)}, f32[32,128]{1,0:T(8,128)S(1)}, u32[]{:S(2)}, u32[]{:S(2)}) %collective-permute-start.6) | collective-permute-done | bytes 16416 | tf_op jit(solution)/shard_map/ppermute | solution.py:509
  20.8 0.0 collective-permute-done.7.refs_21_
  20.8 1.4 %middle.4 = (f32[3,32,128]{2,1,0:T(8,128)S(1)}, f32[16,8,128]{2,1,0:T(8,128)S(1)}, f32[32,128]{1,0:T(8,128)S(1)}, f32[32,128]{1,0:T(8,128)S(1)}, f32[9,8,128]{2,1,0:T(8,128)S(1)}) custom-call(f32[18,32,128]{2,1,0:T(8,128)S(1)} %get-tuple-element.62.refs_0_, f32[18,32,128]{2,1,0:T(8,128)S(1)} %get-tuple-element.63.refs_1_, ...), custom_call_target="tpu_custom_call" | custom-call | tf_op jit(solution)/shard_map/middle/pallas_call | solution.py:491
  22.2 1.5 %collective-permute-start.8 = (f32[32,128]{1,0:T(8,128)S(1)}, f32[32,128]{1,0:T(8,128)S(1)}, u32[]{:S(2)}, u32[]{:S(2)}) collective-permute-start(f32[32,128]{1,0:T(8,128)S(1)} %get-tuple-element.106), channel_id=1, source_target_pairs={{0,1},{1,5},{2,3},{3,7},{4,0},{5,9},{6,2},{7,11},{8,4},{9,13},{10,... | collective-permute-start | bytes 49160 | tf_op jit(solution)/shard_map/ppermute | solution.py:504
  23.6 0.0 collective-permute-start.9
  23.6 1.6 %window.6 = (f32[16,8,128]{2,1,0:T(8,128)S(1)}, f32[32,128]{1,0:T(8,128)S(1)}, f32[32,128]{1,0:T(8,128)S(1)}, f32[12,32,128]{2,1,0:T(8,128)S(1)}, f32[9,8,128]{2,1,0:T(8,128)S(1)}) custom-call(f32[18,32,128]{2,1,0:T(8,128)S(1)} %get-tuple-element.62.refs_0_, f32[18,32,128]{2,1,0:T(8,128)S(1)} %get-tuple-element.63.refs_1_, ...), custom_call_target="tpu_custom_call" | custom-call | tf_op jit(solution)/shard_map/window/pallas_call | solution.py:491
  25.2 0.0 collective-permute-done.8.refs_7_.ra.refs_18_
  25.2 1.0 %collective-permute-done.9.refs_8_.rb.refs_19_ = f32[32,128]{1,0:T(8,128)S(1)} collective-permute-done((f32[32,128]{1,0:T(8,128)S(1)}, f32[32,128]{1,0:T(8,128)S(1)}, u32[]{:S(2)}, u32[]{:S(2)}) %collective-permute-start.9) | collective-permute-done | bytes 16416 | tf_op jit(solution)/shard_map/ppermute | solution.py:504
  26.2 1.0 %collective-permute-start.10 = (f32[32,128]{1,0:T(8,128)S(1)}, f32[32,128]{1,0:T(8,128)S(1)}, u32[]{:S(2)}, u32[]{:S(2)}) collective-permute-start(f32[32,128]{1,0:T(8,128)S(1)} %get-tuple-element.110), channel_id=1, source_target_pairs={{0,3},{1,2},{2,1},{3,0},{4,7},{5,6},{6,5},{7,4},{8,11},{9,10},{10,... | collective-permute-start | bytes 49160 | tf_op jit(solution)/shard_map/ppermute | solution.py:509
  27.2 0.6 %collective-permute-start.11 = (f32[32,128]{1,0:T(8,128)S(1)}, f32[32,128]{1,0:T(8,128)S(1)}, u32[]{:S(2)}, u32[]{:S(2)}) collective-permute-start(f32[32,128]{1,0:T(8,128)S(1)} %get-tuple-element.111), channel_id=1, source_target_pairs={{0,1},{1,0},{2,3},{3,2},{4,5},{5,4},{6,7},{7,6},{8,9},{9,8},{10,11... | collective-permute-start | bytes 49160 | tf_op jit(solution)/shard_map/ppermute | solution.py:509
  27.8 0.4 %side.5.refs_17_ = f32[12,32,128]{2,1,0:T(8,128)S(1)} custom-call(f32[16,8,128]{2,1,0:T(8,128)S(1)} %get-tuple-element.101.refs_8_.refs_0_.refs_11_, f32[9,8,128]{2,1,0:T(8,128)S(1)} %get-tuple-element.102.refs_1_.refs_12_, f32[16,8,128]{2,1,0:T(8,128)S(1)} %get-tuple-element.75.refs_6_.refs_2_.refs_15_.v_own, ...), custom_call_target="tpu_custom_call" | custom-call | tf_op jit(solution)/shard_map/side/pallas_call | solution.py:491
  28.2 1.1 %collective-permute-done.10.refs_20_ = f32[32,128]{1,0:T(8,128)S(1)} collective-permute-done((f32[32,128]{1,0:T(8,128)S(1)}, f32[32,128]{1,0:T(8,128)S(1)}, u32[]{:S(2)}, u32[]{:S(2)}) %collective-permute-start.10) | collective-permute-done | bytes 16416 | tf_op jit(solution)/shard_map/ppermute | solution.py:509
  29.4 0.0 collective-permute-done.11.refs_21_
  29.4 1.4 %middle.5 = (f32[3,32,128]{2,1,0:T(8,128)S(1)}, f32[16,8,128]{2,1,0:T(8,128)S(1)}, f32[24,128]{1,0:T(8,128)S(1)}, f32[24,128]{1,0:T(8,128)S(1)}) custom-call(f32[18,32,128]{2,1,0:T(8,128)S(1)} %get-tuple-element.62.refs_0_, f32[18,32,128]{2,1,0:T(8,128)S(1)} %get-tuple-element.63.refs_1_, f32[9,32,128]{2,1,0:T(8,128)S(1)} %get-tuple-element.64.refs_2_, ...), custom_call_target="tpu_custom_call" | custom-call | tf_op jit(solution)/shard_map/middle/pallas_call | solution.py:491
  30.8 1.6 %collective-permute-start.12 = (f32[24,128]{1,0:T(8,128)S(1)}, f32[24,128]{1,0:T(8,128)S(1)}, u32[]{:S(2)}, u32[]{:S(2)}) collective-permute-start(f32[24,128]{1,0:T(8,128)S(1)} %get-tuple-element.116), channel_id=1, source_target_pairs={{0,1},{1,5},{2,3},{3,7},{4,0},{5,9},{6,2},{7,11},{8,4},{9,13},{10,... | collective-permute-start | bytes 36872 | tf_op jit(solution)/shard_map/ppermute | solution.py:504
  32.4 0.0 collective-permute-start.13
  32.4 1.1 %window.7 = (f32[16,8,128]{2,1,0:T(8,128)S(1)}, f32[24,128]{1,0:T(8,128)S(1)}, f32[24,128]{1,0:T(8,128)S(1)}, f32[3,32,128]{2,1,0:T(8,128)}) custom-call(f32[18,32,128]{2,1,0:T(8,128)S(1)} %get-tuple-element.62.refs_0_, f32[18,32,128]{2,1,0:T(8,128)S(1)} %get-tuple-element.63.refs_1_, f32[3,32,128]{2,1,0:T(8,128)S(1)} %get-tuple-element.112.refs_2_, ...), custom_call_target="tpu_custom_call" | custom-call | tf_op jit(solution)/shard_map/window/pallas_call | solution.py:491
  33.5 0.0 collective-permute-done.12.ra
  33.5 1.4 %collective-permute-done.13.rb = f32[24,128]{1,0:T(8,128)S(1)} collective-permute-done((f32[24,128]{1,0:T(8,128)S(1)}, f32[24,128]{1,0:T(8,128)S(1)}, u32[]{:S(2)}, u32[]{:S(2)}) %collective-permute-start.13) | collective-permute-done | bytes 12320 | tf_op jit(solution)/shard_map/ppermute | solution.py:504
  34.9 0.6 %collective-permute-start.14 = (f32[24,128]{1,0:T(8,128)S(1)}, f32[24,128]{1,0:T(8,128)S(1)}, u32[]{:S(2)}, u32[]{:S(2)}) collective-permute-start(f32[24,128]{1,0:T(8,128)S(1)} %get-tuple-element.120), channel_id=1, source_target_pairs={{0,3},{1,2},{2,1},{3,0},{4,7},{5,6},{6,5},{7,4},{8,11},{9,10},{10,... | collective-permute-start | bytes 36872 | tf_op jit(solution)/shard_map/ppermute | solution.py:509
  35.6 0.0 collective-permute-start.15
  35.6 2.4 %collective-permute-done.14.qe = f32[24,128]{1,0:T(8,128)S(1)} collective-permute-done((f32[24,128]{1,0:T(8,128)S(1)}, f32[24,128]{1,0:T(8,128)S(1)}, u32[]{:S(2)}, u32[]{:S(2)}) %collective-permute-start.14) | collective-permute-done | bytes 12320 | tf_op jit(solution)/shard_map/ppermute | solution.py:509
  38.0 0.0 collective-permute-done.15.qo
  38.0 0.7 %last.1 = f32[96,128]{1,0:T(8,128)} custom-call(f32[16,8,128]{2,1,0:T(8,128)S(1)} %get-tuple-element.113.refs_8_.own_x, f32[16,8,128]{2,1,0:T(8,128)S(1)} %get-tuple-element.115.own, f32[16,8,128]{2,1,0:T(8,128)S(1)} %get-tuple-element.75.refs_6_.refs_2_.refs_15_.v_own, f32[16,8,128]{2,1,0:T(8,128)S(1)} %get-tuple-element.76.refs_7_.refs_3_.refs_16_.m_own, ...), custom_call_target="tpu_custom_call" | custom-call | tf_op jit(solution)/shard_map/last/pallas_call | solution.py:491
  (4 shorter events, 0.0 us)
Async XLA Ops:
  3.4 3.7 %collective-permute-start = (f32[64,128]{1,0:T(8,128)S(1)}, f32[64,128]{1,0:T(8,128)S(1)}, u32[]{:S(2)}, u32[]{:S(2)}) collective-permute-start(f32[64,128]{1,0:T(8,128)S(1)} %get-tuple-element.80), channel_id=1, source_target_pairs={{0,1},{1,5},{2,3},{3,7},{4,0},{5,9},{6,2},{7,11},{8,4},{9,13},{10,... | collective-permute-start | bytes 98312 | tf_op jit(solution)/shard_map/ppermute | solution.py:504
  5.6 2.8 %collective-permute-start.1 = (f32[64,128]{1,0:T(8,128)S(1)}, f32[64,128]{1,0:T(8,128)S(1)}, u32[]{:S(2)}, u32[]{:S(2)}) collective-permute-start(f32[64,128]{1,0:T(8,128)S(1)} %get-tuple-element.81), channel_id=1, source_target_pairs={{1,0},{5,1},{3,2},{7,3},{0,4},{9,5},{2,6},{11,7},{4,8},{13,9},{6,1... | collective-permute-start | bytes 98312 | tf_op jit(solution)/shard_map/ppermute | solution.py:504
  8.3 3.5 %collective-permute-start.2 = (f32[64,128]{1,0:T(8,128)S(1)}, f32[64,128]{1,0:T(8,128)S(1)}, u32[]{:S(2)}, u32[]{:S(2)}) collective-permute-start(f32[64,128]{1,0:T(8,128)S(1)} %get-tuple-element.84), channel_id=1, source_target_pairs={{0,3},{1,2},{2,1},{3,0},{4,7},{5,6},{6,5},{7,4},{8,11},{9,10},{10,... | collective-permute-start | bytes 98312 | tf_op jit(solution)/shard_map/ppermute | solution.py:509
  10.2 1.6 %collective-permute-start.3 = (f32[64,128]{1,0:T(8,128)S(1)}, f32[64,128]{1,0:T(8,128)S(1)}, u32[]{:S(2)}, u32[]{:S(2)}) collective-permute-start(f32[64,128]{1,0:T(8,128)S(1)} %get-tuple-element.85), channel_id=1, source_target_pairs={{0,1},{1,0},{2,3},{3,2},{4,5},{5,4},{6,7},{7,6},{8,9},{9,8},{10,11... | collective-permute-start | bytes 98312 | tf_op jit(solution)/shard_map/ppermute | solution.py:509
  13.2 3.2 %collective-permute-start.4 = (f32[32,128]{1,0:T(8,128)S(1)}, f32[32,128]{1,0:T(8,128)S(1)}, u32[]{:S(2)}, u32[]{:S(2)}) collective-permute-start(f32[32,128]{1,0:T(8,128)S(1)} %get-tuple-element.92), channel_id=1, source_target_pairs={{0,1},{1,5},{2,3},{3,7},{4,0},{5,9},{6,2},{7,11},{8,4},{9,13},{10,... | collective-permute-start | bytes 49160 | tf_op jit(solution)/shard_map/ppermute | solution.py:504
  14.8 2.8 %collective-permute-start.5 = (f32[32,128]{1,0:T(8,128)S(1)}, f32[32,128]{1,0:T(8,128)S(1)}, u32[]{:S(2)}, u32[]{:S(2)}) collective-permute-start(f32[32,128]{1,0:T(8,128)S(1)} %get-tuple-element.93), channel_id=1, source_target_pairs={{1,0},{5,1},{3,2},{7,3},{0,4},{9,5},{2,6},{11,7},{4,8},{13,9},{6,1... | collective-permute-start | bytes 49160 | tf_op jit(solution)/shard_map/ppermute | solution.py:504
  17.6 3.2 %collective-permute-start.6 = (f32[32,128]{1,0:T(8,128)S(1)}, f32[32,128]{1,0:T(8,128)S(1)}, u32[]{:S(2)}, u32[]{:S(2)}) collective-permute-start(f32[32,128]{1,0:T(8,128)S(1)} %get-tuple-element.98), channel_id=1, source_target_pairs={{0,3},{1,2},{2,1},{3,0},{4,7},{5,6},{6,5},{7,4},{8,11},{9,10},{10,... | collective-permute-start | bytes 49160 | tf_op jit(solution)/shard_map/ppermute | solution.py:509
  18.9 1.9 %collective-permute-start.7 = (f32[32,128]{1,0:T(8,128)S(1)}, f32[32,128]{1,0:T(8,128)S(1)}, u32[]{:S(2)}, u32[]{:S(2)}) collective-permute-start(f32[32,128]{1,0:T(8,128)S(1)} %get-tuple-element.99), channel_id=1, source_target_pairs={{0,1},{1,0},{2,3},{3,2},{4,5},{5,4},{6,7},{7,6},{8,9},{9,8},{10,11... | collective-permute-start | bytes 49160 | tf_op jit(solution)/shard_map/ppermute | solution.py:509
  22.2 3.0 %collective-permute-start.8 = (f32[32,128]{1,0:T(8,128)S(1)}, f32[32,128]{1,0:T(8,128)S(1)}, u32[]{:S(2)}, u32[]{:S(2)}) collective-permute-start(f32[32,128]{1,0:T(8,128)S(1)} %get-tuple-element.106), channel_id=1, source_target_pairs={{0,1},{1,5},{2,3},{3,7},{4,0},{5,9},{6,2},{7,11},{8,4},{9,13},{10,... | collective-permute-start | bytes 49160 | tf_op jit(solution)/shard_map/ppermute | solution.py:504
  23.6 2.6 %collective-permute-start.9 = (f32[32,128]{1,0:T(8,128)S(1)}, f32[32,128]{1,0:T(8,128)S(1)}, u32[]{:S(2)}, u32[]{:S(2)}) collective-permute-start(f32[32,128]{1,0:T(8,128)S(1)} %get-tuple-element.107), channel_id=1, source_target_pairs={{1,0},{5,1},{3,2},{7,3},{0,4},{9,5},{2,6},{11,7},{4,8},{13,9},{6,1... | collective-permute-start | bytes 49160 | tf_op jit(solution)/shard_map/ppermute | solution.py:504
  26.2 3.2 %collective-permute-start.10 = (f32[32,128]{1,0:T(8,128)S(1)}, f32[32,128]{1,0:T(8,128)S(1)}, u32[]{:S(2)}, u32[]{:S(2)}) collective-permute-start(f32[32,128]{1,0:T(8,128)S(1)} %get-tuple-element.110), channel_id=1, source_target_pairs={{0,3},{1,2},{2,1},{3,0},{4,7},{5,6},{6,5},{7,4},{8,11},{9,10},{10,... | collective-permute-start | bytes 49160 | tf_op jit(solution)/shard_map/ppermute | solution.py:509
  27.2 2.2 %collective-permute-start.11 = (f32[32,128]{1,0:T(8,128)S(1)}, f32[32,128]{1,0:T(8,128)S(1)}, u32[]{:S(2)}, u32[]{:S(2)}) collective-permute-start(f32[32,128]{1,0:T(8,128)S(1)} %get-tuple-element.111), channel_id=1, source_target_pairs={{0,1},{1,0},{2,3},{3,2},{4,5},{5,4},{6,7},{7,6},{8,9},{9,8},{10,11... | collective-permute-start | bytes 49160 | tf_op jit(solution)/shard_map/ppermute | solution.py:509
  30.8 2.7 %collective-permute-start.12 = (f32[24,128]{1,0:T(8,128)S(1)}, f32[24,128]{1,0:T(8,128)S(1)}, u32[]{:S(2)}, u32[]{:S(2)}) collective-permute-start(f32[24,128]{1,0:T(8,128)S(1)} %get-tuple-element.116), channel_id=1, source_target_pairs={{0,1},{1,5},{2,3},{3,7},{4,0},{5,9},{6,2},{7,11},{8,4},{9,13},{10,... | collective-permute-start | bytes 36872 | tf_op jit(solution)/shard_map/ppermute | solution.py:504
  32.4 2.5 %collective-permute-start.13 = (f32[24,128]{1,0:T(8,128)S(1)}, f32[24,128]{1,0:T(8,128)S(1)}, u32[]{:S(2)}, u32[]{:S(2)}) collective-permute-start(f32[24,128]{1,0:T(8,128)S(1)} %get-tuple-element.117), channel_id=1, source_target_pairs={{1,0},{5,1},{3,2},{7,3},{0,4},{9,5},{2,6},{11,7},{4,8},{13,9},{6,1... | collective-permute-start | bytes 36872 | tf_op jit(solution)/shard_map/ppermute | solution.py:504
  34.9 3.1 %collective-permute-start.14 = (f32[24,128]{1,0:T(8,128)S(1)}, f32[24,128]{1,0:T(8,128)S(1)}, u32[]{:S(2)}, u32[]{:S(2)}) collective-permute-start(f32[24,128]{1,0:T(8,128)S(1)} %get-tuple-element.120), channel_id=1, source_target_pairs={{0,3},{1,2},{2,1},{3,0},{4,7},{5,6},{6,5},{7,4},{8,11},{9,10},{10,... | collective-permute-start | bytes 36872 | tf_op jit(solution)/shard_map/ppermute | solution.py:509
  35.6 2.5 %collective-permute-start.15 = (f32[24,128]{1,0:T(8,128)S(1)}, f32[24,128]{1,0:T(8,128)S(1)}, u32[]{:S(2)}, u32[]{:S(2)}) collective-permute-start(f32[24,128]{1,0:T(8,128)S(1)} %get-tuple-element.121), channel_id=1, source_target_pairs={{0,1},{1,0},{2,3},{3,2},{4,5},{5,4},{6,7},{7,6},{8,9},{9,8},{10,11... | collective-permute-start | bytes 36872 | tf_op jit(solution)/shard_map/ppermute | solution.py:509

commit v7 on v6

--- a/solution.py
+++ b/solution.py
@@ -271,15 +271,18 @@
     lam = [active * lam0[k] for k in range(ROWS)]
     for k in range(ROWS):
         lam0[k] = lam[k]
-    sums, sums_halo = scatter(
-        lam, jac_a, jac_b, id_a, id_b, hot, force, left, X_HEADS,
-        between=lambda: build_onehot(id_b[...], hot.at[hot.shape[0] // 2 :]),
-    )
+    v, m = [], []
+
+    def between():
+        build_onehot(id_b[...], hot.at[hot.shape[0] // 2 :])
+        v.extend(to_tables(start))
+        m.extend(to_tables(minv))
+        for t in range(OWN_TILES):
+            v_own[t], m_own[t] = v[t], m[t]
+
     for copy in copies[6:8]:
         copy.wait()
-    v, m = to_tables(start), to_tables(minv)
-    for t in range(OWN_TILES):
-        v_own[t], m_own[t] = v[t], m[t]
+    sums, sums_halo = scatter(lam, jac_a, jac_b, id_a, id_b, hot, force, left, X_HEADS, between)
     put_dict(own, sums)
     put_dict(halo, sums_halo)
     put_x(even, [(sums, sums_halo), (dict(enumerate(v)), dict(enumerate(m)))], xa, xb)

time: 39 us -> 38.9 us (level)
  no operation moved by 1% of the time
where the time goes in v7:
time: 38.9 us; the launch traced here: 38.7 us
  Pallas kernels  14.6 us (38%)
  starting transfers between devices  12.9 us (33%)
  waiting for transfers between devices  10.5 us (27%)
  between operations  0.73 us (2%)
    pallas_call x16, Pallas kernels, call(): pl.pallas_call(kernel, out_shape=outs, in_specs=[pl.BlockSpec(memory_spac...  14.6 us
    ppermute x4, starting transfers between devices, along_x(): lax.ppermute(xa, ('gx', 'gy'), up)  6.81 us
    ppermute x8, starting transfers between devices, along_y(): return (lax.ppermute(ye, 'gy', far), lax.ppermute(yo, 'gy', near))  6.06 us
    ppermute x8, waiting for transfers between devices, along_y(): return (lax.ppermute(ye, 'gy', far), lax.ppermute(yo, 'gy', near))  5.65 us
    ppermute x4, waiting for transfers between devices, along_x(): lax.ppermute(xb, ('gx', 'gy'), down)  4.83 us
  transfers between devices with their start and end apart: 16, of which 8 were waited for; matrix products, arithmetic and copies ran while one was open for 0% of the time, Pallas kernels for 18%

profile of v7, /device:TPU:1, one launch (start us, length us, event | category | flops | bytes accessed | tf_op | source)
XLA Modules:
  0.0 38.7 jit_solution(8449655468230372435)
XLA Ops:
  0.6 2.7 %first.1 = (f32[18,32,128]{2,1,0:T(8,128)S(1)}, f32[18,32,128]{2,1,0:T(8,128)S(1)}, f32[9,32,128]{2,1,0:T(8,128)S(1)}, f32[3,32,128]{2,1,0:T(8,128)S(1)}, f32[32...) custom-call(s32[32,128]{1,0:T(8,128)} %bitcast.24, ...), custom_call_target="tpu_custom_call" | custom-call | tf_op jit(solution)/shard_map/first/pallas_call | solution.py:494
  3.4 2.1 %collective-permute-start = (f32[64,128]{1,0:T(8,128)S(1)}, f32[64,128]{1,0:T(8,128)S(1)}, u32[]{:S(2)}, u32[]{:S(2)}) collective-permute-start(f32[64,128]{1,0:T(8,128)S(1)} %get-tuple-element.80), channel_id=1, source_target_pairs={{0,1},{1,5},{2,3},{3,7},{4,0},{5,9},{6,2},{7,11},{8,4},{9,13},{10,... | collective-permute-start | bytes 98312 | tf_op jit(solution)/shard_map/ppermute | solution.py:507
  5.5 0.0 collective-permute-start.1
  5.5 1.6 %window.4 = (f32[16,8,128]{2,1,0:T(8,128)S(1)}, f32[64,128]{1,0:T(8,128)S(1)}, f32[64,128]{1,0:T(8,128)S(1)}, f32[12,32,128]{2,1,0:T(8,128)S(1)}, f32[9,8,128]{2,1,0:T(8,128)S(1)}) custom-call(f32[18,32,128]{2,1,0:T(8,128)S(1)} %get-tuple-element.62.refs_0_, f32[18,32,128]{2,1,0:T(8,128)S(1)} %get-tuple-element.63.refs_1_, ...), custom_call_target="tpu_custom_call" | custom-call | tf_op jit(solution)/shard_map/window/pallas_call | solution.py:494
  7.1 0.0 collective-permute-done.refs_7_.ra.refs_18_
  7.1 1.2 %collective-permute-done.1.refs_8_.rb.refs_19_ = f32[64,128]{1,0:T(8,128)S(1)} collective-permute-done((f32[64,128]{1,0:T(8,128)S(1)}, f32[64,128]{1,0:T(8,128)S(1)}, u32[]{:S(2)}, u32[]{:S(2)}) %collective-permute-start.1) | collective-permute-done | bytes 32800 | tf_op jit(solution)/shard_map/ppermute | solution.py:507
  8.3 1.9 %collective-permute-start.2 = (f32[64,128]{1,0:T(8,128)S(1)}, f32[64,128]{1,0:T(8,128)S(1)}, u32[]{:S(2)}, u32[]{:S(2)}) collective-permute-start(f32[64,128]{1,0:T(8,128)S(1)} %get-tuple-element.84), channel_id=1, source_target_pairs={{0,3},{1,2},{2,1},{3,0},{4,7},{5,6},{6,5},{7,4},{8,11},{9,10},{10,... | collective-permute-start | bytes 98312 | tf_op jit(solution)/shard_map/ppermute | solution.py:512
  10.2 0.1 collective-permute-start.3
  10.3 0.4 %side.3.refs_17_ = f32[12,32,128]{2,1,0:T(8,128)S(1)} custom-call(f32[16,8,128]{2,1,0:T(8,128)S(1)} %get-tuple-element.73.refs_8_.refs_0_.refs_11_, f32[9,8,128]{2,1,0:T(8,128)S(1)} %get-tuple-element.74.refs_1_.refs_12_, f32[16,8,128]{2,1,0:T(8,128)S(1)} %get-tuple-element.75.refs_6_.refs_2_.refs_15_.v_own, ...), custom_call_target="tpu_custom_call" | custom-call | tf_op jit(solution)/shard_map/side/pallas_call | solution.py:494
  10.7 1.1 %collective-permute-done.2.refs_20_ = f32[64,128]{1,0:T(8,128)S(1)} collective-permute-done((f32[64,128]{1,0:T(8,128)S(1)}, f32[64,128]{1,0:T(8,128)S(1)}, u32[]{:S(2)}, u32[]{:S(2)}) %collective-permute-start.2) | collective-permute-done | bytes 32800 | tf_op jit(solution)/shard_map/ppermute | solution.py:512
  11.8 0.0 collective-permute-done.3.refs_21_
  11.8 1.4 %middle.3 = (f32[3,32,128]{2,1,0:T(8,128)S(1)}, f32[16,8,128]{2,1,0:T(8,128)S(1)}, f32[32,128]{1,0:T(8,128)S(1)}, f32[32,128]{1,0:T(8,128)S(1)}, f32[9,8,128]{2,...) custom-call(f32[18,32,128]{2,1,0:T(8,128)S(1)} %get-tuple-element.62.refs_0_, ...), custom_call_target="tpu_custom_call" | custom-call | tf_op jit(solution)/shard_map/middle/pallas_call | solution.py:494
  13.2 1.6 %collective-permute-start.4 = (f32[32,128]{1,0:T(8,128)S(1)}, f32[32,128]{1,0:T(8,128)S(1)}, u32[]{:S(2)}, u32[]{:S(2)}) collective-permute-start(f32[32,128]{1,0:T(8,128)S(1)} %get-tuple-element.92), channel_id=1, source_target_pairs={{0,1},{1,5},{2,3},{3,7},{4,0},{5,9},{6,2},{7,11},{8,4},{9,13},{10,... | collective-permute-start | bytes 49160 | tf_op jit(solution)/shard_map/ppermute | solution.py:507
  14.8 0.0 collective-permute-start.5
  14.8 1.6 %window.5 = (f32[16,8,128]{2,1,0:T(8,128)S(1)}, f32[32,128]{1,0:T(8,128)S(1)}, f32[32,128]{1,0:T(8,128)S(1)}, f32[12,32,128]{2,1,0:T(8,128)S(1)}, f32[9,8,128]{2,1,0:T(8,128)S(1)}) custom-call(f32[18,32,128]{2,1,0:T(8,128)S(1)} %get-tuple-element.62.refs_0_, f32[18,32,128]{2,1,0:T(8,128)S(1)} %get-tuple-element.63.refs_1_, ...), custom_call_target="tpu_custom_call" | custom-call | tf_op jit(solution)/shard_map/window/pallas_call | solution.py:494
  16.4 0.0 collective-permute-done.4.refs_7_.ra.refs_18_
  16.4 1.2 %collective-permute-done.5.refs_8_.rb.refs_19_ = f32[32,128]{1,0:T(8,128)S(1)} collective-permute-done((f32[32,128]{1,0:T(8,128)S(1)}, f32[32,128]{1,0:T(8,128)S(1)}, u32[]{:S(2)}, u32[]{:S(2)}) %collective-permute-start.5) | collective-permute-done | bytes 16416 | tf_op jit(solution)/shard_map/ppermute | solution.py:507
  17.6 1.2 %collective-permute-start.6 = (f32[32,128]{1,0:T(8,128)S(1)}, f32[32,128]{1,0:T(8,128)S(1)}, u32[]{:S(2)}, u32[]{:S(2)}) collective-permute-start(f32[32,128]{1,0:T(8,128)S(1)} %get-tuple-element.98), channel_id=1, source_target_pairs={{0,3},{1,2},{2,1},{3,0},{4,7},{5,6},{6,5},{7,4},{8,11},{9,10},{10,... | collective-permute-start | bytes 49160 | tf_op jit(solution)/shard_map/ppermute | solution.py:512
  18.8 0.5 %collective-permute-start.7 = (f32[32,128]{1,0:T(8,128)S(1)}, f32[32,128]{1,0:T(8,128)S(1)}, u32[]{:S(2)}, u32[]{:S(2)}) collective-permute-start(f32[32,128]{1,0:T(8,128)S(1)} %get-tuple-element.99), channel_id=1, source_target_pairs={{0,1},{1,0},{2,3},{3,2},{4,5},{5,4},{6,7},{7,6},{8,9},{9,8},{10,11... | collective-permute-start | bytes 49160 | tf_op jit(solution)/shard_map/ppermute | solution.py:512
  19.3 0.4 %side.4.refs_17_ = f32[12,32,128]{2,1,0:T(8,128)S(1)} custom-call(f32[16,8,128]{2,1,0:T(8,128)S(1)} %get-tuple-element.87.refs_8_.refs_0_.refs_11_, f32[9,8,128]{2,1,0:T(8,128)S(1)} %get-tuple-element.88.refs_1_.refs_12_, f32[16,8,128]{2,1,0:T(8,128)S(1)} %get-tuple-element.75.refs_6_.refs_2_.refs_15_.v_own, ...), custom_call_target="tpu_custom_call" | custom-call | tf_op jit(solution)/shard_map/side/pallas_call | solution.py:494
  19.8 1.0 %collective-permute-done.6.refs_20_ = f32[32,128]{1,0:T(8,128)S(1)} collective-permute-done((f32[32,128]{1,0:T(8,128)S(1)}, f32[32,128]{1,0:T(8,128)S(1)}, u32[]{:S(2)}, u32[]{:S(2)}) %collective-permute-start.6) | collective-permute-done | bytes 16416 | tf_op jit(solution)/shard_map/ppermute | solution.py:512
  20.7 0.0 collective-permute-done.7.refs_21_
  20.7 1.4 %middle.4 = (f32[3,32,128]{2,1,0:T(8,128)S(1)}, f32[16,8,128]{2,1,0:T(8,128)S(1)}, f32[32,128]{1,0:T(8,128)S(1)}, f32[32,128]{1,0:T(8,128)S(1)}, f32[9,8,128]{2,1,0:T(8,128)S(1)}) custom-call(f32[18,32,128]{2,1,0:T(8,128)S(1)} %get-tuple-element.62.refs_0_, f32[18,32,128]{2,1,0:T(8,128)S(1)} %get-tuple-element.63.refs_1_, ...), custom_call_target="tpu_custom_call" | custom-call | tf_op jit(solution)/shard_map/middle/pallas_call | solution.py:494
  22.1 1.5 %collective-permute-start.8 = (f32[32,128]{1,0:T(8,128)S(1)}, f32[32,128]{1,0:T(8,128)S(1)}, u32[]{:S(2)}, u32[]{:S(2)}) collective-permute-start(f32[32,128]{1,0:T(8,128)S(1)} %get-tuple-element.106), channel_id=1, source_target_pairs={{0,1},{1,5},{2,3},{3,7},{4,0},{5,9},{6,2},{7,11},{8,4},{9,13},{10,... | collective-permute-start | bytes 49160 | tf_op jit(solution)/shard_map/ppermute | solution.py:507
  23.6 0.0 collective-permute-start.9
  23.6 1.6 %window.6 = (f32[16,8,128]{2,1,0:T(8,128)S(1)}, f32[32,128]{1,0:T(8,128)S(1)}, f32[32,128]{1,0:T(8,128)S(1)}, f32[12,32,128]{2,1,0:T(8,128)S(1)}, f32[9,8,128]{2,1,0:T(8,128)S(1)}) custom-call(f32[18,32,128]{2,1,0:T(8,128)S(1)} %get-tuple-element.62.refs_0_, f32[18,32,128]{2,1,0:T(8,128)S(1)} %get-tuple-element.63.refs_1_, ...), custom_call_target="tpu_custom_call" | custom-call | tf_op jit(solution)/shard_map/window/pallas_call | solution.py:494
  25.2 0.0 collective-permute-done.8.refs_7_.ra.refs_18_
  25.2 1.0 %collective-permute-done.9.refs_8_.rb.refs_19_ = f32[32,128]{1,0:T(8,128)S(1)} collective-permute-done((f32[32,128]{1,0:T(8,128)S(1)}, f32[32,128]{1,0:T(8,128)S(1)}, u32[]{:S(2)}, u32[]{:S(2)}) %collective-permute-start.9) | collective-permute-done | bytes 16416 | tf_op jit(solution)/shard_map/ppermute | solution.py:507
  26.2 1.0 %collective-permute-start.10 = (f32[32,128]{1,0:T(8,128)S(1)}, f32[32,128]{1,0:T(8,128)S(1)}, u32[]{:S(2)}, u32[]{:S(2)}) collective-permute-start(f32[32,128]{1,0:T(8,128)S(1)} %get-tuple-element.110), channel_id=1, source_target_pairs={{0,3},{1,2},{2,1},{3,0},{4,7},{5,6},{6,5},{7,4},{8,11},{9,10},{10,... | collective-permute-start | bytes 49160 | tf_op jit(solution)/shard_map/ppermute | solution.py:512
  27.2 0.6 %collective-permute-start.11 = (f32[32,128]{1,0:T(8,128)S(1)}, f32[32,128]{1,0:T(8,128)S(1)}, u32[]{:S(2)}, u32[]{:S(2)}) collective-permute-start(f32[32,128]{1,0:T(8,128)S(1)} %get-tuple-element.111), channel_id=1, source_target_pairs={{0,1},{1,0},{2,3},{3,2},{4,5},{5,4},{6,7},{7,6},{8,9},{9,8},{10,11... | collective-permute-start | bytes 49160 | tf_op jit(solution)/shard_map/ppermute | solution.py:512
  27.8 0.4 %side.5.refs_17_ = f32[12,32,128]{2,1,0:T(8,128)S(1)} custom-call(f32[16,8,128]{2,1,0:T(8,128)S(1)} %get-tuple-element.101.refs_8_.refs_0_.refs_11_, f32[9,8,128]{2,1,0:T(8,128)S(1)} %get-tuple-element.102.refs_1_.refs_12_, f32[16,8,128]{2,1,0:T(8,128)S(1)} %get-tuple-element.75.refs_6_.refs_2_.refs_15_.v_own, ...), custom_call_target="tpu_custom_call" | custom-call | tf_op jit(solution)/shard_map/side/pallas_call | solution.py:494
  28.2 1.1 %collective-permute-done.10.refs_20_ = f32[32,128]{1,0:T(8,128)S(1)} collective-permute-done((f32[32,128]{1,0:T(8,128)S(1)}, f32[32,128]{1,0:T(8,128)S(1)}, u32[]{:S(2)}, u32[]{:S(2)}) %collective-permute-start.10) | collective-permute-done | bytes 16416 | tf_op jit(solution)/shard_map/ppermute | solution.py:512
  29.4 0.0 collective-permute-done.11.refs_21_
  29.4 1.4 %middle.5 = (f32[3,32,128]{2,1,0:T(8,128)S(1)}, f32[16,8,128]{2,1,0:T(8,128)S(1)}, f32[24,128]{1,0:T(8,128)S(1)}, f32[24,128]{1,0:T(8,128)S(1)}) custom-call(f32[18,32,128]{2,1,0:T(8,128)S(1)} %get-tuple-element.62.refs_0_, f32[18,32,128]{2,1,0:T(8,128)S(1)} %get-tuple-element.63.refs_1_, f32[9,32,128]{2,1,0:T(8,128)S(1)} %get-tuple-element.64.refs_2_, ...), custom_call_target="tpu_custom_call" | custom-call | tf_op jit(solution)/shard_map/middle/pallas_call | solution.py:494
  30.7 1.6 %collective-permute-start.12 = (f32[24,128]{1,0:T(8,128)S(1)}, f32[24,128]{1,0:T(8,128)S(1)}, u32[]{:S(2)}, u32[]{:S(2)}) collective-permute-start(f32[24,128]{1,0:T(8,128)S(1)} %get-tuple-element.116), channel_id=1, source_target_pairs={{0,1},{1,5},{2,3},{3,7},{4,0},{5,9},{6,2},{7,11},{8,4},{9,13},{10,... | collective-permute-start | bytes 36872 | tf_op jit(solution)/shard_map/ppermute | solution.py:507
  32.3 0.0 collective-permute-start.13
  32.3 1.1 %window.7 = (f32[16,8,128]{2,1,0:T(8,128)S(1)}, f32[24,128]{1,0:T(8,128)S(1)}, f32[24,128]{1,0:T(8,128)S(1)}, f32[3,32,128]{2,1,0:T(8,128)}) custom-call(f32[18,32,128]{2,1,0:T(8,128)S(1)} %get-tuple-element.62.refs_0_, f32[18,32,128]{2,1,0:T(8,128)S(1)} %get-tuple-element.63.refs_1_, f32[3,32,128]{2,1,0:T(8,128)S(1)} %get-tuple-element.112.refs_2_, ...), custom_call_target="tpu_custom_call" | custom-call | tf_op jit(solution)/shard_map/window/pallas_call | solution.py:494
  33.4 0.0 collective-permute-done.12.ra
  33.4 1.4 %collective-permute-done.13.rb = f32[24,128]{1,0:T(8,128)S(1)} collective-permute-done((f32[24,128]{1,0:T(8,128)S(1)}, f32[24,128]{1,0:T(8,128)S(1)}, u32[]{:S(2)}, u32[]{:S(2)}) %collective-permute-start.13) | collective-permute-done | bytes 12320 | tf_op jit(solution)/shard_map/ppermute | solution.py:507
  34.9 0.7 %collective-permute-start.14 = (f32[24,128]{1,0:T(8,128)S(1)}, f32[24,128]{1,0:T(8,128)S(1)}, u32[]{:S(2)}, u32[]{:S(2)}) collective-permute-start(f32[24,128]{1,0:T(8,128)S(1)} %get-tuple-element.120), channel_id=1, source_target_pairs={{0,3},{1,2},{2,1},{3,0},{4,7},{5,6},{6,5},{7,4},{8,11},{9,10},{10,... | collective-permute-start | bytes 36872 | tf_op jit(solution)/shard_map/ppermute | solution.py:512
  35.5 0.0 collective-permute-start.15
  35.6 2.4 %collective-permute-done.14.qe = f32[24,128]{1,0:T(8,128)S(1)} collective-permute-done((f32[24,128]{1,0:T(8,128)S(1)}, f32[24,128]{1,0:T(8,128)S(1)}, u32[]{:S(2)}, u32[]{:S(2)}) %collective-permute-start.14) | collective-permute-done | bytes 12320 | tf_op jit(solution)/shard_map/ppermute | solution.py:512
  38.0 0.0 collective-permute-done.15.qo
  38.0 0.7 %last.1 = f32[96,128]{1,0:T(8,128)} custom-call(f32[16,8,128]{2,1,0:T(8,128)S(1)} %get-tuple-element.113.refs_8_.own_x, f32[16,8,128]{2,1,0:T(8,128)S(1)} %get-tuple-element.115.own, f32[16,8,128]{2,1,0:T(8,128)S(1)} %get-tuple-element.75.refs_6_.refs_2_.refs_15_.v_own, f32[16,8,128]{2,1,0:T(8,128)S(1)} %get-tuple-element.76.refs_7_.refs_3_.refs_16_.m_own, ...), custom_call_target="tpu_custom_call" | custom-call | tf_op jit(solution)/shard_map/last/pallas_call | solution.py:494
  (4 shorter events, 0.0 us)
Async XLA Ops:
  3.4 3.7 %collective-permute-start = (f32[64,128]{1,0:T(8,128)S(1)}, f32[64,128]{1,0:T(8,128)S(1)}, u32[]{:S(2)}, u32[]{:S(2)}) collective-permute-start(f32[64,128]{1,0:T(8,128)S(1)} %get-tuple-element.80), channel_id=1, source_target_pairs={{0,1},{1,5},{2,3},{3,7},{4,0},{5,9},{6,2},{7,11},{8,4},{9,13},{10,... | collective-permute-start | bytes 98312 | tf_op jit(solution)/shard_map/ppermute | solution.py:507
  5.5 2.8 %collective-permute-start.1 = (f32[64,128]{1,0:T(8,128)S(1)}, f32[64,128]{1,0:T(8,128)S(1)}, u32[]{:S(2)}, u32[]{:S(2)}) collective-permute-start(f32[64,128]{1,0:T(8,128)S(1)} %get-tuple-element.81), channel_id=1, source_target_pairs={{1,0},{5,1},{3,2},{7,3},{0,4},{9,5},{2,6},{11,7},{4,8},{13,9},{6,1... | collective-permute-start | bytes 98312 | tf_op jit(solution)/shard_map/ppermute | solution.py:507
  8.3 3.5 %collective-permute-start.2 = (f32[64,128]{1,0:T(8,128)S(1)}, f32[64,128]{1,0:T(8,128)S(1)}, u32[]{:S(2)}, u32[]{:S(2)}) collective-permute-start(f32[64,128]{1,0:T(8,128)S(1)} %get-tuple-element.84), channel_id=1, source_target_pairs={{0,3},{1,2},{2,1},{3,0},{4,7},{5,6},{6,5},{7,4},{8,11},{9,10},{10,... | collective-permute-start | bytes 98312 | tf_op jit(solution)/shard_map/ppermute | solution.py:512
  10.2 1.6 %collective-permute-start.3 = (f32[64,128]{1,0:T(8,128)S(1)}, f32[64,128]{1,0:T(8,128)S(1)}, u32[]{:S(2)}, u32[]{:S(2)}) collective-permute-start(f32[64,128]{1,0:T(8,128)S(1)} %get-tuple-element.85), channel_id=1, source_target_pairs={{0,1},{1,0},{2,3},{3,2},{4,5},{5,4},{6,7},{7,6},{8,9},{9,8},{10,11... | collective-permute-start | bytes 98312 | tf_op jit(solution)/shard_map/ppermute | solution.py:512
  13.2 3.2 %collective-permute-start.4 = (f32[32,128]{1,0:T(8,128)S(1)}, f32[32,128]{1,0:T(8,128)S(1)}, u32[]{:S(2)}, u32[]{:S(2)}) collective-permute-start(f32[32,128]{1,0:T(8,128)S(1)} %get-tuple-element.92), channel_id=1, source_target_pairs={{0,1},{1,5},{2,3},{3,7},{4,0},{5,9},{6,2},{7,11},{8,4},{9,13},{10,... | collective-permute-start | bytes 49160 | tf_op jit(solution)/shard_map/ppermute | solution.py:507
  14.8 2.8 %collective-permute-start.5 = (f32[32,128]{1,0:T(8,128)S(1)}, f32[32,128]{1,0:T(8,128)S(1)}, u32[]{:S(2)}, u32[]{:S(2)}) collective-permute-start(f32[32,128]{1,0:T(8,128)S(1)} %get-tuple-element.93), channel_id=1, source_target_pairs={{1,0},{5,1},{3,2},{7,3},{0,4},{9,5},{2,6},{11,7},{4,8},{13,9},{6,1... | collective-permute-start | bytes 49160 | tf_op jit(solution)/shard_map/ppermute | solution.py:507
  17.6 3.2 %collective-permute-start.6 = (f32[32,128]{1,0:T(8,128)S(1)}, f32[32,128]{1,0:T(8,128)S(1)}, u32[]{:S(2)}, u32[]{:S(2)}) collective-permute-start(f32[32,128]{1,0:T(8,128)S(1)} %get-tuple-element.98), channel_id=1, source_target_pairs={{0,3},{1,2},{2,1},{3,0},{4,7},{5,6},{6,5},{7,4},{8,11},{9,10},{10,... | collective-permute-start | bytes 49160 | tf_op jit(solution)/shard_map/ppermute | solution.py:512
  18.8 1.9 %collective-permute-start.7 = (f32[32,128]{1,0:T(8,128)S(1)}, f32[32,128]{1,0:T(8,128)S(1)}, u32[]{:S(2)}, u32[]{:S(2)}) collective-permute-start(f32[32,128]{1,0:T(8,128)S(1)} %get-tuple-element.99), channel_id=1, source_target_pairs={{0,1},{1,0},{2,3},{3,2},{4,5},{5,4},{6,7},{7,6},{8,9},{9,8},{10,11... | collective-permute-start | bytes 49160 | tf_op jit(solution)/shard_map/ppermute | solution.py:512
  22.1 3.0 %collective-permute-start.8 = (f32[32,128]{1,0:T(8,128)S(1)}, f32[32,128]{1,0:T(8,128)S(1)}, u32[]{:S(2)}, u32[]{:S(2)}) collective-permute-start(f32[32,128]{1,0:T(8,128)S(1)} %get-tuple-element.106), channel_id=1, source_target_pairs={{0,1},{1,5},{2,3},{3,7},{4,0},{5,9},{6,2},{7,11},{8,4},{9,13},{10,... | collective-permute-start | bytes 49160 | tf_op jit(solution)/shard_map/ppermute | solution.py:507
  23.6 2.6 %collective-permute-start.9 = (f32[32,128]{1,0:T(8,128)S(1)}, f32[32,128]{1,0:T(8,128)S(1)}, u32[]{:S(2)}, u32[]{:S(2)}) collective-permute-start(f32[32,128]{1,0:T(8,128)S(1)} %get-tuple-element.107), channel_id=1, source_target_pairs={{1,0},{5,1},{3,2},{7,3},{0,4},{9,5},{2,6},{11,7},{4,8},{13,9},{6,1... | collective-permute-start | bytes 49160 | tf_op jit(solution)/shard_map/ppermute | solution.py:507
  26.2 3.2 %collective-permute-start.10 = (f32[32,128]{1,0:T(8,128)S(1)}, f32[32,128]{1,0:T(8,128)S(1)}, u32[]{:S(2)}, u32[]{:S(2)}) collective-permute-start(f32[32,128]{1,0:T(8,128)S(1)} %get-tuple-element.110), channel_id=1, source_target_pairs={{0,3},{1,2},{2,1},{3,0},{4,7},{5,6},{6,5},{7,4},{8,11},{9,10},{10,... | collective-permute-start | bytes 49160 | tf_op jit(solution)/shard_map/ppermute | solution.py:512
  27.2 2.2 %collective-permute-start.11 = (f32[32,128]{1,0:T(8,128)S(1)}, f32[32,128]{1,0:T(8,128)S(1)}, u32[]{:S(2)}, u32[]{:S(2)}) collective-permute-start(f32[32,128]{1,0:T(8,128)S(1)} %get-tuple-element.111), channel_id=1, source_target_pairs={{0,1},{1,0},{2,3},{3,2},{4,5},{5,4},{6,7},{7,6},{8,9},{9,8},{10,11... | collective-permute-start | bytes 49160 | tf_op jit(solution)/shard_map/ppermute | solution.py:512
  30.7 2.7 %collective-permute-start.12 = (f32[24,128]{1,0:T(8,128)S(1)}, f32[24,128]{1,0:T(8,128)S(1)}, u32[]{:S(2)}, u32[]{:S(2)}) collective-permute-start(f32[24,128]{1,0:T(8,128)S(1)} %get-tuple-element.116), channel_id=1, source_target_pairs={{0,1},{1,5},{2,3},{3,7},{4,0},{5,9},{6,2},{7,11},{8,4},{9,13},{10,... | collective-permute-start | bytes 36872 | tf_op jit(solution)/shard_map/ppermute | solution.py:507
  32.3 2.5 %collective-permute-start.13 = (f32[24,128]{1,0:T(8,128)S(1)}, f32[24,128]{1,0:T(8,128)S(1)}, u32[]{:S(2)}, u32[]{:S(2)}) collective-permute-start(f32[24,128]{1,0:T(8,128)S(1)} %get-tuple-element.117), channel_id=1, source_target_pairs={{1,0},{5,1},{3,2},{7,3},{0,4},{9,5},{2,6},{11,7},{4,8},{13,9},{6,1... | collective-permute-start | bytes 36872 | tf_op jit(solution)/shard_map/ppermute | solution.py:507
  34.9 3.1 %collective-permute-start.14 = (f32[24,128]{1,0:T(8,128)S(1)}, f32[24,128]{1,0:T(8,128)S(1)}, u32[]{:S(2)}, u32[]{:S(2)}) collective-permute-start(f32[24,128]{1,0:T(8,128)S(1)} %get-tuple-element.120), channel_id=1, source_target_pairs={{0,3},{1,2},{2,1},{3,0},{4,7},{5,6},{6,5},{7,4},{8,11},{9,10},{10,... | collective-permute-start | bytes 36872 | tf_op jit(solution)/shard_map/ppermute | solution.py:512
  35.5 2.5 %collective-permute-start.15 = (f32[24,128]{1,0:T(8,128)S(1)}, f32[24,128]{1,0:T(8,128)S(1)}, u32[]{:S(2)}, u32[]{:S(2)}) collective-permute-start(f32[24,128]{1,0:T(8,128)S(1)} %get-tuple-element.121), channel_id=1, source_target_pairs={{0,1},{1,0},{2,3},{3,2},{4,5},{5,4},{6,7},{7,6},{8,9},{9,8},{10,11... | collective-permute-start | bytes 36872 | tf_op jit(solution)/shard_map/ppermute | solution.py:512
